TPU v7x, 128 devices: a whole 4x4x4 slice. The times are simulated.
128 devices in a mesh: seq: 16 (over y, z), slide: 8 (over x, core).
Axes of the slice: x: 4, y: 4, z: 4, core: 2. Of those that a mesh axis runs over, the one named last changes fastest.
Arguments:
- inputs: bfloat16 [8, 4096, 768], P('slide', 'seq'), may hold values from -6 to 6
- cotangent: bfloat16 [8, 4096, 768], P('slide', 'seq'), may hold values from -6 to 6
- key_tiles: int32 [8, 4, 16, 8], P('slide'), may hold values from 0 to 31, as said below
- tile_valid: int32 [8, 32], P('slide'), may hold values from 0 to 1, as said below
- w_qkv: bfloat16 [768, 2304], replicated, may hold values from -0.21650635 to 0.21650635
- w_out: bfloat16 [768, 768], replicated, may hold values from -0.21875 to 0.21875
Outputs:
- outputs: bfloat16 [8, 4096, 768], P('slide', 'seq')
- grad_inputs: bfloat16 [8, 4096, 768], P('slide', 'seq')
- w_qkv_grad: float32 [768, 2304], P('seq')
- w_out_grad: float32 [768, 768], P('seq')
Inputs may be any that keep to these rules, and one draw needn't show every extreme that they name: Row key_tiles[s,g,p] is start + o + i*r for i < 8, with dilation r of 2 or 4 for the group of the slide, 0 <= o < r, and start the first tile of the segment of 8*r tiles that holds block p. At most 1 entry of a row lies in one block of 2 tiles, and every slide has at least one group with dilation 2, whose rows hold exactly one tile of each block of their segment. `tile_valid`: the first tile of every block of 2 tiles is 1.
All inputs are finite; a program needn't handle non-finite values.
Results may differ from a plain program's by a relative error of at most 0.013.
Values may be sent and summed in bfloat16 or wider, within the bound.
No kernel may reach another device: no remote copies, remote signals or barrier semaphores. Data moves between devices by JAX's collectives and lax.ppermute only.
A program may use at most 192 MiB of HBM per device.

v0:
```python
import jax
import jax.numpy as jnp
from jax import lax
from jax.sharding import PartitionSpec as P

H = 12


NEG_FILL = -1e30


def softmax_rows(scores, allowed):
    scores = jnp.where(allowed, scores, NEG_FILL)
    top = jnp.max(scores, axis=-1, keepdims=True)
    expo = jnp.exp(scores - top)
    return expo / jnp.sum(expo, axis=-1, keepdims=True)


def plan_slots(lists, myself, per_dev, cap, peers):
    owner = lists // per_dev
    listed = lists.shape[-1]
    same_owner = owner[..., :, None] == owner[..., None, :]
    before = jnp.arange(listed)[:, None] < jnp.arange(listed)[None, :]
    slot_rank = jnp.sum(jnp.logical_and(same_owner, before), axis=-2)
    local_tile = lists - myself * per_dev
    chosen = jnp.logical_and(
        jnp.logical_and(
            (owner == myself)[..., None, None],
            slot_rank[..., None, None] == jnp.arange(cap)[:, None],
        ),
        local_tile[..., None, None] == jnp.arange(per_dev)[None, :],
    )
    send_pick = jnp.sum(chosen.astype(jnp.float32), axis=-3)
    dims = send_pick.shape
    send_pick = send_pick.reshape(dims[0], dims[1], peers * cap, per_dev).astype(jnp.bfloat16)
    own_slot = lax.dynamic_index_in_dim(owner * cap + slot_rank, myself, 2, keepdims=False)
    recv_pick = (own_slot[..., None] == jnp.arange(peers * cap)).astype(jnp.bfloat16)
    own_list = lax.dynamic_index_in_dim(lists, myself, 2, keepdims=False)
    return (send_pick, recv_pick, own_list)


def group_tiles(keys, values, groups, per_dev):
    slides, tok, heads, head_dim = keys.shape

    def arrange(array):
        array = array.reshape(slides, per_dev, tok // per_dev, groups, heads // groups * head_dim)
        return jnp.moveaxis(array, 3, 1)

    return jnp.concatenate([arrange(keys), arrange(values)], axis=-1)


def fetch(send):
    pieces = []
    for group in range(send.shape[2]):
        pieces.append(
            lax.all_to_all(send[:, :, group], "seq", split_axis=1, concat_axis=1, tiled=True)
        )
    return jnp.stack(pieces, axis=2)


def give_back(back):
    pieces = []
    for group in range(back.shape[2]):
        pieces.append(
            lax.all_to_all(back[:, :, group], "seq", split_axis=1, concat_axis=1, tiled=True)
        )
    return jnp.stack(pieces, axis=2)


def shards(inputs, cotangent, key_tiles, tile_valid, w_qkv, w_out):
    f32 = jnp.float32
    bf16 = jnp.bfloat16
    slides, tok, width = inputs.shape
    groups = key_tiles.shape[1]
    listed = key_tiles.shape[3]
    peers = lax.axis_size("seq")
    total_tiles = tile_valid.shape[1]
    per_dev = total_tiles // peers
    tile_len = tok // per_dev
    cap = per_dev // 2
    heads = H
    head_dim = width // heads
    per_group = heads // groups
    scale = head_dim ** (-0.5)
    myself = lax.axis_index("seq")
    projected = jnp.einsum("std,de->ste", inputs, w_qkv, preferred_element_type=f32).astype(bf16)
    queries = projected[..., :width].reshape(slides, tok, heads, head_dim)
    keys = projected[..., width : 2 * width].reshape(slides, tok, heads, head_dim)
    values = projected[..., 2 * width :].reshape(slides, tok, heads, head_dim)
    send_pick, recv_pick, own_list = plan_slots(key_tiles, myself, per_dev, cap, peers)
    tiles = group_tiles(keys, values, groups, per_dev)
    send = jnp.einsum("sgmc,sgctf->smgtf", send_pick, tiles, preferred_element_type=f32).astype(
        bf16
    )
    received = fetch(send)
    far = jnp.einsum("sgim,smgtf->sgitf", recv_pick, received, preferred_element_type=f32).astype(
        bf16
    )
    near_valid = jnp.repeat(
        lax.dynamic_slice_in_dim(tile_valid, myself * per_dev, per_dev, 1), tile_len, axis=1
    )
    far_valid = jnp.sum(
        jnp.where(own_list[..., None] == jnp.arange(total_tiles), tile_valid[:, None, None, :], 0),
        axis=-1,
    )
    far_valid = jnp.repeat(far_valid, tile_len, axis=2)

    def assemble(far_block, group):
        lower = group * per_group
        upper = lower + per_group
        half = far_block.shape[-1] // 2
        far_keys = far_block[:, group, :, :, :half].reshape(
            slides, listed * tile_len, per_group, head_dim
        )
        far_values = far_block[:, group, :, :, half:].reshape(
            slides, listed * tile_len, per_group, head_dim
        )
        all_keys = jnp.concatenate([keys[:, :, lower:upper], far_keys], axis=1)
        all_values = jnp.concatenate([values[:, :, lower:upper], far_values], axis=1)
        allowed = jnp.concatenate([near_valid, far_valid[:, group]], axis=1) > 0
        query_group = queries[:, :, lower:upper]
        scores = (
            jnp.einsum("sqhd,skhd->shqk", query_group, all_keys, preferred_element_type=f32) * scale
        )
        probs = softmax_rows(scores, allowed[:, None, None, :])
        return (query_group, all_keys, all_values, probs)

    attended_parts = []
    for group in range(groups):
        query_group, all_keys, all_values, probs = assemble(far, group)
        attended_parts.append(
            jnp.einsum(
                "shqk,skhd->sqhd", probs.astype(bf16), all_values, preferred_element_type=f32
            ).astype(bf16)
        )
    attended_flat = jnp.concatenate(attended_parts, axis=2).reshape(slides, tok, width)
    outputs = jnp.einsum("std,de->ste", attended_flat, w_out, preferred_element_type=f32).astype(
        bf16
    )
    grad_attended = jnp.einsum("ste,de->std", cotangent, w_out, preferred_element_type=f32).astype(
        bf16
    )
    grad_attended = grad_attended.reshape(slides, tok, heads, head_dim)
    grad_q_parts = []
    near_k_parts = []
    near_v_parts = []
    far_grads = []
    for group in range(groups):
        query_group, all_keys, all_values, probs = assemble(far, group)
        grad_group = grad_attended[:, :, group * per_group : (group + 1) * per_group]
        grad_probs = jnp.einsum(
            "sqhd,skhd->shqk", grad_group, all_values, preferred_element_type=f32
        )
        center = jnp.sum(probs * grad_probs, axis=-1, keepdims=True)
        grad_scores = (probs * (grad_probs - center) * scale).astype(bf16)
        grad_q_parts.append(
            jnp.einsum("shqk,skhd->sqhd", grad_scores, all_keys, preferred_element_type=f32)
        )
        grad_k = jnp.einsum("shqk,sqhd->skhd", grad_scores, query_group, preferred_element_type=f32)
        grad_v = jnp.einsum(
            "shqk,sqhd->skhd", probs.astype(bf16), grad_group, preferred_element_type=f32
        )
        near_k_parts.append(grad_k[:, :tok])
        near_v_parts.append(grad_v[:, :tok])
        far_k = grad_k[:, tok:].astype(bf16).reshape(slides, listed, tile_len, per_group * head_dim)
        far_v = grad_v[:, tok:].astype(bf16).reshape(slides, listed, tile_len, per_group * head_dim)
        far_grads.append(jnp.concatenate([far_k, far_v], axis=-1))
    grad_far = jnp.stack(far_grads, axis=1)
    back = jnp.einsum("sgim,sgitf->smgtf", recv_pick, grad_far, preferred_element_type=f32).astype(
        bf16
    )
    returned = give_back(back)
    added = jnp.einsum("sgmc,smgtf->sgctf", send_pick, returned, preferred_element_type=f32)
    added = jnp.moveaxis(added, 1, 3)
    half = added.shape[-1] // 2
    added_k = added[..., :half].reshape(slides, tok, heads, head_dim)
    added_v = added[..., half:].reshape(slides, tok, heads, head_dim)
    grad_query = jnp.concatenate(grad_q_parts, axis=2).reshape(slides, tok, width)
    grad_keys = (jnp.concatenate(near_k_parts, axis=2) + added_k).reshape(slides, tok, width)
    grad_values = (jnp.concatenate(near_v_parts, axis=2) + added_v).reshape(slides, tok, width)
    grad_proj = jnp.concatenate([grad_query, grad_keys, grad_values], axis=-1).astype(bf16)
    grad_inputs = jnp.einsum("ste,de->std", grad_proj, w_qkv, preferred_element_type=f32).astype(
        bf16
    )
    rows = width // peers
    first_part = jnp.einsum("std,ste->de", inputs, grad_proj, preferred_element_type=f32)
    second_part = jnp.einsum("std,ste->de", attended_flat, cotangent, preferred_element_type=f32)
    whole = lax.psum(jnp.concatenate([first_part, second_part], axis=1), ("seq", "slide"))
    share = lax.dynamic_slice_in_dim(whole, myself * rows, rows, 0)
    return (outputs, grad_inputs, share[:, : 3 * width], share[:, 3 * width :])


def solution(mesh):
    placed = (
        P("slide", "seq", None),
        P("slide", "seq", None),
        P("slide", None, None, None),
        P("slide", None),
        P(),
        P(),
    )
    return jax.shard_map(
        shards,
        mesh=mesh,
        in_specs=placed,
        out_specs=(
            P("slide", "seq", None),
            P("slide", "seq", None),
            P("seq", None),
            P("seq", None),
        ),
        check_vma=False,
    )
```

profile of v0, /device:TPU:1, one launch (start us, length us, event | category | flops | bytes accessed | tf_op | source)
XLA Modules:
  0.0 700.0 jit_solution(5224778581964247851)
XLA Ops:
  28.3 8.6 %all-to-all-start = ((bf16[1,16,128,384]{3,2,0,1:T(8,128)(2,1)}), bf16[1,16,128,384]{3,2,0,1:T(8,128)(2,1)}, u32[]{:S(2)}, u32[]{:S(2)}) async-start(bf16[1,16,128,384]{3,2,0,1:T(8,128)(2,1)} %copy.127), calls=%async_computation | async-start | bytes 3145728 | tf_op jit(solution)/shard_map/all_to_all | solution.py:56
  36.9 3.0 copy.133
  39.9 17.7 %all-to-all-done = bf16[1,16,128,384]{3,2,0,1:T(8,128)(2,1)} async-done(((bf16[1,16,128,384]{3,2,0,1:T(8,128)(2,1)}), bf16[1,16,128,384]{3,2,0,1:T(8,128)(2,1)}, u32[]{:S(2)}, u32[]{:S(2)}) %all-to-all-start) | async-done | bytes 1572896 | tf_op jit(solution)/shard_map/all_to_all | solution.py:56
  57.6 5.4 all-to-all-start.3
  63.0 3.0 copy.131
  66.0 16.9 %all-to-all-done.3 = bf16[1,16,128,384]{3,2,0,1:T(8,128)(2,1)} async-done(((bf16[1,16,128,384]{3,2,0,1:T(8,128)(2,1)}), bf16[1,16,128,384]{3,2,0,1:T(8,128)(2,1)}, u32[]{:S(2)}, u32[]{:S(2)}) %all-to-all-start.3) | async-done | bytes 1572896 | tf_op jit(solution)/shard_map/all_to_all | solution.py:56
  82.9 4.8 all-to-all-start.2
  87.7 3.0 copy.129
  90.6 16.2 %all-to-all-done.2 = bf16[1,16,128,384]{3,2,0,1:T(8,128)(2,1)} async-done(((bf16[1,16,128,384]{3,2,0,1:T(8,128)(2,1)}), bf16[1,16,128,384]{3,2,0,1:T(8,128)(2,1)}, u32[]{:S(2)}, u32[]{:S(2)}) %all-to-all-start.2) | async-done | bytes 1572896 | tf_op jit(solution)/shard_map/all_to_all | solution.py:56
  106.8 7.4 %all-to-all-start.1 = ((bf16[1,16,128,384]{3,2,0,1:T(8,128)(2,1)}), bf16[1,16,128,384]{3,2,0,1:T(8,128)(2,1)}, u32[]{:S(2)}, u32[]{:S(2)}) async-start(bf16[1,16,128,384]{3,2,0,1:T(8,128)(2,1)} %copy.129), calls=%async_computation.1 | async-start | bytes 3145728 | tf_op jit(solution)/shard_map/all_to_all | solution.py:56
  121.8 2.7 convolution_convert_fusion.2
  133.6 3.6 copy.201
  137.2 3.5 copy.198
  140.7 3.5 copy.199
  146.5 3.4 convert_bitcast_fusion.2
  149.8 3.0 fusion.226
  186.7 4.9 fusion.234
  191.6 3.6 convolution_bitcast_fusion.3
  195.2 3.8 fusion.147
  199.0 10.8 %convolution_bitcast_fusion.7 = f32[1,1280,3,64]{1,3,2,0:T(8,128)} fusion(f32[3,256,1280]{2,1,0:T(8,128)} %fusion.147, bf16[1,256,12,64]{1,3,2,0:T(8,128)(2,1)} %bitcast.523, f32[3,256,1280]{2,1,0:T(8,128)} %get-tuple-element.65, f32[3,256]{1,0:T(4,128)} %get-tuple-element.64), kind=kOutput, calls=%fused_computation.84 | convolution fusion | flops 132712448 | bytes 16818176 | tf_op jit(solution)/shard_map/shqk,sqhd->skhd/dot_general | solution.py:159
  211.7 2.7 copy.148
  218.8 4.9 fusion.233
  223.7 3.6 convolution_bitcast_fusion.2
  227.3 3.7 fusion.146
  231.0 10.8 %convolution_bitcast_fusion.6 = f32[1,1280,3,64]{1,3,2,0:T(8,128)} fusion(f32[3,256,1280]{2,1,0:T(8,128)} %fusion.146, bf16[1,256,12,64]{1,3,2,0:T(8,128)(2,1)} %bitcast.526, f32[3,256,1280]{2,1,0:T(8,128)} %get-tuple-element.63, f32[3,256]{1,0:T(4,128)} %get-tuple-element.62), kind=kOutput, calls=%fused_computation.83 | convolution fusion | flops 132712448 | bytes 16818176 | tf_op jit(solution)/shard_map/shqk,sqhd->skhd/dot_general | solution.py:159
  250.4 4.9 fusion.232
  255.3 3.6 convolution_bitcast_fusion.1
  258.9 3.7 fusion.145
  262.6 10.7 %convolution_bitcast_fusion.5 = f32[1,1280,3,64]{1,3,2,0:T(8,128)} fusion(f32[3,256,1280]{2,1,0:T(8,128)} %fusion.145, bf16[1,256,12,64]{1,3,2,0:T(8,128)(2,1)} %bitcast.529, f32[3,256,1280]{2,1,0:T(8,128)} %get-tuple-element.61, f32[3,256]{1,0:T(4,128)} %get-tuple-element.60), kind=kOutput, calls=%fused_computation.82 | convolution fusion | flops 132712448 | bytes 16818176 | tf_op jit(solution)/shard_map/shqk,sqhd->skhd/dot_general | solution.py:159
  282.2 4.9 fusion.235
  287.1 3.7 convolution_bitcast_fusion.4
  295.1 3.8 fusion.148
  298.9 10.7 %convolution_bitcast_fusion.8 = f32[1,1280,3,64]{1,3,2,0:T(8,128)} fusion(f32[3,256,1280]{2,1,0:T(8,128)} %fusion.148, bf16[1,256,12,64]{1,3,2,0:T(8,128)(2,1)} %bitcast.532, f32[3,256,1280]{2,1,0:T(8,128)} %get-tuple-element.67, f32[3,256]{1,0:T(4,128)} %get-tuple-element.66), kind=kOutput, calls=%fused_computation.85 | convolution fusion | flops 132712448 | bytes 16818176 | tf_op jit(solution)/shard_map/shqk,sqhd->skhd/dot_general | solution.py:159
  323.8 6.8 all-to-all-start.4
  330.6 3.0 copy.160
  333.5 16.2 %all-to-all-done.4 = bf16[1,16,128,384]{3,2,0,1:T(8,128)(2,1)} async-done(((bf16[1,16,128,384]{3,2,0,1:T(8,128)(2,1)}), bf16[1,16,128,384]{3,2,0,1:T(8,128)(2,1)}, u32[]{:S(2)}, u32[]{:S(2)}) %all-to-all-start.4) | async-done | bytes 1572896 | tf_op jit(solution)/shard_map/all_to_all | solution.py:65
  349.7 6.3 all-to-all-start.7
  356.0 2.9 copy.158
  358.9 16.7 %all-to-all-done.7 = bf16[1,16,128,384]{3,2,0,1:T(8,128)(2,1)} async-done(((bf16[1,16,128,384]{3,2,0,1:T(8,128)(2,1)}), bf16[1,16,128,384]{3,2,0,1:T(8,128)(2,1)}, u32[]{:S(2)}, u32[]{:S(2)}) %all-to-all-start.7) | async-done | bytes 1572896 | tf_op jit(solution)/shard_map/all_to_all | solution.py:65
  375.7 5.2 all-to-all-start.6
  380.9 3.0 copy.156
  383.8 3.6 fusion.125
  387.4 3.5 fusion.126
  390.9 3.5 fusion.127
  394.5 5.4 all-to-all-done.6
  399.9 6.7 all-to-all-start.5
  406.8 3.6 fusion.124
  425.1 10.1 %fusion.115 = bf16[1,256,3,64]{1,3,2,0:T(8,128)(2,1)} fusion(f32[3,256,1280]{2,1,0:T(8,128)} %fusion.147, bf16[1,1024,3,64]{1,3,2,0:T(8,128)(2,1)} %reshape_squeeze.35, bf16[1,256,3,64]{1,3,2,0:T(8,128)(2,1)} %get-tuple-element.44, f32[3,256,1280]{2,1,0:T(8,128)} %get-tuple-element.65, f32[3,256]{1,0:T(4,128)S(1)} %copy-done.14), kind=kOutput, calls=%fused_computation.134 | convolution fusion | flops 133744640 | bytes 8457216 | tf_op jit(solution)/shard_map/shqk,skhd->sqhd/dot_general | solution.py:157
  435.3 10.1 %fusion.118 = bf16[1,256,3,64]{1,3,2,0:T(8,128)(2,1)} fusion(f32[3,256,1280]{2,1,0:T(8,128)} %fusion.146, bf16[1,1024,3,64]{1,3,2,0:T(8,128)(2,1)} %reshape_squeeze.37, bf16[1,256,3,64]{1,3,2,0:T(8,128)(2,1)} %get-tuple-element.43, f32[3,256,1280]{2,1,0:T(8,128)} %get-tuple-element.63, f32[3,256]{1,0:T(4,128)S(1)} %copy-done.15), kind=kOutput, calls=%fused_computation.135 | convolution fusion | flops 133744640 | bytes 8457216 | tf_op jit(solution)/shard_map/shqk,skhd->sqhd/dot_general | solution.py:157
  445.4 10.1 %fusion.121 = bf16[1,256,3,64]{1,3,2,0:T(8,128)(2,1)} fusion(f32[3,256,1280]{2,1,0:T(8,128)} %fusion.145, bf16[1,1024,3,64]{1,3,2,0:T(8,128)(2,1)} %reshape_squeeze.39, bf16[1,256,3,64]{1,3,2,0:T(8,128)(2,1)} %get-tuple-element.42, f32[3,256,1280]{2,1,0:T(8,128)} %get-tuple-element.61, f32[3,256]{1,0:T(4,128)S(1)} %copy-done.16), kind=kOutput, calls=%fused_computation.136 | convolution fusion | flops 133744640 | bytes 8457216 | tf_op jit(solution)/shard_map/shqk,skhd->sqhd/dot_general | solution.py:157
  455.6 10.1 %fusion.112 = bf16[1,256,3,64]{1,3,2,0:T(8,128)(2,1)} fusion(f32[3,256,1280]{2,1,0:T(8,128)} %fusion.148, bf16[1,1024,3,64]{1,3,2,0:T(8,128)(2,1)} %reshape_squeeze.33, bf16[1,256,3,64]{1,3,2,0:T(8,128)(2,1)} %get-tuple-element.41, f32[3,256,1280]{2,1,0:T(8,128)} %get-tuple-element.67, f32[3,256]{1,0:T(4,128)S(1)} %copy-done.17), kind=kOutput, calls=%fused_computation.133 | convolution fusion | flops 133744640 | bytes 8457216 | tf_op jit(solution)/shard_map/shqk,skhd->sqhd/dot_general | solution.py:157
  474.0 3.5 copy.197
  477.5 3.5 copy.194
  480.9 3.5 copy.195
  487.0 2.9 fusion.97
  489.9 2.8 fusion.227
  492.7 3.6 copy.162
  496.3 3.5 copy.163
  503.7 4.0 convolution_bitcast_fusion
  507.7 8.0 %pad_maximum_fusion = f32[768,3072]{0,1:T(8,128)} fusion(f32[768,768]{0,1:T(8,128)} %fusion.140, f32[768,2304]{0,1:T(8,128)} %convolution_bitcast_fusion), kind=kLoop, calls=%fused_computation.8 | loop fusion | flops 2359296 | bytes 18874368 | tf_op jit(solution)/shard_map/concatenate | solution.py:188
  515.7 2.7 fusion.98
  518.4 3.1 fusion.99
  521.5 162.0 %all-reduce.2.cloned.1.call-done = f32[768,3072]{0,1:T(8,128)} async-done(((f32[768,3072]{0,1:T(8,128)}), f32[768,3072]{0,1:T(8,128)}) %all-reduce.2.cloned.1.call-update) | async-done | bytes 9437200 | tf_op jit(solution)/shard_map/psum | solution.py:188
  683.5 3.0 constant_dynamic-slice_fusion
  (133 shorter events, 152.1 us)
Async XLA Ops:
  7.2 4.3 copy-start
  19.9 2.3 copy-start.11
  28.3 29.3 %all-to-all-start = ((bf16[1,16,128,384]{3,2,0,1:T(8,128)(2,1)}), bf16[1,16,128,384]{3,2,0,1:T(8,128)(2,1)}, u32[]{:S(2)}, u32[]{:S(2)}) async-start(bf16[1,16,128,384]{3,2,0,1:T(8,128)(2,1)} %copy.127), calls=%async_computation | async-start | bytes 3145728 | tf_op jit(solution)/shard_map/all_to_all | solution.py:56
  57.6 25.3 %all-to-all-start.3 = ((bf16[1,16,128,384]{3,2,0,1:T(8,128)(2,1)}), bf16[1,16,128,384]{3,2,0,1:T(8,128)(2,1)}, u32[]{:S(2)}, u32[]{:S(2)}) async-start(bf16[1,16,128,384]{3,2,0,1:T(8,128)(2,1)} %copy.133), calls=%async_computation.3 | async-start | bytes 3145728 | tf_op jit(solution)/shard_map/all_to_all | solution.py:56
  82.9 23.9 %all-to-all-start.2 = ((bf16[1,16,128,384]{3,2,0,1:T(8,128)(2,1)}), bf16[1,16,128,384]{3,2,0,1:T(8,128)(2,1)}, u32[]{:S(2)}, u32[]{:S(2)}) async-start(bf16[1,16,128,384]{3,2,0,1:T(8,128)(2,1)} %copy.131), calls=%async_computation.2 | async-start | bytes 3145728 | tf_op jit(solution)/shard_map/all_to_all | solution.py:56
  106.8 37.3 %all-to-all-start.1 = ((bf16[1,16,128,384]{3,2,0,1:T(8,128)(2,1)}), bf16[1,16,128,384]{3,2,0,1:T(8,128)(2,1)}, u32[]{:S(2)}, u32[]{:S(2)}) async-start(bf16[1,16,128,384]{3,2,0,1:T(8,128)(2,1)} %copy.129), calls=%async_computation.1 | async-start | bytes 3145728 | tf_op jit(solution)/shard_map/all_to_all | solution.py:56
  313.9 3.2 copy-start.2
  313.9 3.2 copy-start.3
  313.9 3.5 copy-start.4
  313.9 3.5 copy-start.5
  313.9 3.8 copy-start.13
  323.8 25.9 %all-to-all-start.4 = ((bf16[1,16,128,384]{3,2,0,1:T(8,128)(2,1)}), bf16[1,16,128,384]{3,2,0,1:T(8,128)(2,1)}, u32[]{:S(2)}, u32[]{:S(2)}) async-start(bf16[1,16,128,384]{3,2,0,1:T(8,128)(2,1)} %copy.154), calls=%async_computation.4 | async-start | bytes 3145728 | tf_op jit(solution)/shard_map/all_to_all | solution.py:65
  349.7 26.0 %all-to-all-start.7 = ((bf16[1,16,128,384]{3,2,0,1:T(8,128)(2,1)}), bf16[1,16,128,384]{3,2,0,1:T(8,128)(2,1)}, u32[]{:S(2)}, u32[]{:S(2)}) async-start(bf16[1,16,128,384]{3,2,0,1:T(8,128)(2,1)} %copy.160), calls=%async_computation.7 | async-start | bytes 3145728 | tf_op jit(solution)/shard_map/all_to_all | solution.py:65
  375.7 24.2 %all-to-all-start.6 = ((bf16[1,16,128,384]{3,2,0,1:T(8,128)(2,1)}), bf16[1,16,128,384]{3,2,0,1:T(8,128)(2,1)}, u32[]{:S(2)}, u32[]{:S(2)}) async-start(bf16[1,16,128,384]{3,2,0,1:T(8,128)(2,1)} %copy.158), calls=%async_computation.6 | async-start | bytes 3145728 | tf_op jit(solution)/shard_map/all_to_all | solution.py:65
  387.4 3.6 copy-start.16
  390.9 15.9 %copy-start.17 = (f32[3,256]{1,0:T(4,128)S(1)}, f32[3,256]{1,0:T(4,128)}, u32[]{:S(2)}) copy-start(f32[3,256]{1,0:T(4,128)} %get-tuple-element.66) | copy-start | bytes 9220
  399.9 84.6 %all-to-all-start.5 = ((bf16[1,16,128,384]{3,2,0,1:T(8,128)(2,1)}), bf16[1,16,128,384]{3,2,0,1:T(8,128)(2,1)}, u32[]{:S(2)}, u32[]{:S(2)}) async-start(bf16[1,16,128,384]{3,2,0,1:T(8,128)(2,1)} %copy.156), calls=%async_computation.5 | async-start | bytes 3145728 | tf_op jit(solution)/shard_map/all_to_all | solution.py:65
  406.6 276.9 %all-reduce.2.cloned.1.call-start = ((), (), s32[]{:S(2)}) async-start(), calls=%async_computation.8 | async-start | bytes 18874368 | tf_op jit(solution)/shard_map/psum | solution.py:188
  410.4 14.8 %copy-start.14 = (f32[3,256]{1,0:T(4,128)S(1)}, f32[3,256]{1,0:T(4,128)}, u32[]{:S(2)}) copy-start(f32[3,256]{1,0:T(4,128)} %get-tuple-element.64) | copy-start | bytes 9220
  425.1 10.1 %copy-start.15 = (f32[3,256]{1,0:T(4,128)S(1)}, f32[3,256]{1,0:T(4,128)}, u32[]{:S(2)}) copy-start(f32[3,256]{1,0:T(4,128)} %get-tuple-element.62) | copy-start | bytes 9220
  465.7 6.3 copy-start.1
  465.7 6.3 copy-start.9
  480.9 6.1 copy-start.12
  499.8 3.9 copy-start.6
  499.8 3.9 copy-start.10
  501.3 1.6 copy-start.7
  502.9 0.7 copy-start.8
Sparse Core Ops, SparseCore 0:
  515.8 167.5 all-reduce.1
where the time goes:
time: 710 us; the launch traced here: 700 us
  waiting for transfers between devices  251 us (35%)
  local copies, waits for them, and re-layouts  178 us (25%)
  matrix products  174 us (25%)
  starting transfers between devices  51.4 us (7%)
  other arithmetic  30.4 us (4%)
  between operations  14.9 us (2%)
    psum x1, waiting for transfers between devices, shards(): lax.psum(jnp.concatenate([first_part, second_part], axis=1), ('seq', 'sli...  162 us
    all_to_all x4, waiting for transfers between devices, fetch(): lax.all_to_all(send[:, :, group], 'seq', split_axis=1, concat_axis=1, til...  50.8 us
    dot_general x4, matrix products, shards(): jnp.einsum('shqk,sqhd->skhd', grad_scores, query_group, preferred_element...  43 us
    dot_general x4, matrix products, shards(): jnp.einsum('shqk,skhd->sqhd', grad_scores, all_keys, preferred_element_ty...  40.6 us
    all_to_all x4, waiting for transfers between devices, give_back(): lax.all_to_all(back[:, :, group], 'seq', split_axis=1, concat_axis=1, til...  38.3 us
    all_to_all x4, starting transfers between devices, fetch(): lax.all_to_all(send[:, :, group], 'seq', split_axis=1, concat_axis=1, til...  26.2 us
    all_to_all x4, starting transfers between devices, give_back(): lax.all_to_all(back[:, :, group], 'seq', split_axis=1, concat_axis=1, til...  24.9 us
    sub x4, matrix products, softmax_rows(): expo = jnp.exp(scores - top)  19.5 us
  transfers between devices with their start and end apart: 9, of which 7 were waited for; matrix products, arithmetic and copies ran while one was open for 20% of the time, Pallas kernels for 0%

commit v1 on v0

v1 whole, which is shorter than its diff:
```python
import jax
import jax.numpy as jnp
from jax import lax
from jax.experimental import pallas as pl
from jax.experimental.pallas import tpu as pltpu
from jax.sharding import PartitionSpec as P

H = 12
HPG = 3
HD = 64
TILE = 128
NEG_FILL = -1e30
F32 = jnp.float32
BF16 = jnp.bfloat16
SCALE = HD ** (-0.5)


def slot_of(head):
    row = head // HPG
    place = head % HPG
    return 4 * row + place + (place >= row)


def project_body(x_ref, cot_ref, wq_ref, wk_ref, wv_ref, wo_ref, out_ref):
    step = pl.program_id(0)
    x = x_ref[...]
    contract = (((0,), (1,)), ((), ()))
    qt = lax.dot_general(wq_ref[...], x, contract, preferred_element_type=F32).astype(BF16)
    kt = lax.dot_general(wk_ref[...], x, contract, preferred_element_type=F32).astype(BF16)
    vt = lax.dot_general(wv_ref[...], x, contract, preferred_element_type=F32).astype(BF16)
    gt = lax.dot_general(
        wo_ref[...], cot_ref[...], (((1,), (1,)), ((), ())), preferred_element_type=F32
    ).astype(BF16)
    qt = qt * jnp.asarray(SCALE, BF16)
    for half in range(2):
        head = 2 * step + half
        row = head // HPG
        place = head - row * HPG
        slot = 4 * row + place + jnp.where(place >= row, 1, 0)
        rows = slice(half * HD, half * HD + HD)
        out_ref[slot, 0:HD, :] = qt[rows]
        out_ref[slot, HD : 2 * HD, :] = kt[rows]
        out_ref[slot, 2 * HD : 3 * HD, :] = vt[rows]
        out_ref[slot, 3 * HD :, :] = gt[rows]

    @pl.when(step == 0)
    def _():
        for row in range(4):
            out_ref[5 * row] = jnp.zeros(out_ref.shape[1:], BF16)


def project(x, cot, w_qkv, w_out):
    tok, width = x.shape
    pairs = H // 2
    return pl.pallas_call(
        project_body,
        grid=(pairs,),
        in_specs=[
            pl.BlockSpec((tok, width), lambda i: (0, 0)),
            pl.BlockSpec((tok, width), lambda i: (0, 0)),
            pl.BlockSpec((width, 2 * HD), lambda i: (0, i)),
            pl.BlockSpec((width, 2 * HD), lambda i: (0, i + pairs)),
            pl.BlockSpec((width, 2 * HD), lambda i: (0, i + 2 * pairs)),
            pl.BlockSpec((2 * HD, width), lambda i: (i, 0)),
        ],
        out_specs=pl.BlockSpec((16, 4 * HD, tok), lambda i: (0, 0, 0)),
        out_shape=jax.ShapeDtypeStruct((16, 4 * HD, tok), BF16),
        compiler_params=pltpu.CompilerParams(vmem_limit_bytes=32 * 2**20),
        cost_estimate=pl.CostEstimate(
            flops=2 * tok * width * 4 * width, bytes_accessed=8 * 2**20, transcendentals=0
        ),
        name="project",
    )(x, cot, w_qkv, w_qkv, w_qkv, w_out)


def attend_body(tiles_ref, valid_ref, in_ref, out_ref, kv, kvt, dkv):
    blocks = in_ref.shape[0]
    listed = tiles_ref.shape[1]

    def prepare(b, carry):
        both = in_ref[b, HD : 3 * HD, :]
        flipped = both.T
        for c in range(2):
            kvt[2 * b + c] = both[:, c * TILE : (c + 1) * TILE]
            kv[2 * b + c] = flipped[c * TILE : (c + 1) * TILE]
            dkv[2 * b + c] = jnp.zeros((TILE, 2 * HD), F32)
        return carry

    lax.fori_loop(0, blocks, prepare, 0)

    def block(b, carry):
        tiles = [2 * b, 2 * b + 1] + [tiles_ref[b, i] for i in range(listed)]
        qt = in_ref[b, 0:HD, :]
        gt = in_ref[b, 3 * HD :, :]
        zero = jnp.zeros_like(qt)
        keys = jnp.concatenate([kv[t] for t in tiles], axis=0)
        scores = jnp.dot(
            keys, jnp.concatenate([qt, zero], axis=0), preferred_element_type=F32
        )
        grad_probs = jnp.dot(
            keys, jnp.concatenate([zero, gt], axis=0), preferred_element_type=F32
        )
        pieces = []
        for i, t in enumerate(tiles):
            bias = jnp.where(valid_ref[t] > 0, 0.0, NEG_FILL).astype(F32)
            pieces.append(scores[i * TILE : (i + 1) * TILE] + bias)
        scores = jnp.concatenate(pieces, axis=0)
        top = jnp.max(scores, axis=0, keepdims=True)
        expo = jnp.exp(scores - top)
        probs = expo * (1.0 / jnp.sum(expo, axis=0, keepdims=True))
        low = probs.astype(BF16)
        keys_t = jnp.concatenate([kvt[t, 0:HD] for t in tiles], axis=1)
        values_t = jnp.concatenate([kvt[t, HD:] for t in tiles], axis=1)
        attended = jnp.dot(values_t, low, preferred_element_type=F32)
        center = jnp.sum(attended * gt.astype(F32), axis=0, keepdims=True)
        grad_scores = (probs * (grad_probs - center)).astype(BF16)
        grad_q = jnp.dot(keys_t, grad_scores, preferred_element_type=F32) * SCALE
        out_ref[b, 0:HD, :] = attended.astype(BF16)
        out_ref[b, HD : 2 * HD, :] = grad_q.astype(BF16)
        flipped = jnp.concatenate([qt, gt], axis=0).T
        lane = lax.broadcasted_iota(jnp.int32, flipped.shape, 1)
        nothing = jnp.zeros_like(flipped)
        right = jnp.concatenate(
            [jnp.where(lane < HD, flipped, nothing), jnp.where(lane < HD, nothing, flipped)],
            axis=0,
        )
        terms = jnp.dot(
            jnp.concatenate([grad_scores, low], axis=1), right, preferred_element_type=F32
        )
        for i, t in enumerate(tiles):
            dkv[t] += terms[i * TILE : (i + 1) * TILE]
        return carry

    lax.fori_loop(0, blocks, block, 0)

    def finish(b, carry):
        both = jnp.concatenate([dkv[2 * b], dkv[2 * b + 1]], axis=0)
        out_ref[b, 2 * HD :, :] = both.T.astype(BF16)
        return carry

    lax.fori_loop(0, blocks, finish, 0)


def attend(tiles, valid, arrived):
    blocks, rows, tok = arrived.shape
    total = blocks * tok // TILE
    slots = 10 * TILE
    return pl.pallas_call(
        attend_body,
        in_specs=[
            pl.BlockSpec(memory_space=pltpu.SMEM),
            pl.BlockSpec(memory_space=pltpu.SMEM),
            pl.BlockSpec(memory_space=pltpu.VMEM),
        ],
        out_specs=pl.BlockSpec(memory_space=pltpu.VMEM),
        out_shape=jax.ShapeDtypeStruct(arrived.shape, BF16),
        scratch_shapes=[
            pltpu.VMEM((total, TILE, 2 * HD), BF16),
            pltpu.VMEM((total, 2 * HD, TILE), BF16),
            pltpu.VMEM((total, TILE, 2 * HD), F32),
        ],
        compiler_params=pltpu.CompilerParams(vmem_limit_bytes=48 * 2**20),
        cost_estimate=pl.CostEstimate(
            flops=blocks * 6 * 2 * tok * slots * HD,
            bytes_accessed=4 * 2**20,
            transcendentals=blocks * tok * slots,
        ),
        name="attend",
    )(tiles, valid, arrived)


def shards(inputs, cotangent, key_tiles, tile_valid, w_qkv, w_out):
    width = inputs.shape[2]
    x = inputs[0]
    cot = cotangent[0]
    myself = lax.axis_index("seq")
    sent = project(x, cot, w_qkv, w_out)
    arrived = lax.all_to_all(sent, "seq", split_axis=0, concat_axis=0, tiled=True)
    group_tiles = lax.dynamic_index_in_dim(key_tiles[0], myself // 4, 0, keepdims=False)
    results = attend(group_tiles, tile_valid[0], arrived)
    back = lax.all_to_all(results, "seq", split_axis=0, concat_axis=0, tiled=True)
    heads = jnp.stack([back[slot_of(h)] for h in range(H)], axis=0)
    tok = heads.shape[-1]
    heads = heads.reshape(H, 4, HD, tok).swapaxes(0, 1).reshape(4, width, tok)
    attended_t = heads[0]
    grad_proj_t = heads[1:].reshape(3 * width, tok)
    outputs = jnp.einsum("dt,de->te", attended_t, w_out, preferred_element_type=F32).astype(BF16)
    grad_inputs = jnp.einsum("et,de->td", grad_proj_t, w_qkv, preferred_element_type=F32).astype(
        BF16
    )
    first_part = jnp.einsum("td,et->de", x, grad_proj_t, preferred_element_type=F32)
    second_part = jnp.einsum("dt,te->de", attended_t, cot, preferred_element_type=F32)
    rows = width // 16
    whole = lax.psum(jnp.concatenate([first_part, second_part], axis=1), ("seq", "slide"))
    share = lax.dynamic_slice_in_dim(whole, myself * rows, rows, 0)
    return (outputs[None], grad_inputs[None], share[:, : 3 * width], share[:, 3 * width :])


def solution(mesh):
    placed = (
        P("slide", "seq", None),
        P("slide", "seq", None),
        P("slide", None, None, None),
        P("slide", None),
        P(),
        P(),
    )
    return jax.shard_map(
        shards,
        mesh=mesh,
        in_specs=placed,
        out_specs=(
            P("slide", "seq", None),
            P("slide", "seq", None),
            P("seq", None),
            P("seq", None),
        ),
        check_vma=False,
    )
```

time: 710 us -> 310 us (0.44); the launches traced: 700 us -> 310 us
  local copies, waits for them, and re-layouts: 178 us -> 12 us
  matrix products: 174 us -> 10.4 us
  waiting for transfers between devices: 251 us -> 188 us
  starting transfers between devices: 51.4 us -> 8.77 us
  Pallas kernels: 0 us -> 40.9 us
  blocking collectives: 0 us -> 28 us
  other arithmetic: 30.4 us -> 7.45 us
    dot_general x30 -> x4, matrix products: 155 us -> 10.4 us  [the longest x1 3.91 us: shards(): jnp.einsum('td,et->de', x, grad_proj_t, preferred_element_type=F32)]
    slice x36 -> x5, local copies, waits for them, and re-layouts: 68.6 us -> 3.58 us  [the longest x1 2.03 us: shards(): share[:, :3 * width]]
    all_to_all x8 -> x1, waiting for transfers between devices: 89.1 us -> 27.7 us  [shards(): lax.all_to_all(sent, 'seq', split_axis=0, concat_axis=0, tiled=True)]
    all_to_all x8 -> x1, starting transfers between devices: 51.1 us -> 8.73 us  [shards(): lax.all_to_all(sent, 'seq', split_axis=0, concat_axis=0, tiled=True)]
    pallas_call x0 -> x2, Pallas kernels: none -> 40.9 us  [the longest x1 34.9 us: attend(): pl.pallas_call(attend_body, in_specs=[pl.BlockSpec(memory_space=pltpu.SME...]
    all_to_all x0 -> x1, blocking collectives: none -> 28 us  [shards(): lax.all_to_all(results, 'seq', split_axis=0, concat_axis=0, tiled=True)]
    all_to_all x8 -> x0, local copies, waits for them, and re-layouts: 25.8 us -> none  [the longest x4 13 us: give_back(): lax.all_to_all(back[:, :, group], 'seq', split_axis=1, concat_axis=1, til...]
    squeeze x10 -> x2, local copies, waits for them, and re-layouts: 25.4 us -> 0.08 us  [shards(): lax.dynamic_index_in_dim(key_tiles[0], myself // 4, 0, keepdims=False)]
  transfers between devices with their start and end apart: 9 -> 2, of which waited for: 7 -> 2; matrix products, arithmetic and copies ran while one was open for 20% -> 2% of each run, Pallas kernels for 0% -> 0%
where the time goes in v1:
time: 310 us
  waiting for transfers between devices  188 us (61%)
  Pallas kernels  40.9 us (13%)
  blocking collectives  28 us (9%)
  between operations  14.2 us (5%)
  local copies, waits for them, and re-layouts  12 us (4%)
  matrix products  10.4 us (3%)
  starting transfers between devices  8.77 us (3%)
  other arithmetic  7.45 us (2%)
    psum x1, waiting for transfers between devices, shards(): lax.psum(jnp.concatenate([first_part, second_part], axis=1), ('seq', 'sli...  160 us
    pallas_call x1, Pallas kernels, attend(): pl.pallas_call(attend_body, in_specs=[pl.BlockSpec(memory_space=pltpu.SME...  34.9 us
    all_to_all x1, blocking collectives, shards(): lax.all_to_all(results, 'seq', split_axis=0, concat_axis=0, tiled=True)  28 us
    all_to_all x1, waiting for transfers between devices, shards(): lax.all_to_all(sent, 'seq', split_axis=0, concat_axis=0, tiled=True)  27.7 us
    all_to_all x1, starting transfers between devices, shards(): lax.all_to_all(sent, 'seq', split_axis=0, concat_axis=0, tiled=True)  8.73 us
    unnamed x24, local copies, waits for them, and re-layouts  8.16 us
    concatenate x1, other arithmetic, shards(): jnp.concatenate([first_part, second_part], axis=1)  7.27 us
  transfers between devices with their start and end apart: 2, of which 2 were waited for; matrix products, arithmetic and copies ran while one was open for 2% of the time, Pallas kernels for 0%

profile of v1, /device:TPU:1, one launch (start us, length us, event | category | flops | bytes accessed | tf_op | source)
XLA Modules:
  0.0 309.7 jit_solution(6023530512359267646)
XLA Ops:
  7.2 0.0 copy-start
  7.2 0.0 copy-start.1
  7.2 2.0 copy-done.1
  9.2 0.0 copy-start.3
  9.2 1.3 copy-done.3
  10.5 0.0 copy-start.4
  10.5 1.0 copy-done.4
  11.5 0.0 copy-start.6
  11.5 1.0 copy-done.6
  12.5 6.0 %project.1 = bf16[16,256,256]{2,1,0:T(8,128)(2,1)} custom-call(bf16[256,768]{1,0:T(8,128)(2,1)S(1)} %bitcast.27, bf16[256,768]{1,0:T(8,128)(2,1)S(1)} %bitcast.28, bf16[768,2304]{1,0:T(8,128)(2,1)S(1)} %copy-done.1, bf16[768,2304]{1,0:T(8,128)(2,1)S(1)} %copy-done.1, bf16[768,2304]{1,0:T(8,128)(2,1)S(1)} %copy-done.1, bf16[768,768]{1,0:T(8,128)(2,1)S(1)} %copy-done.3), custom_call_target="tpu_custom_call" | custom-call | flops 1207959552 | bytes 8388608 | tf_op jit(solution)/shard_map/project/pallas_call | solution.py:55
  18.5 0.0 copy-start.8
  18.5 8.7 %all-to-all-start = ((bf16[16,256,256]{2,1,0:T(8,128)(2,1)}), bf16[16,256,256]{2,1,0:T(8,128)(2,1)S(1)}, u32[]{:S(2)}, u32[]{:S(2)}) async-start(bf16[16,256,256]{2,1,0:T(8,128)(2,1)} %project.1), calls=%async_computation | async-start | bytes 4194304 | tf_op jit(solution)/shard_map/all_to_all | solution.py:178
  27.2 0.0 all-reduce.2.cloned.1.call-start
  27.3 0.0 copy-done
  27.3 0.1 copy.13.tiles_ref
  27.4 27.7 %all-to-all-done.in_ref = bf16[16,256,256]{2,1,0:T(8,128)(2,1)S(1)} async-done(((bf16[16,256,256]{2,1,0:T(8,128)(2,1)}), bf16[16,256,256]{2,1,0:T(8,128)(2,1)S(1)}, u32[]{:S(2)}, u32[]{:S(2)}) %all-to-all-start) | async-done | bytes 2097184 | tf_op jit(solution)/shard_map/all_to_all | solution.py:178
  55.1 0.0 copy-done.8
  55.1 34.9 %attend.1 = bf16[16,256,256]{2,1,0:T(8,128)(2,1)S(1)} custom-call(s32[16,8]{1,0:T(8,128)S(1)} %copy.13.tiles_ref, s32[32]{0:T(128)S(1)} %bitcast.29, bf16[16,256,256]{2,1,0:T(8,128)(2,1)S(1)} %all-to-all-done.in_ref), custom_call_target="tpu_custom_call" | custom-call | flops 4026531840 | bytes 4194304 | tf_op jit(solution)/shard_map/attend/pallas_call | solution.py:148
  90.0 28.0 %all_to_all.10 = bf16[16,256,256]{2,1,0:T(8,128)(2,1)S(1)} all-to-all(bf16[16,256,256]{2,1,0:T(8,128)(2,1)S(1)} %attend.1), channel_id=1, replica_groups=mesh['seq'=16,'slide'=8] {'seq'}, dimensions={0} | all-to-all | bytes 4194304 | tf_op jit(solution)/shard_map/all_to_all | solution.py:181
  117.9 0.1 fusion.5
  118.1 0.2 pad_maximum_fusion.1
  118.2 0.2 copy.18
  118.4 0.0 copy-start.7
  118.5 0.0 copy-start.10
  118.5 0.1 slice.46
  118.6 0.0 copy-start.9
  118.6 0.0 copy-start.5
  118.6 0.9 copy-done.7
  119.6 0.5 fusion.2
  120.1 0.0 copy-done.10
  120.1 0.0 copy-done.9
  120.1 0.0 copy-done.5
  120.1 3.9 %convolution_bitcast_fusion = f32[768,2304]{0,1:T(8,128)} fusion(bf16[2304,256]{1,0:T(8,128)(2,1)S(1)} %bitcast.30, bf16[1,256,768]{2,1,0:T(8,128)(2,1)S(1)} %copy-done.5), kind=kOutput, calls=%fused_computation.1 | convolution fusion | flops 905969664 | bytes 8650752 | tf_op jit(solution)/shard_map/td,et->de/dot_general | solution.py:191
  124.0 7.3 %pad_maximum_fusion = f32[768,3072]{0,1:T(8,128)} fusion(f32[768,768]{0,1:T(8,128)S(1)} %fusion.2, f32[768,2304]{0,1:T(8,128)} %convolution_bitcast_fusion), kind=kLoop, calls=%fused_computation | loop fusion | flops 2359296 | bytes 18874368 | tf_op jit(solution)/shard_map/concatenate | solution.py:194
  131.3 0.0 copy-start.2
  131.3 0.0 all-reduce.2.cloned.1.call-update
  131.3 2.8 fusion
  134.1 0.0 copy-done.2
  134.1 3.1 %fusion.1 = bf16[1,256,768]{2,1,0:T(8,128)(2,1)} fusion(bf16[2304,256]{1,0:T(8,128)(2,1)} %bitcast.31, bf16[768,2304]{1,0:T(8,128)(2,1)S(1)} %copy-done.2), kind=kOutput, calls=%fused_computation.7 | convolution fusion | flops 906166272 | bytes 5111808 | tf_op jit(solution)/shard_map/et,de->td/dot_general | solution.py:188
  137.3 160.3 %all-reduce.2.cloned.1.call-done = f32[768,3072]{0,1:T(8,128)} async-done(((f32[768,3072]{0,1:T(8,128)}), f32[768,3072]{0,1:T(8,128)}) %all-reduce.2.cloned.1.call-update) | async-done | bytes 9437200 | tf_op jit(solution)/shard_map/psum | solution.py:194
  297.6 2.0 constant_dynamic-slice_fusion
  299.6 1.1 copy.15
  300.7 1.3 dynamic-slice.2
  302.0 0.8 copy.16
  (2 shorter events, 0.0 us)
Async XLA Ops:
  7.2 20.1 %copy-start = (s32[1,4,16,8]{2,3,1,0:T(8,128)S(1)}, s32[1,4,16,8]{2,3,1,0:T(8,128)}, u32[]{:S(2)}) copy-start(s32[1,4,16,8]{2,3,1,0:T(8,128)} %param.8) | copy-start | bytes 6148
  7.2 2.0 copy-start.1
  9.2 1.3 copy-start.3
  10.5 1.0 copy-start.4
  11.5 1.0 copy-start.6
  18.5 36.6 %copy-start.8 = (s32[1,32]{1,0:T(1,128)S(1)}, s32[1,32]{1,0:T(1,128)}, u32[]{:S(2)}) copy-start(s32[1,32]{1,0:T(1,128)} %param.9) | copy-start | bytes 388
  18.5 36.6 %all-to-all-start = ((bf16[16,256,256]{2,1,0:T(8,128)(2,1)}), bf16[16,256,256]{2,1,0:T(8,128)(2,1)S(1)}, u32[]{:S(2)}, u32[]{:S(2)}) async-start(bf16[16,256,256]{2,1,0:T(8,128)(2,1)} %project.1), calls=%async_computation | async-start | bytes 4194304 | tf_op jit(solution)/shard_map/all_to_all | solution.py:178
  27.2 270.4 %all-reduce.2.cloned.1.call-start = ((), (), s32[]{:S(2)}) async-start(), calls=%async_computation.2 | async-start | bytes 18874368 | tf_op jit(solution)/shard_map/psum | solution.py:194
  118.4 1.1 copy-start.7
  118.5 1.6 copy-start.10
  118.6 1.5 copy-start.9
  118.6 1.5 copy-start.5
  131.3 2.8 copy-start.2
Sparse Core Ops, SparseCore 0:
  131.4 166.0 all-reduce.1

commit v2 on v1

--- a/solution.py
+++ b/solution.py
@@ -169,18 +169,85 @@
     )(tiles, valid, arrived)
 
 
+def weigh_body(res_ref, x_ref, out_ref, acc):
+    step = pl.program_id(0)
+    part = jnp.dot(res_ref[0, HD:, :], x_ref[0], preferred_element_type=F32)
+
+    @pl.when(step == 0)
+    def _():
+        acc[...] = part
+
+    @pl.when(step > 0)
+    def _():
+        acc[...] += part
+
+    @pl.when(step == pl.num_programs(0) - 1)
+    def _():
+        out_ref[...] = acc[...].T.astype(BF16)
+
+
+def weigh(results, x_all):
+    blocks, rows, tok = results.shape
+    width = x_all.shape[2]
+    wide = rows - HD
+    return pl.pallas_call(
+        weigh_body,
+        grid=(blocks,),
+        in_specs=[
+            pl.BlockSpec((1, rows, tok), lambda i: (i, 0, 0)),
+            pl.BlockSpec((1, tok, width), lambda i: (i, 0, 0)),
+        ],
+        out_specs=pl.BlockSpec((width, wide), lambda i: (0, 0)),
+        out_shape=jax.ShapeDtypeStruct((width, wide), BF16),
+        scratch_shapes=[pltpu.VMEM((wide, width), F32)],
+        compiler_params=pltpu.CompilerParams(vmem_limit_bytes=32 * 2**20),
+        cost_estimate=pl.CostEstimate(
+            flops=2 * blocks * tok * width * wide,
+            bytes_accessed=9 * 2**20,
+            transcendentals=0,
+        ),
+        name="weigh",
+    )(results, x_all)
+
+
+def swap_cores(value):
+    return lax.ppermute(value, "slide", [(i, i ^ 1) for i in range(lax.axis_size("slide"))])
+
+
+def sum_slides(part):
+    n = lax.axis_size("slide")
+    core = lax.rem(lax.axis_index("slide"), 2)
+    halves = part.reshape(2, part.shape[0] // 2, part.shape[1])
+    mine = lax.dynamic_index_in_dim(halves, core, 0, keepdims=False)
+    theirs = lax.dynamic_index_in_dim(halves, 1 - core, 0, keepdims=False)
+    chip = (mine.astype(F32) + swap_cores(theirs).astype(F32)).astype(BF16)
+    others = [
+        lax.ppermute(chip, "slide", [(i, (i + 2 * k) % n) for i in range(n)]).astype(F32)
+        for k in (1, 2, 3)
+    ]
+    total = (chip.astype(F32) + others[1]) + (others[0] + others[2])
+    rest = swap_cores(total)
+    return jnp.where(
+        core == 0,
+        jnp.concatenate([total, rest], axis=0),
+        jnp.concatenate([rest, total], axis=0),
+    )
+
+
 def shards(inputs, cotangent, key_tiles, tile_valid, w_qkv, w_out):
     width = inputs.shape[2]
     x = inputs[0]
     cot = cotangent[0]
+    tok = x.shape[0]
+    peers = lax.axis_size("seq")
     myself = lax.axis_index("seq")
+    x_all = lax.all_gather(x, "seq", axis=0)
     sent = project(x, cot, w_qkv, w_out)
     arrived = lax.all_to_all(sent, "seq", split_axis=0, concat_axis=0, tiled=True)
     group_tiles = lax.dynamic_index_in_dim(key_tiles[0], myself // 4, 0, keepdims=False)
     results = attend(group_tiles, tile_valid[0], arrived)
     back = lax.all_to_all(results, "seq", split_axis=0, concat_axis=0, tiled=True)
     heads = jnp.stack([back[slot_of(h)] for h in range(H)], axis=0)
-    tok = heads.shape[-1]
     heads = heads.reshape(H, 4, HD, tok).swapaxes(0, 1).reshape(4, width, tok)
     attended_t = heads[0]
     grad_proj_t = heads[1:].reshape(3 * width, tok)
@@ -188,12 +255,23 @@
     grad_inputs = jnp.einsum("et,de->td", grad_proj_t, w_qkv, preferred_element_type=F32).astype(
         BF16
     )
-    first_part = jnp.einsum("td,et->de", x, grad_proj_t, preferred_element_type=F32)
-    second_part = jnp.einsum("dt,te->de", attended_t, cot, preferred_element_type=F32)
-    rows = width // 16
-    whole = lax.psum(jnp.concatenate([first_part, second_part], axis=1), ("seq", "slide"))
-    share = lax.dynamic_slice_in_dim(whole, myself * rows, rows, 0)
-    return (outputs[None], grad_inputs[None], share[:, : 3 * width], share[:, 3 * width :])
+    rows = width // peers
+    in_part = weigh(results, x_all)
+    out_part = jnp.einsum("dt,te->de", attended_t, cot, preferred_element_type=F32).astype(BF16)
+    chunks = jnp.concatenate([in_part, out_part], axis=1).reshape(peers, rows, -1)
+    spread = lax.all_to_all(chunks, "seq", split_axis=0, concat_axis=0, tiled=True)
+    wide = 3 * HD
+    in_rows = jnp.concatenate(
+        [
+            spread[slot_of(h), :, m * HD : (m + 1) * HD]
+            for m in range(3)
+            for h in range(H)
+        ],
+        axis=1,
+    )
+    out_rows = jnp.sum(spread[:, :, wide:].astype(F32), axis=0).astype(BF16)
+    total = sum_slides(jnp.concatenate([in_rows, out_rows], axis=1))
+    return (outputs[None], grad_inputs[None], total[:, : 3 * width], total[:, 3 * width :])
 
 
 def solution(mesh):

time: 310 us -> 211 us (0.68)
  waiting for transfers between devices: 188 us -> 61.5 us
  starting transfers between devices: 8.77 us -> 22.5 us
  local copies, waits for them, and re-layouts: 12 us -> 23.2 us
  matrix products: 10.4 us -> 4.8 us
  Pallas kernels: 40.9 us -> 46 us
  blocking collectives: 28 us -> 32.6 us
    psum x1 -> x0, waiting for transfers between devices: 160 us -> none  [shards(): lax.psum(jnp.concatenate([first_part, second_part], axis=1), ('seq', 'sli...]
    all_to_all x0 -> x1, waiting for transfers between devices: none -> 20.2 us  [shards(): lax.all_to_all(chunks, 'seq', split_axis=0, concat_axis=0, tiled=True)]
    ppermute x0 -> x5, starting transfers between devices: none -> 9.9 us  [the longest x2 5.8 us: swap_cores(): lax.ppermute(value, 'slide', [(i, i ^ 1) for i in range(lax.axis_size('sl...]
    ppermute x0 -> x5, waiting for transfers between devices: none -> 8 us  [the longest x3 6.65 us: sum_slides(): lax.ppermute(chip, 'slide', [(i, (i + 2 * k) % n) for i in range(n)])]
    concatenate x1, other arithmetic: 7.27 us -> 1.37 us  [shards(): jnp.concatenate([in_part, out_part], axis=1).reshape(peers, rows, -1)]
    pallas_call x0 -> x1, Pallas kernels: none -> 5.08 us  [weigh(): pl.pallas_call(weigh_body, grid=(blocks,), in_specs=[pl.BlockSpec((1, row...]
    all_to_all x1, waiting for transfers between devices: 27.7 us -> 32.6 us  [shards(): lax.all_to_all(sent, 'seq', split_axis=0, concat_axis=0, tiled=True)]
    unnamed x24 -> x30, local copies, waits for them, and re-layouts: 8.16 us -> 12.9 us
  transfers between devices with their start and end apart: 2 -> 8, of which waited for: 2 -> 5; matrix products, arithmetic and copies ran while one was open for 2% -> 3% of each run, Pallas kernels for 0% -> 19%
where the time goes in v2:
time: 211 us; the launch traced here: 210 us
  waiting for transfers between devices  61.5 us (29%)
  Pallas kernels  46 us (22%)
  blocking collectives  32.6 us (15%)
  local copies, waits for them, and re-layouts  23.2 us (11%)
  starting transfers between devices  22.5 us (11%)
  between operations  14.2 us (7%)
  other arithmetic  5.62 us (3%)
  matrix products  4.8 us (2%)
    pallas_call x1, Pallas kernels, attend(): pl.pallas_call(attend_body, in_specs=[pl.BlockSpec(memory_space=pltpu.SME...  34.9 us
    all_to_all x1, waiting for transfers between devices, shards(): lax.all_to_all(sent, 'seq', split_axis=0, concat_axis=0, tiled=True)  32.6 us
    all_to_all x1, blocking collectives, shards(): lax.all_to_all(results, 'seq', split_axis=0, concat_axis=0, tiled=True)  32.6 us
    all_to_all x1, waiting for transfers between devices, shards(): lax.all_to_all(chunks, 'seq', split_axis=0, concat_axis=0, tiled=True)  20.2 us
    unnamed x30, local copies, waits for them, and re-layouts  12.9 us
    all_to_all x1, starting transfers between devices, shards(): lax.all_to_all(sent, 'seq', split_axis=0, concat_axis=0, tiled=True)  8.73 us
    ppermute x3, waiting for transfers between devices, sum_slides(): lax.ppermute(chip, 'slide', [(i, (i + 2 * k) % n) for i in range(n)])  6.65 us
    pallas_call x1, Pallas kernels, project(): pl.pallas_call(project_body, grid=(pairs,), in_specs=[pl.BlockSpec((tok,...  6.08 us
  transfers between devices with their start and end apart: 8, of which 5 were waited for; matrix products, arithmetic and copies ran while one was open for 3% of the time, Pallas kernels for 19%

profile of v2, /device:TPU:1, one launch (start us, length us, event | category | flops | bytes accessed | tf_op | source)
XLA Modules:
  0.0 210.4 jit_solution(8640597580325868057)
XLA Ops:
  7.2 0.0 copy-start
  7.2 0.0 all-gather.2.cloned.1.call-start
  7.2 0.7 all-gather.2.cloned.1.call-update
  7.9 0.0 copy-start.1
  7.9 2.0 copy-done.1
  9.9 0.0 copy-start.4
  9.9 1.3 copy-done.4
  11.2 0.0 copy-start.8
  11.2 1.0 copy-done.8
  12.2 0.0 copy-start.9
  12.2 1.0 copy-done.9
  13.2 6.1 %project.1 = bf16[16,256,256]{2,1,0:T(8,128)(2,1)} custom-call(bf16[256,768]{1,0:T(8,128)(2,1)S(1)} %bitcast.65, bf16[256,768]{1,0:T(8,128)(2,1)S(1)} %bitcast.66, bf16[768,2304]{1,0:T(8,128)(2,1)S(1)} %copy-done.1, bf16[768,2304]{1,0:T(8,128)(2,1)S(1)} %copy-done.1, bf16[768,2304]{1,0:T(8,128)(2,1)S(1)} %copy-done.1, bf16[768,768]{1,0:T(8,128)(2,1)S(1)} %copy-done.4), custom_call_target="tpu_custom_call" | custom-call | flops 1207959552 | bytes 8388608 | tf_op jit(solution)/shard_map/project/pallas_call | solution.py:55
  19.3 0.0 copy-start.11
  19.3 8.7 %all-to-all-start = ((bf16[16,256,256]{2,1,0:T(8,128)(2,1)}), bf16[16,256,256]{2,1,0:T(8,128)(2,1)S(1)}, u32[]{:S(2)}, u32[]{:S(2)}) async-start(bf16[16,256,256]{2,1,0:T(8,128)(2,1)} %project.1), calls=%async_computation | async-start | bytes 4194304 | tf_op jit(solution)/shard_map/all_to_all | solution.py:246
  28.0 0.0 copy-done
  28.1 0.1 copy.52.tiles_ref
  28.1 32.6 %all-to-all-done.in_ref = bf16[16,256,256]{2,1,0:T(8,128)(2,1)S(1)} async-done(((bf16[16,256,256]{2,1,0:T(8,128)(2,1)}), bf16[16,256,256]{2,1,0:T(8,128)(2,1)S(1)}, u32[]{:S(2)}, u32[]{:S(2)}) %all-to-all-start) | async-done | bytes 2097184 | tf_op jit(solution)/shard_map/all_to_all | solution.py:246
  60.7 1.4 copy-done.6
  62.1 0.0 copy-done.11
  62.1 1.6 copy-done.7
  63.7 34.9 %attend.1.res_ref = bf16[16,256,256]{2,1,0:T(8,128)(2,1)S(1)} custom-call(s32[16,8]{1,0:T(8,128)S(1)} %copy.52.tiles_ref, s32[32]{0:T(128)S(1)} %bitcast.67, bf16[16,256,256]{2,1,0:T(8,128)(2,1)S(1)} %copy-done.7), custom_call_target="tpu_custom_call" | custom-call | flops 4026531840 | bytes 4194304 | tf_op jit(solution)/shard_map/attend/pallas_call | solution.py:148
  98.6 32.6 %all_to_all.15 = bf16[16,256,256]{2,1,0:T(8,128)(2,1)S(1)} all-to-all(bf16[16,256,256]{2,1,0:T(8,128)(2,1)S(1)} %attend.1.res_ref), channel_id=1, replica_groups=mesh['seq'=16,'slide'=8] {'seq'}, dimensions={0} | all-to-all | bytes 4194304 | tf_op jit(solution)/shard_map/all_to_all | solution.py:249
  131.2 0.1 fusion.4
  131.3 0.2 pad_maximum_fusion
  131.5 0.0 copy-start.10
  131.5 0.2 copy.57
  131.6 0.0 copy-start.12
  131.7 1.1 copy-done.12
  132.8 0.0 copy-start.13
  132.8 0.7 copy-done.13
  133.6 0.0 copy-done.10
  133.6 1.6 convolution_convert_fusion
  135.2 2.8 %copy-done.3 = bf16[16,256,768]{2,1,0:T(8,128)(2,1)S(1)} copy-done((bf16[16,256,768]{2,1,0:T(8,128)(2,1)S(1)}, bf16[16,256,768]{2,1,0:T(8,128)(2,1)}, u32[]{:S(2)}) %copy-start.3) | copy-done | bytes 6291480
  138.0 5.1 %weigh.1 = bf16[768,192]{1,0:T(8,128)(2,1)S(1)} custom-call(bf16[16,256,256]{2,1,0:T(8,128)(2,1)S(1)} %attend.1.res_ref, bf16[16,256,768]{2,1,0:T(8,128)(2,1)S(1)} %copy-done.3), custom_call_target="tpu_custom_call" | custom-call | flops 1207959552 | bytes 9437184 | tf_op jit(solution)/shard_map/weigh/pallas_call | solution.py:193
  143.1 0.2 copy.54
  143.2 1.4 pad_maximum_fusion.1
  144.6 1.7 copy.55
  146.3 3.8 %all-to-all-start.2 = ((bf16[16,48,960]{2,1,0:T(8,128)(2,1)}), bf16[16,48,960]{2,1,0:T(8,128)(2,1)S(1)}, u32[]{:S(2)}, u32[]{:S(2)}) async-start(bf16[16,48,960]{2,1,0:T(8,128)(2,1)} %bitcast.10), calls=%async_computation.2 | async-start | bytes 3145728 | tf_op jit(solution)/shard_map/all_to_all | solution.py:262
  150.1 20.2 %all-to-all-done.2 = bf16[16,48,960]{2,1,0:T(8,128)(2,1)S(1)} async-done(((bf16[16,48,960]{2,1,0:T(8,128)(2,1)}), bf16[16,48,960]{2,1,0:T(8,128)(2,1)S(1)}, u32[]{:S(2)}, u32[]{:S(2)}) %all-to-all-start.2) | async-done | bytes 1474592 | tf_op jit(solution)/shard_map/all_to_all | solution.py:262
  170.3 1.2 slice_reduce_fusion
  171.5 0.7 fusion.6
  172.2 0.8 fusion.5
  172.9 2.2 %concatenate.125 = bf16[2,24,3072]{2,1,0:T(8,128)(2,1)} concatenate(bf16[2,24,64]{2,1,0:T(8,128)(2,1)} %bitcast.91, bf16[2,24,64]{2,1,0:T(8,128)(2,1)} %bitcast.90, bf16[2,24,64]{2,1,0:T(8,128)(2,1)} %bitcast.89, bf16[2,24,64]{2,1,0:T(8,128)(2,1)} %bitcast.88, bf16[2,24,64]{2,1,0:T(8,128)(2,1)} %bitcast.87, bf16[2,24,64]{2,1,0:T(8,128)(2,1)} %bitcast.86, ...), dimensions={2} | concatenate | bytes 589824 | tf_op jit(solution)/shard_map/concatenate | solution.py:273
  175.2 1.6 dynamic-slice_bitcast_fusion
  176.8 4.3 %collective-permute-start = (bf16[24,3072]{1,0:T(8,128)(2,1)}, bf16[24,3072]{1,0:T(8,128)(2,1)}, u32[]{:S(2)}, u32[]{:S(2)}) collective-permute-start(bf16[24,3072]{1,0:T(8,128)(2,1)} %dynamic-slice_bitcast_fusion), channel_id=1, source_target_pairs={{0,1},{1,0},{2,3},{3,2},{4,5},{5,4},{6,7},{7,6},{8,9},{9,8},{10,11... | collective-permute-start | bytes 442376 | tf_op jit(solution)/shard_map/ppermute | solution.py:214
  181.1 1.3 collective-permute-done
  182.4 1.7 fusion.2
  184.1 2.6 %collective-permute-start.3 = (bf16[24,3072]{1,0:T(8,128)(2,1)}, bf16[24,3072]{1,0:T(8,128)(2,1)}, u32[]{:S(2)}, u32[]{:S(2)}) collective-permute-start(bf16[24,3072]{1,0:T(8,128)(2,1)} %fusion.2), channel_id=1, source_target_pairs={{0,6},{1,7},{2,0},{3,1},{4,2},{5,3},{6,4},{7,5},{8,14},{9,15},{10,... | collective-permute-start | bytes 442376 | tf_op jit(solution)/shard_map/ppermute | solution.py:225
  186.7 0.0 collective-permute-start.2
  186.7 1.5 collective-permute-start.1
  188.2 1.3 slice.194
  189.6 0.3 collective-permute-done.3
  189.9 6.4 %collective-permute-done.2 = bf16[24,3072]{1,0:T(8,128)(2,1)} collective-permute-done((bf16[24,3072]{1,0:T(8,128)(2,1)}, bf16[24,3072]{1,0:T(8,128)(2,1)}, u32[]{:S(2)}, u32[]{:S(2)}) %collective-permute-start.2) | collective-permute-done | bytes 147488 | tf_op jit(solution)/shard_map/ppermute | solution.py:225
  196.2 0.0 collective-permute-done.1
  196.2 1.2 add_add_fusion
  197.4 1.5 collective-permute-start.4
  198.9 0.0 copy-done.2
  198.9 1.9 fusion.1
  200.8 0.0 copy-done.5
  200.8 0.0 copy-done.14
  200.8 1.3 fusion
  202.1 0.0 collective-permute-done.4
  202.1 0.7 slice.233
  202.8 0.8 slice.232
  (10 shorter events, 0.1 us)
Async XLA Ops:
  7.2 20.9 %copy-start = (s32[1,4,16,8]{2,3,1,0:T(8,128)S(1)}, s32[1,4,16,8]{2,3,1,0:T(8,128)}, u32[]{:S(2)}) copy-start(s32[1,4,16,8]{2,3,1,0:T(8,128)} %param.8) | copy-start | bytes 6148
  7.2 128.0 %all-gather.2.cloned.1.call-start = ((), (), s32[]{:S(2)}) async-start(), calls=%async_computation.3 | async-start | bytes 6684672 | tf_op jit(solution)/shard_map/all_gather | solution.py:244
  7.9 2.0 copy-start.1
  9.9 1.3 copy-start.4
  11.2 1.0 copy-start.8
  12.2 1.0 copy-start.9
  19.3 42.9 %copy-start.11 = (s32[1,32]{1,0:T(1,128)S(1)}, s32[1,32]{1,0:T(1,128)}, u32[]{:S(2)}) copy-start(s32[1,32]{1,0:T(1,128)} %param.9) | copy-start | bytes 388
  19.3 41.5 %all-to-all-start = ((bf16[16,256,256]{2,1,0:T(8,128)(2,1)}), bf16[16,256,256]{2,1,0:T(8,128)(2,1)S(1)}, u32[]{:S(2)}, u32[]{:S(2)}) async-start(bf16[16,256,256]{2,1,0:T(8,128)(2,1)} %project.1), calls=%async_computation | async-start | bytes 4194304 | tf_op jit(solution)/shard_map/all_to_all | solution.py:246
  60.7 1.4 copy-start.6
  62.1 1.6 copy-start.7
  131.5 2.1 %copy-start.10 = (bf16[1,256,768]{2,1,0:T(8,128)(2,1)S(1)}, bf16[1,256,768]{2,1,0:T(8,128)(2,1)}, u32[]{:S(2)}) copy-start(bf16[1,256,768]{2,1,0:T(8,128)(2,1)} %param.7) | copy-start | bytes 1179652
  131.6 1.2 copy-start.12
  132.8 0.7 copy-start.13
  135.2 2.8 %copy-start.3 = (bf16[16,256,768]{2,1,0:T(8,128)(2,1)S(1)}, bf16[16,256,768]{2,1,0:T(8,128)(2,1)}, u32[]{:S(2)}) copy-start(bf16[16,256,768]{2,1,0:T(8,128)(2,1)} %all-gather.2.cloned.1.call-done.x_ref) | copy-start | bytes 18874372
  146.3 24.0 %all-to-all-start.2 = ((bf16[16,48,960]{2,1,0:T(8,128)(2,1)}), bf16[16,48,960]{2,1,0:T(8,128)(2,1)S(1)}, u32[]{:S(2)}, u32[]{:S(2)}) async-start(bf16[16,48,960]{2,1,0:T(8,128)(2,1)} %bitcast.10), calls=%async_computation.2 | async-start | bytes 3145728 | tf_op jit(solution)/shard_map/all_to_all | solution.py:262
  172.9 26.0 %copy-start.2 = (bf16[768,2304]{1,0:T(8,128)(2,1)S(1)}, bf16[768,2304]{1,0:T(8,128)(2,1)}, u32[]{:S(2)}) copy-start(bf16[768,2304]{1,0:T(8,128)(2,1)} %wv_ref.1) | copy-start | bytes 10616836
  176.8 5.7 %collective-permute-start = (bf16[24,3072]{1,0:T(8,128)(2,1)}, bf16[24,3072]{1,0:T(8,128)(2,1)}, u32[]{:S(2)}, u32[]{:S(2)}) collective-permute-start(bf16[24,3072]{1,0:T(8,128)(2,1)} %dynamic-slice_bitcast_fusion), channel_id=1, source_target_pairs={{0,1},{1,0},{2,3},{3,2},{4,5},{5,4},{6,7},{7,6},{8,9},{9,8},{10,11... | collective-permute-start | bytes 442376 | tf_op jit(solution)/shard_map/ppermute | solution.py:214
  184.1 5.7 %collective-permute-start.3 = (bf16[24,3072]{1,0:T(8,128)(2,1)}, bf16[24,3072]{1,0:T(8,128)(2,1)}, u32[]{:S(2)}, u32[]{:S(2)}) collective-permute-start(bf16[24,3072]{1,0:T(8,128)(2,1)} %fusion.2), channel_id=1, source_target_pairs={{0,6},{1,7},{2,0},{3,1},{4,2},{5,3},{6,4},{7,5},{8,14},{9,15},{10,... | collective-permute-start | bytes 442376 | tf_op jit(solution)/shard_map/ppermute | solution.py:225
  186.7 9.5 %collective-permute-start.2 = (bf16[24,3072]{1,0:T(8,128)(2,1)}, bf16[24,3072]{1,0:T(8,128)(2,1)}, u32[]{:S(2)}, u32[]{:S(2)}) collective-permute-start(bf16[24,3072]{1,0:T(8,128)(2,1)} %fusion.2), channel_id=1, source_target_pairs={{0,2},{1,3},{2,4},{3,5},{4,6},{5,7},{6,0},{7,1},{8,10},{9,11},{10,... | collective-permute-start | bytes 442376 | tf_op jit(solution)/shard_map/ppermute | solution.py:225
  186.7 9.5 %collective-permute-start.1 = (bf16[24,3072]{1,0:T(8,128)(2,1)}, bf16[24,3072]{1,0:T(8,128)(2,1)}, u32[]{:S(2)}, u32[]{:S(2)}) collective-permute-start(bf16[24,3072]{1,0:T(8,128)(2,1)} %fusion.2), channel_id=1, source_target_pairs={{0,4},{1,5},{2,6},{3,7},{4,0},{5,1},{6,2},{7,3},{8,12},{9,13},{10,... | collective-permute-start | bytes 442376 | tf_op jit(solution)/shard_map/ppermute | solution.py:225
  197.4 4.7 %collective-permute-start.4 = (f32[24,3072]{1,0:T(8,128)S(1)}, f32[24,3072]{1,0:T(8,128)S(1)}, u32[]{:S(2)}, u32[]{:S(2)}) collective-permute-start(f32[24,3072]{1,0:T(8,128)S(1)} %add_add_fusion), channel_id=1, source_target_pairs={{0,1},{1,0},{2,3},{3,2},{4,5},{5,4},{6,7},{7,6},{8,9},{9,8},{10,11... | collective-permute-start | bytes 884744 | tf_op jit(solution)/shard_map/ppermute | solution.py:214
  198.9 1.9 copy-start.5
  198.9 1.9 copy-start.14
Sparse Core Ops, SparseCore 0:
  10.2 82.4 all-gather.1

commit v3 on v2

v3 whole, which is shorter than its diff:
```python
import jax
import jax.numpy as jnp
from jax import lax
from jax.experimental import pallas as pl
from jax.experimental.pallas import tpu as pltpu
from jax.sharding import PartitionSpec as P

H = 12
HPG = 3
HD = 64
TILE = 128
NEG_FILL = -1e30
F32 = jnp.float32
BF16 = jnp.bfloat16
SCALE = HD ** (-0.5)
NB = 4


def slot_of(head):
    row = head // HPG
    place = head % HPG
    return 4 * row + place + (place >= row)


def project_body(x_ref, cot_ref, wq_ref, wk_ref, wv_ref, wo_ref, out_ref):
    step = pl.program_id(0)
    x = x_ref[...]
    contract = (((0,), (1,)), ((), ()))
    qt = lax.dot_general(wq_ref[...], x, contract, preferred_element_type=F32).astype(BF16)
    kt = lax.dot_general(wk_ref[...], x, contract, preferred_element_type=F32).astype(BF16)
    vt = lax.dot_general(wv_ref[...], x, contract, preferred_element_type=F32).astype(BF16)
    gt = lax.dot_general(
        wo_ref[...], cot_ref[...], (((1,), (1,)), ((), ())), preferred_element_type=F32
    ).astype(BF16)
    qt = qt * jnp.asarray(SCALE, BF16)
    for half in range(2):
        head = 2 * step + half
        row = head // HPG
        place = head - row * HPG
        slot = 4 * row + place + jnp.where(place >= row, 1, 0)
        rows = slice(half * HD, half * HD + HD)
        out_ref[slot, 0:HD, :] = qt[rows]
        out_ref[slot, HD : 2 * HD, :] = kt[rows]
        out_ref[slot, 2 * HD : 3 * HD, :] = vt[rows]
        out_ref[slot, 3 * HD :, :] = gt[rows]

    @pl.when(step == 0)
    def _():
        for row in range(4):
            out_ref[5 * row] = jnp.zeros(out_ref.shape[1:], BF16)


def project(x, cot, w_qkv, w_out):
    tok, width = x.shape
    pairs = H // 2
    return pl.pallas_call(
        project_body,
        grid=(pairs,),
        in_specs=[
            pl.BlockSpec((tok, width), lambda i: (0, 0)),
            pl.BlockSpec((tok, width), lambda i: (0, 0)),
            pl.BlockSpec((width, 2 * HD), lambda i: (0, i)),
            pl.BlockSpec((width, 2 * HD), lambda i: (0, i + pairs)),
            pl.BlockSpec((width, 2 * HD), lambda i: (0, i + 2 * pairs)),
            pl.BlockSpec((2 * HD, width), lambda i: (i, 0)),
        ],
        out_specs=pl.BlockSpec((16, 4 * HD, tok), lambda i: (0, 0, 0)),
        out_shape=jax.ShapeDtypeStruct((16, 4 * HD, tok), BF16),
        compiler_params=pltpu.CompilerParams(vmem_limit_bytes=32 * 2**20),
        cost_estimate=pl.CostEstimate(
            flops=2 * tok * width * 4 * width, bytes_accessed=8 * 2**20, transcendentals=0
        ),
        name="project",
    )(x, cot, w_qkv, w_qkv, w_qkv, w_out)


def forward_body(tiles_ref, valid_ref, in_ref, att_ref, exp_ref, stat_ref, kv, vt):
    b = pl.program_id(0)
    blocks = in_ref.shape[0]
    listed = tiles_ref.shape[1]

    @pl.when(b == 0)
    def _():
        def prepare(i, carry):
            both = in_ref[i, HD : 3 * HD, :]
            flipped = both.T
            for c in range(2):
                vt[2 * i + c] = both[HD:, c * TILE : (c + 1) * TILE]
                kv[2 * i + c] = flipped[c * TILE : (c + 1) * TILE]
            return carry

        lax.fori_loop(0, blocks, prepare, 0)

    work = []
    for n in range(NB):
        p = NB * b + n
        tiles = [2 * p, 2 * p + 1] + [tiles_ref[p, i] for i in range(listed)]
        qt = in_ref[p, 0:HD, :]
        keys = jnp.concatenate([kv[t] for t in tiles], axis=0)
        scores = jnp.dot(
            keys, jnp.concatenate([qt, jnp.zeros_like(qt)], axis=0), preferred_element_type=F32
        )
        work.append((n, p, tiles, scores))
    for n, p, tiles, scores in work:
        gt = in_ref[p, 3 * HD :, :]
        pieces = []
        for i, t in enumerate(tiles):
            bias = jnp.where(valid_ref[t] > 0, 0.0, NEG_FILL).astype(F32)
            pieces.append(scores[i * TILE : (i + 1) * TILE] + bias)
        scores = jnp.concatenate(pieces, axis=0)
        top = jnp.max(scores, axis=0, keepdims=True)
        expo = jnp.exp(scores - top)
        share = 1.0 / jnp.sum(expo, axis=0, keepdims=True)
        low = expo.astype(BF16)
        exp_ref[n] = low
        values_t = jnp.concatenate([vt[t] for t in tiles], axis=1)
        attended = jnp.dot(values_t, low, preferred_element_type=F32) * share
        scaled = (gt.astype(F32) * share).astype(BF16)
        center = jnp.sum(attended * scaled.astype(F32), axis=0, keepdims=True)
        att_ref[p] = attended.astype(BF16)
        stat_ref[p, 0:1, :] = share
        stat_ref[p, 1:2, :] = center


def forward(tiles, valid, arrived):
    blocks, rows, tok = arrived.shape
    total = blocks * tok // TILE
    slots = 10 * TILE
    whole = pl.BlockSpec(memory_space=pltpu.VMEM)
    return pl.pallas_call(
        forward_body,
        grid=(blocks // NB,),
        in_specs=[
            pl.BlockSpec(memory_space=pltpu.SMEM),
            pl.BlockSpec(memory_space=pltpu.SMEM),
            whole,
        ],
        out_specs=[whole, pl.BlockSpec((NB, slots, tok), lambda i: (i, 0, 0)), whole],
        out_shape=[
            jax.ShapeDtypeStruct((blocks, HD, tok), BF16),
            jax.ShapeDtypeStruct((blocks, slots, tok), BF16),
            jax.ShapeDtypeStruct((blocks, 8, tok), F32),
        ],
        scratch_shapes=[
            pltpu.VMEM((total, TILE, 2 * HD), BF16),
            pltpu.VMEM((total, HD, TILE), BF16),
        ],
        compiler_params=pltpu.CompilerParams(vmem_limit_bytes=60 * 2**20),
        cost_estimate=pl.CostEstimate(
            flops=blocks * 4 * 2 * tok * slots * 2 * HD,
            bytes_accessed=14 * 2**20,
            transcendentals=blocks * tok * slots,
        ),
        name="forward",
    )(tiles, valid, arrived)


def backward_body(tiles_ref, in_ref, exp_ref, stat_ref, out_ref, kv, kt, dkv):
    b = pl.program_id(0)
    blocks = in_ref.shape[0]
    listed = tiles_ref.shape[1]

    @pl.when(b == 0)
    def _():
        def prepare(i, carry):
            both = in_ref[i, HD : 3 * HD, :]
            flipped = both.T
            for c in range(2):
                kt[2 * i + c] = both[:HD, c * TILE : (c + 1) * TILE]
                kv[2 * i + c] = flipped[c * TILE : (c + 1) * TILE]
                dkv[2 * i + c] = jnp.zeros((TILE, 2 * HD), F32)
            return carry

        lax.fori_loop(0, blocks, prepare, 0)

    work = []
    for n in range(NB):
        p = NB * b + n
        tiles = [2 * p, 2 * p + 1] + [tiles_ref[p, i] for i in range(listed)]
        gt = in_ref[p, 3 * HD :, :]
        scaled = (gt.astype(F32) * stat_ref[p, 0:1, :]).astype(BF16)
        keys = jnp.concatenate([kv[t] for t in tiles], axis=0)
        grad_probs = jnp.dot(
            keys,
            jnp.concatenate([jnp.zeros_like(scaled), scaled], axis=0),
            preferred_element_type=F32,
        )
        work.append((n, p, tiles, scaled, grad_probs))
    for n, p, tiles, scaled, grad_probs in work:
        qt = in_ref[p, 0:HD, :]
        low = exp_ref[n]
        center = stat_ref[p, 1:2, :]
        grad_scores = (low.astype(F32) * (grad_probs - center)).astype(BF16)
        keys_t = jnp.concatenate([kt[t] for t in tiles], axis=1)
        grad_q = jnp.dot(keys_t, grad_scores, preferred_element_type=F32) * SCALE
        out_ref[p, 0:HD, :] = grad_q.astype(BF16)
        flipped = jnp.concatenate([qt, scaled], axis=0).T
        lane = lax.broadcasted_iota(jnp.int32, flipped.shape, 1)
        nothing = jnp.zeros_like(flipped)
        right = jnp.concatenate(
            [jnp.where(lane < HD, flipped, nothing), jnp.where(lane < HD, nothing, flipped)],
            axis=0,
        )
        terms = jnp.dot(
            jnp.concatenate([grad_scores, low], axis=1), right, preferred_element_type=F32
        )
        for i, t in enumerate(tiles):
            dkv[t] += terms[i * TILE : (i + 1) * TILE]

    @pl.when(b == blocks // NB - 1)
    def _():
        def finish(i, carry):
            both = jnp.concatenate([dkv[2 * i], dkv[2 * i + 1]], axis=0)
            out_ref[i, HD:, :] = both.T.astype(BF16)
            return carry

        lax.fori_loop(0, blocks, finish, 0)


def backward(tiles, arrived, low, stats):
    blocks, rows, tok = arrived.shape
    total = blocks * tok // TILE
    slots = 10 * TILE
    whole = pl.BlockSpec(memory_space=pltpu.VMEM)
    return pl.pallas_call(
        backward_body,
        grid=(blocks // NB,),
        in_specs=[
            pl.BlockSpec(memory_space=pltpu.SMEM),
            whole,
            pl.BlockSpec((NB, slots, tok), lambda i: (i, 0, 0)),
            whole,
        ],
        out_specs=whole,
        out_shape=jax.ShapeDtypeStruct((blocks, 3 * HD, tok), BF16),
        scratch_shapes=[
            pltpu.VMEM((total, TILE, 2 * HD), BF16),
            pltpu.VMEM((total, HD, TILE), BF16),
            pltpu.VMEM((total, TILE, 2 * HD), F32),
        ],
        compiler_params=pltpu.CompilerParams(vmem_limit_bytes=60 * 2**20),
        cost_estimate=pl.CostEstimate(
            flops=blocks * 8 * 2 * tok * slots * 2 * HD,
            bytes_accessed=16 * 2**20,
            transcendentals=0,
        ),
        name="backward",
    )(tiles, arrived, low, stats)


def weigh_body(res_ref, x_ref, back_ref, cot_ref, w_ref, chunk_ref, out_ref, acc):
    step = pl.program_id(0)
    part = jnp.dot(res_ref[0], x_ref[0], preferred_element_type=F32)

    @pl.when(step == 0)
    def _():
        attended = jnp.concatenate([back_ref[slot_of(h)] for h in range(H)], axis=0)
        chunk_ref[:, : cot_ref.shape[1]] = jnp.dot(
            attended, cot_ref[...], preferred_element_type=F32
        ).astype(BF16)
        out_ref[...] = jnp.dot(attended.T, w_ref[...], preferred_element_type=F32).astype(BF16)
        acc[...] = part

    @pl.when(step > 0)
    def _():
        acc[...] += part

    @pl.when(step == pl.num_programs(0) - 1)
    def _():
        chunk_ref[:, cot_ref.shape[1] :] = acc[...].T.astype(BF16)


def weigh(results, x_all, att_back, cot, w_out):
    blocks, wide, tok = results.shape
    width = x_all.shape[2]
    whole = pl.BlockSpec(memory_space=pltpu.VMEM)
    return pl.pallas_call(
        weigh_body,
        grid=(blocks,),
        in_specs=[
            pl.BlockSpec((1, wide, tok), lambda i: (i, 0, 0)),
            pl.BlockSpec((1, tok, width), lambda i: (i, 0, 0)),
            whole,
            whole,
            whole,
        ],
        out_specs=[whole, whole],
        out_shape=[
            jax.ShapeDtypeStruct((width, width + wide), BF16),
            jax.ShapeDtypeStruct((tok, width), BF16),
        ],
        scratch_shapes=[pltpu.VMEM((wide, width), F32)],
        compiler_params=pltpu.CompilerParams(vmem_limit_bytes=60 * 2**20),
        cost_estimate=pl.CostEstimate(
            flops=2 * blocks * tok * width * wide,
            bytes_accessed=10 * 2**20,
            transcendentals=0,
        ),
        name="weigh",
    )(results, x_all, att_back, cot, w_out)


def collect_body(core_ref, spread_ref, mine_ref, theirs_ref):
    width = spread_ref.shape[2] - 3 * HD
    out_rows = spread_ref[0, :, :width].astype(F32)
    for source in range(1, spread_ref.shape[0]):
        out_rows += spread_ref[source, :, :width].astype(F32)
    parts = [
        jnp.concatenate(
            [
                spread_ref[slot_of(h), :, width + m * HD : width + (m + 1) * HD]
                for h in range(H)
            ],
            axis=1,
        )
        for m in range(3)
    ]
    low = jnp.concatenate(parts[:2], axis=1)
    high = jnp.concatenate([parts[2], out_rows.astype(BF16)], axis=1)

    @pl.when(core_ref[0] == 0)
    def _():
        mine_ref[...] = low
        theirs_ref[...] = high

    @pl.when(core_ref[0] != 0)
    def _():
        mine_ref[...] = high
        theirs_ref[...] = low


def collect(core, spread):
    peers, rows, wide = spread.shape
    half = 2 * (wide - 3 * HD)
    whole = pl.BlockSpec(memory_space=pltpu.VMEM)
    return pl.pallas_call(
        collect_body,
        in_specs=[pl.BlockSpec(memory_space=pltpu.SMEM), whole],
        out_specs=[whole, whole],
        out_shape=[jax.ShapeDtypeStruct((rows, half), BF16)] * 2,
        compiler_params=pltpu.CompilerParams(vmem_limit_bytes=16 * 2**20),
        cost_estimate=pl.CostEstimate(flops=10**6, bytes_accessed=2 * 10**6, transcendentals=0),
        name="collect",
    )(core, spread)


def close_body(back_ref, w_ref, out_ref):
    grad = jnp.concatenate(
        [
            back_ref[slot_of(h), m * HD : (m + 1) * HD, :]
            for m in range(3)
            for h in range(H)
        ],
        axis=0,
    )
    out_ref[...] = lax.dot_general(
        grad.T, w_ref[...], (((1,), (1,)), ((), ())), preferred_element_type=F32
    ).astype(BF16)


def close(back, w_qkv):
    tok = back.shape[2]
    width = w_qkv.shape[0]
    whole = pl.BlockSpec(memory_space=pltpu.VMEM)
    return pl.pallas_call(
        close_body,
        in_specs=[whole, whole],
        out_specs=whole,
        out_shape=jax.ShapeDtypeStruct((tok, width), BF16),
        compiler_params=pltpu.CompilerParams(vmem_limit_bytes=32 * 2**20),
        cost_estimate=pl.CostEstimate(
            flops=2 * tok * width * 3 * width, bytes_accessed=6 * 2**20, transcendentals=0
        ),
        name="close",
    )(back, w_qkv)


def swap_cores(value):
    return lax.ppermute(value, "slide", [(i, i ^ 1) for i in range(lax.axis_size("slide"))])


def sum_slides(core, mine, theirs):
    n = lax.axis_size("slide")
    chip = (mine.astype(F32) + swap_cores(theirs).astype(F32)).astype(BF16)
    others = [
        lax.ppermute(chip, "slide", [(i, (i + 2 * k) % n) for i in range(n)]).astype(F32)
        for k in (1, 2, 3)
    ]
    total = (chip.astype(F32) + others[1]) + (others[0] + others[2])
    rest = swap_cores(total)
    return jnp.where(core == 0, total, rest), jnp.where(core == 0, rest, total)


def shards(inputs, cotangent, key_tiles, tile_valid, w_qkv, w_out):
    width = inputs.shape[2]
    x = inputs[0]
    cot = cotangent[0]
    peers = lax.axis_size("seq")
    myself = lax.axis_index("seq")
    core = lax.rem(lax.axis_index("slide"), 2)
    x_all = lax.all_gather(x, "seq", axis=0)
    sent = project(x, cot, w_qkv, w_out)
    arrived = lax.all_to_all(sent, "seq", split_axis=0, concat_axis=0, tiled=True)
    group_tiles = lax.dynamic_index_in_dim(key_tiles[0], myself // 4, 0, keepdims=False)
    att_sent, low, stats = forward(group_tiles, tile_valid[0], arrived)
    att_back = lax.all_to_all(att_sent, "seq", split_axis=0, concat_axis=0, tiled=True)
    results = backward(group_tiles, arrived, low, stats)
    chunks, outputs = weigh(results, x_all, att_back, cot, w_out)
    chunks = chunks.reshape(peers, width // peers, -1)
    spread = lax.all_to_all(chunks, "seq", split_axis=0, concat_axis=0, tiled=True)
    results, spread = lax.optimization_barrier((results, spread))
    back = lax.all_to_all(results, "seq", split_axis=0, concat_axis=0, tiled=True)
    mine, theirs = collect(core[None], spread)
    low_half, high_half = sum_slides(core, mine, theirs)
    grad_inputs = close(back, w_qkv)
    return (
        outputs[None],
        grad_inputs[None],
        jnp.concatenate([low_half, high_half[:, :width]], axis=1),
        high_half[:, width:],
    )


def solution(mesh):
    placed = (
        P("slide", "seq", None),
        P("slide", "seq", None),
        P("slide", None, None, None),
        P("slide", None),
        P(),
        P(),
    )
    return jax.shard_map(
        shards,
        mesh=mesh,
        in_specs=placed,
        out_specs=(
            P("slide", "seq", None),
            P("slide", "seq", None),
            P("seq", None),
            P("seq", None),
        ),
        check_vma=False,
    )
```

time: 211 us -> 191 us (0.905); the launches traced: 210 us -> 187 us
  blocking collectives: 32.6 us -> 0 us
  local copies, waits for them, and re-layouts: 23.2 us -> 7.98 us
  starting transfers between devices: 22.5 us -> 35.5 us
  waiting for transfers between devices: 61.5 us -> 70.6 us
  Pallas kernels: 46 us -> 54.5 us
  matrix products: 4.8 us -> 0 us
    all_to_all x1 -> x0, blocking collectives: 32.6 us -> none  [shards(): lax.all_to_all(results, 'seq', split_axis=0, concat_axis=0, tiled=True)]
    all_to_all x0 -> x2, waiting for transfers between devices: none -> 12.8 us  [the longest x1 12.8 us: shards(): lax.all_to_all(results, 'seq', split_axis=0, concat_axis=0, tiled=True)]
    all_to_all x0 -> x2, starting transfers between devices: none -> 10.3 us  [the longest x1 5.89 us: shards(): lax.all_to_all(att_sent, 'seq', split_axis=0, concat_axis=0, tiled=True)]
    pallas_call x2 -> x5, Pallas kernels: 40 us -> 48.5 us  [the longest x1 17.4 us: backward(): pl.pallas_call(backward_body, grid=(blocks // NB,), in_specs=[pl.BlockSpe...]
    unnamed x30 -> x16, local copies, waits for them, and re-layouts: 12.9 us -> 6.62 us
    ppermute x3, waiting for transfers between devices: 6.65 us -> 0.76 us  [sum_slides(): lax.ppermute(chip, 'slide', [(i, (i + 2 * k) % n) for i in range(n)])]
    dot_general x3 -> x0, matrix products: 4.8 us -> none  [the longest x1 1.91 us: shards(): jnp.einsum('et,de->td', grad_proj_t, w_qkv, preferred_element_type=F32)]
    concatenate x2 -> x0, local copies, waits for them, and re-layouts: 3.91 us -> none  [the longest x1 2.24 us: shards(): total = sum_slides(jnp.concatenate([in_rows, out_rows], axis=1))]
  transfers between devices with their start and end apart: 8 -> 10, of which waited for: 5 -> 7; matrix products, arithmetic and copies ran while one was open for 3% -> 3% of each run, Pallas kernels for 19% -> 19%
where the time goes in v3:
time: 191 us; the launch traced here: 187 us
  waiting for transfers between devices  70.6 us (37%)
  Pallas kernels  54.5 us (29%)
  starting transfers between devices  35.5 us (19%)
  between operations  14.2 us (7%)
  local copies, waits for them, and re-layouts  7.98 us (4%)
  other arithmetic  4.77 us (2%)
    all_to_all x1, waiting for transfers between devices, shards(): lax.all_to_all(sent, 'seq', split_axis=0, concat_axis=0, tiled=True)  32.1 us
    all_to_all x1, waiting for transfers between devices, shards(): lax.all_to_all(chunks, 'seq', split_axis=0, concat_axis=0, tiled=True)  20.5 us
    pallas_call x1, Pallas kernels, backward(): pl.pallas_call(backward_body, grid=(blocks // NB,), in_specs=[pl.BlockSpe...  17.4 us
    pallas_call x1, Pallas kernels, weigh(): pl.pallas_call(weigh_body, grid=(blocks,), in_specs=[pl.BlockSpec((1, wid...  14.4 us
    pallas_call x1, Pallas kernels, forward(): pl.pallas_call(forward_body, grid=(blocks // NB,), in_specs=[pl.BlockSpec...  13.1 us
    all_to_all x1, waiting for transfers between devices, shards(): lax.all_to_all(results, 'seq', split_axis=0, concat_axis=0, tiled=True)  12.8 us
    all_to_all x1, starting transfers between devices, shards(): lax.all_to_all(sent, 'seq', split_axis=0, concat_axis=0, tiled=True)  8.6 us
    unnamed x16, local copies, waits for them, and re-layouts  6.62 us
  transfers between devices with their start and end apart: 10, of which 7 were waited for; matrix products, arithmetic and copies ran while one was open for 3% of the time, Pallas kernels for 19%

profile of v3, /device:TPU:1, one launch (start us, length us, event | category | flops | bytes accessed | tf_op | source)
XLA Modules:
  0.0 187.5 jit_solution(11602404827449175953)
XLA Ops:
  7.2 0.0 copy-start
  7.2 0.0 all-gather.2.cloned.1.call-start
  7.2 0.7 all-gather.2.cloned.1.call-update
  7.9 0.0 copy-start.1
  7.9 2.0 %copy-done.1 = bf16[768,2304]{1,0:T(8,128)(2,1)S(1)} copy-done((bf16[768,2304]{1,0:T(8,128)(2,1)S(1)}, bf16[768,2304]{1,0:T(8,128)(2,1)}, u32[]{:S(2)}) %copy-start.1) | copy-done | bytes 3538968
  9.9 0.0 copy-start.3
  9.9 1.3 copy-done.3
  11.2 0.0 copy-start.4
  11.2 1.0 copy-done.4
  12.2 0.0 copy-start.5
  12.2 1.0 copy-done.5
  13.2 6.0 %project.1 = bf16[16,256,256]{2,1,0:T(8,128)(2,1)} custom-call(bf16[256,768]{1,0:T(8,128)(2,1)S(1)} %bitcast.11, bf16[256,768]{1,0:T(8,128)(2,1)S(1)} %bitcast.10, bf16[768,2304]{1,0:T(8,128)(2,1)S(1)} %copy-done.1, bf16[768,2304]{1,0:T(8,128)(2,1)S(1)} %copy-done.1, bf16[768,2304]{1,0:T(8,128)(2,1)S(1)} %copy-done.1, bf16[768,768]{1,0:T(8,128)(2,1)S(1)} %copy-done.3), custom_call_target="tpu_custom_call" | custom-call | flops 1207959552 | bytes 8388608 | tf_op jit(solution)/shard_map/project/pallas_call | solution.py:56
  19.2 8.6 %all-to-all-start = ((bf16[16,256,256]{2,1,0:T(8,128)(2,1)}), bf16[16,256,256]{2,1,0:T(8,128)(2,1)S(1)}, u32[]{:S(2)}, u32[]{:S(2)}) async-start(bf16[16,256,256]{2,1,0:T(8,128)(2,1)} %project.1), calls=%async_computation | async-start | bytes 4194304 | tf_op jit(solution)/shard_map/all_to_all | solution.py:403
  27.8 0.0 copy-done
  27.9 0.7 copy.13.tiles_ref
  28.5 32.1 %all-to-all-done.in_ref = bf16[16,256,256]{2,1,0:T(8,128)(2,1)S(1)} async-done(((bf16[16,256,256]{2,1,0:T(8,128)(2,1)}), bf16[16,256,256]{2,1,0:T(8,128)(2,1)S(1)}, u32[]{:S(2)}, u32[]{:S(2)}) %all-to-all-start) | async-done | bytes 2097184 | tf_op jit(solution)/shard_map/all_to_all | solution.py:403
  60.7 0.0 copy-start.7
  60.7 1.3 copy-done.7
  62.0 13.1 %forward.1 = (bf16[16,64,256]{2,1,0:T(8,128)(2,1)}, bf16[16,1280,256]{2,1,0:T(8,128)(2,1)}, f32[16,8,256]{2,1,0:T(8,128)}) custom-call(s32[16,8]{1,0:T(8,128)} %copy.13.tiles_ref, s32[32]{0:T(128)} %bitcast.15, bf16[16,256,256]{2,1,0:T(8,128)(2,1)} %copy-done.7), custom_call_target="tpu_custom_call" | custom-call | flops 5368709120 | bytes 14680064 | tf_op jit(solution)/shard_map/forward/pallas_call | solution.py:130
  75.1 5.9 %all-to-all-start.1 = ((bf16[16,64,256]{2,1,0:T(8,128)(2,1)}), bf16[16,64,256]{2,1,0:T(8,128)(2,1)S(1)}, u32[]{:S(2)}, u32[]{:S(2)}) async-start(bf16[16,64,256]{2,1,0:T(8,128)(2,1)} %get-tuple-element.15), calls=%async_computation.1 | async-start | bytes 1048576 | tf_op jit(solution)/shard_map/all_to_all | solution.py:406
  81.0 17.4 %backward.1.res_ref = bf16[16,192,256]{2,1,0:T(8,128)(2,1)} custom-call(s32[16,8]{1,0:T(8,128)} %copy.13.tiles_ref, bf16[16,256,256]{2,1,0:T(8,128)(2,1)} %copy-done.7, bf16[16,1280,256]{2,1,0:T(8,128)(2,1)} %get-tuple-element.13.exp_ref, f32[16,8,256]{2,1,0:T(8,128)} %get-tuple-element.14.stat_ref), custom_call_target="tpu_custom_call" | custom-call | flops 10737418240 | bytes 16777216 | tf_op jit(solution)/shard_map/backward/pallas_call | solution.py:225
  98.4 0.0 all-to-all-done.1.back_ref
  98.4 0.0 copy-start.6
  98.4 1.2 all-gather.2.cloned.1.call-done.x_ref
  99.6 0.0 copy-done.6
  99.6 14.4 %weigh.1 = (bf16[768,960]{1,0:T(8,128)(2,1)}, bf16[256,768]{1,0:T(8,128)(2,1)}) custom-call(bf16[16,192,256]{2,1,0:T(8,128)(2,1)} %backward.1.res_ref, bf16[16,256,768]{2,1,0:T(8,128)(2,1)} %all-gather.2.cloned.1.call-done.x_ref, bf16[16,64,256]{2,1,0:T(8,128)(2,1)} %copy-done.6, bf16[256,768]{1,0:T(8,128)(2,1)} %bitcast.9, bf16[768,768]{1,0:T(8,128)(2,1)} %w_ref.2), custom_call_target="tpu_custom_call" | custom-call | flops 1207959552 | bytes 10485760 | tf_op jit(solution)/shard_map/weigh/pallas_call | solution.py:277
  114.0 6.2 %all-to-all-start.2 = ((bf16[16,48,960]{2,1,0:T(8,128)(2,1)}), bf16[16,48,960]{2,1,0:T(8,128)(2,1)S(1)}, u32[]{:S(2)}, u32[]{:S(2)}) async-start(bf16[16,48,960]{2,1,0:T(8,128)(2,1)} %bitcast.12), calls=%async_computation.2 | async-start | bytes 3145728 | tf_op jit(solution)/shard_map/all_to_all | solution.py:410
  120.3 20.5 %all-to-all-done.2.spread_ref = bf16[16,48,960]{2,1,0:T(8,128)(2,1)S(1)} async-done(((bf16[16,48,960]{2,1,0:T(8,128)(2,1)}), bf16[16,48,960]{2,1,0:T(8,128)(2,1)S(1)}, u32[]{:S(2)}, u32[]{:S(2)}) %all-to-all-start.2) | async-done | bytes 1474592 | tf_op jit(solution)/shard_map/all_to_all | solution.py:410
  140.7 0.2 collect.1
  141.0 4.3 %collective-permute-start = (bf16[48,1536]{1,0:T(8,128)(2,1)S(1)}, bf16[48,1536]{1,0:T(8,128)(2,1)S(1)}, u32[]{:S(2)}, u32[]{:S(2)}) collective-permute-start(bf16[48,1536]{1,0:T(8,128)(2,1)S(1)} %get-tuple-element.21), channel_id=1, source_target_pairs={{0,1},{1,0},{2,3},{3,2},{4,5},{5,4},{6,7},{7,6},{8,9},{9,8},{10,11... | collective-permute-start | bytes 442376 | tf_op jit(solution)/shard_map/ppermute | solution.py:379
  145.3 1.0 collective-permute-done
  146.3 0.7 add_convert_fusion
  147.0 2.5 %collective-permute-start.1 = (bf16[48,1536]{1,0:T(8,128)(2,1)}, bf16[48,1536]{1,0:T(8,128)(2,1)}, u32[]{:S(2)}, u32[]{:S(2)}) collective-permute-start(bf16[48,1536]{1,0:T(8,128)(2,1)} %add_convert_fusion), channel_id=1, source_target_pairs={{0,4},{1,5},{2,6},{3,7},{4,0},{5,1},{6,2},{7,3},{8,12},{9,13},{10,... | collective-permute-start | bytes 442376 | tf_op jit(solution)/shard_map/ppermute | solution.py:386
  149.5 0.1 collective-permute-start.2
  149.7 2.5 %collective-permute-start.3 = (bf16[48,1536]{1,0:T(8,128)(2,1)}, bf16[48,1536]{1,0:T(8,128)(2,1)}, u32[]{:S(2)}, u32[]{:S(2)}) collective-permute-start(bf16[48,1536]{1,0:T(8,128)(2,1)} %add_convert_fusion), channel_id=1, source_target_pairs={{0,6},{1,7},{2,0},{3,1},{4,2},{5,3},{6,4},{7,5},{8,14},{9,15},{10,... | collective-permute-start | bytes 442376 | tf_op jit(solution)/shard_map/ppermute | solution.py:386
  152.2 4.4 %all-to-all-start.3 = ((bf16[16,192,256]{2,1,0:T(8,128)(2,1)}), bf16[16,192,256]{2,1,0:T(8,128)(2,1)}, u32[]{:S(2)}, u32[]{:S(2)}) async-start(bf16[16,192,256]{2,1,0:T(8,128)(2,1)} %backward.1.res_ref), calls=%async_computation.3 | async-start | bytes 3145728 | tf_op jit(solution)/shard_map/all_to_all | solution.py:412
  156.6 0.0 copy-start.2
  156.6 0.0 collective-permute-done.1
  156.6 0.8 collective-permute-done.2
  157.4 0.0 collective-permute-done.3
  157.4 2.2 %add_add_fusion = f32[48,1536]{1,0:T(8,128)} fusion(bf16[48,1536]{1,0:T(8,128)(2,1)} %collective-permute-done.3, bf16[48,1536]{1,0:T(8,128)(2,1)} %collective-permute-done.2, bf16[48,1536]{1,0:T(8,128)(2,1)} %collective-permute-done.1, bf16[48,1536]{1,0:T(8,128)(2,1)} %add_convert_fusion), kind=kLoop, calls=%fused_computation.1 | loop fusion | flops 516096 | bytes 884736 | tf_op jit(solution)/shard_map/add | solution.py:389
  159.6 0.8 collective-permute-start.4
  160.4 1.6 collective-permute-done.4
  162.0 1.1 broadcast_select_fusion.1
  163.1 0.7 fusion
  163.7 0.8 pad_maximum_fusion
  164.5 12.8 %all-to-all-done.3.back_ref = bf16[16,192,256]{2,1,0:T(8,128)(2,1)} async-done(((bf16[16,192,256]{2,1,0:T(8,128)(2,1)}), bf16[16,192,256]{2,1,0:T(8,128)(2,1)}, u32[]{:S(2)}, u32[]{:S(2)}) %all-to-all-start.3) | async-done | bytes 1572896 | tf_op jit(solution)/shard_map/all_to_all | solution.py:412
  177.3 0.0 copy-done.2
  177.3 3.3 %close.1 = bf16[256,768]{1,0:T(8,128)(2,1)} custom-call(bf16[16,192,256]{2,1,0:T(8,128)(2,1)} %all-to-all-done.3.back_ref, bf16[768,2304]{1,0:T(8,128)(2,1)S(1)} %copy-done.2), custom_call_target="tpu_custom_call" | custom-call | flops 905969664 | bytes 6291456 | tf_op jit(solution)/shard_map/close/pallas_call | solution.py:365
  (1 shorter events, 0.0 us)
Async XLA Ops:
  7.2 20.7 %copy-start = (s32[1,4,16,8]{2,3,1,0:T(8,128)S(1)}, s32[1,4,16,8]{2,3,1,0:T(8,128)}, u32[]{:S(2)}) copy-start(s32[1,4,16,8]{2,3,1,0:T(8,128)} %param.8) | copy-start | bytes 6148
  7.2 92.4 %all-gather.2.cloned.1.call-start = ((), (), s32[]{:S(2)}) async-start(), calls=%async_computation.4 | async-start | bytes 6684672 | tf_op jit(solution)/shard_map/all_gather | solution.py:401
  7.9 2.0 %copy-start.1 = (bf16[768,2304]{1,0:T(8,128)(2,1)S(1)}, bf16[768,2304]{1,0:T(8,128)(2,1)}, u32[]{:S(2)}) copy-start(bf16[768,2304]{1,0:T(8,128)(2,1)} %w_ref.3) | copy-start | bytes 10616836
  9.9 1.3 copy-start.3
  11.2 1.0 copy-start.4
  12.2 1.0 copy-start.5
  19.2 41.5 %all-to-all-start = ((bf16[16,256,256]{2,1,0:T(8,128)(2,1)}), bf16[16,256,256]{2,1,0:T(8,128)(2,1)S(1)}, u32[]{:S(2)}, u32[]{:S(2)}) async-start(bf16[16,256,256]{2,1,0:T(8,128)(2,1)} %project.1), calls=%async_computation | async-start | bytes 4194304 | tf_op jit(solution)/shard_map/all_to_all | solution.py:403
  60.7 1.3 copy-start.7
  75.1 23.3 %all-to-all-start.1 = ((bf16[16,64,256]{2,1,0:T(8,128)(2,1)}), bf16[16,64,256]{2,1,0:T(8,128)(2,1)S(1)}, u32[]{:S(2)}, u32[]{:S(2)}) async-start(bf16[16,64,256]{2,1,0:T(8,128)(2,1)} %get-tuple-element.15), calls=%async_computation.1 | async-start | bytes 1048576 | tf_op jit(solution)/shard_map/all_to_all | solution.py:406
  98.4 1.2 copy-start.6
  114.0 26.7 %all-to-all-start.2 = ((bf16[16,48,960]{2,1,0:T(8,128)(2,1)}), bf16[16,48,960]{2,1,0:T(8,128)(2,1)S(1)}, u32[]{:S(2)}, u32[]{:S(2)}) async-start(bf16[16,48,960]{2,1,0:T(8,128)(2,1)} %bitcast.12), calls=%async_computation.2 | async-start | bytes 3145728 | tf_op jit(solution)/shard_map/all_to_all | solution.py:410
  141.0 5.3 %collective-permute-start = (bf16[48,1536]{1,0:T(8,128)(2,1)S(1)}, bf16[48,1536]{1,0:T(8,128)(2,1)S(1)}, u32[]{:S(2)}, u32[]{:S(2)}) collective-permute-start(bf16[48,1536]{1,0:T(8,128)(2,1)S(1)} %get-tuple-element.21), channel_id=1, source_target_pairs={{0,1},{1,0},{2,3},{3,2},{4,5},{5,4},{6,7},{7,6},{8,9},{9,8},{10,11... | collective-permute-start | bytes 442376 | tf_op jit(solution)/shard_map/ppermute | solution.py:379
  147.0 9.6 %collective-permute-start.1 = (bf16[48,1536]{1,0:T(8,128)(2,1)}, bf16[48,1536]{1,0:T(8,128)(2,1)}, u32[]{:S(2)}, u32[]{:S(2)}) collective-permute-start(bf16[48,1536]{1,0:T(8,128)(2,1)} %add_convert_fusion), channel_id=1, source_target_pairs={{0,4},{1,5},{2,6},{3,7},{4,0},{5,1},{6,2},{7,3},{8,12},{9,13},{10,... | collective-permute-start | bytes 442376 | tf_op jit(solution)/shard_map/ppermute | solution.py:386
  149.5 7.9 %collective-permute-start.2 = (bf16[48,1536]{1,0:T(8,128)(2,1)}, bf16[48,1536]{1,0:T(8,128)(2,1)}, u32[]{:S(2)}, u32[]{:S(2)}) collective-permute-start(bf16[48,1536]{1,0:T(8,128)(2,1)} %add_convert_fusion), channel_id=1, source_target_pairs={{0,2},{1,3},{2,4},{3,5},{4,6},{5,7},{6,0},{7,1},{8,10},{9,11},{10,... | collective-permute-start | bytes 442376 | tf_op jit(solution)/shard_map/ppermute | solution.py:386
  149.7 7.7 %collective-permute-start.3 = (bf16[48,1536]{1,0:T(8,128)(2,1)}, bf16[48,1536]{1,0:T(8,128)(2,1)}, u32[]{:S(2)}, u32[]{:S(2)}) collective-permute-start(bf16[48,1536]{1,0:T(8,128)(2,1)} %add_convert_fusion), channel_id=1, source_target_pairs={{0,6},{1,7},{2,0},{3,1},{4,2},{5,3},{6,4},{7,5},{8,14},{9,15},{10,... | collective-permute-start | bytes 442376 | tf_op jit(solution)/shard_map/ppermute | solution.py:386
  152.2 25.1 %all-to-all-start.3 = ((bf16[16,192,256]{2,1,0:T(8,128)(2,1)}), bf16[16,192,256]{2,1,0:T(8,128)(2,1)}, u32[]{:S(2)}, u32[]{:S(2)}) async-start(bf16[16,192,256]{2,1,0:T(8,128)(2,1)} %backward.1.res_ref), calls=%async_computation.3 | async-start | bytes 3145728 | tf_op jit(solution)/shard_map/all_to_all | solution.py:412
  156.6 20.7 %copy-start.2 = (bf16[768,2304]{1,0:T(8,128)(2,1)S(1)}, bf16[768,2304]{1,0:T(8,128)(2,1)}, u32[]{:S(2)}) copy-start(bf16[768,2304]{1,0:T(8,128)(2,1)} %w_ref.3) | copy-start | bytes 10616836
  159.6 2.4 %collective-permute-start.4 = (f32[48,1536]{1,0:T(8,128)}, f32[48,1536]{1,0:T(8,128)}, u32[]{:S(2)}, u32[]{:S(2)}) collective-permute-start(f32[48,1536]{1,0:T(8,128)} %add_add_fusion), channel_id=1, source_target_pairs={{0,1},{1,0},{2,3},{3,2},{4,5},{5,4},{6,7},{7,6},{8,9},{9,8},{10,11... | collective-permute-start | bytes 884744 | tf_op jit(solution)/shard_map/ppermute | solution.py:379
Sparse Core Ops, SparseCore 0:
  10.2 89.3 all-gather.1

commit v4 on v3

--- a/solution.py
+++ b/solution.py
@@ -25,10 +25,10 @@
 def project_body(x_ref, cot_ref, wq_ref, wk_ref, wv_ref, wo_ref, out_ref):
     step = pl.program_id(0)
     x = x_ref[...]
-    contract = (((0,), (1,)), ((), ()))
-    qt = lax.dot_general(wq_ref[...], x, contract, preferred_element_type=F32).astype(BF16)
-    kt = lax.dot_general(wk_ref[...], x, contract, preferred_element_type=F32).astype(BF16)
-    vt = lax.dot_general(wv_ref[...], x, contract, preferred_element_type=F32).astype(BF16)
+    qt, kt, vt = [
+        jnp.dot(x, ref[...], preferred_element_type=F32).astype(BF16).T
+        for ref in (wq_ref, wk_ref, wv_ref)
+    ]
     gt = lax.dot_general(
         wo_ref[...], cot_ref[...], (((1,), (1,)), ((), ())), preferred_element_type=F32
     ).astype(BF16)
@@ -66,7 +66,7 @@
         ],
         out_specs=pl.BlockSpec((16, 4 * HD, tok), lambda i: (0, 0, 0)),
         out_shape=jax.ShapeDtypeStruct((16, 4 * HD, tok), BF16),
-        compiler_params=pltpu.CompilerParams(vmem_limit_bytes=32 * 2**20),
+        compiler_params=pltpu.CompilerParams(vmem_limit_bytes=60 * 2**20),
         cost_estimate=pl.CostEstimate(
             flops=2 * tok * width * 4 * width, bytes_accessed=8 * 2**20, transcendentals=0
         ),
@@ -248,17 +248,16 @@
     )(tiles, arrived, low, stats)
 
 
-def weigh_body(res_ref, x_ref, back_ref, cot_ref, w_ref, chunk_ref, out_ref, acc):
+def weigh_body(core_ref, res_ref, x_ref, back_ref, cot_ref, mine_ref, theirs_ref, acc, out_acc):
     step = pl.program_id(0)
     part = jnp.dot(res_ref[0], x_ref[0], preferred_element_type=F32)
+    for i in range(1, res_ref.shape[0]):
+        part += jnp.dot(res_ref[i], x_ref[i], preferred_element_type=F32)
 
     @pl.when(step == 0)
     def _():
         attended = jnp.concatenate([back_ref[slot_of(h)] for h in range(H)], axis=0)
-        chunk_ref[:, : cot_ref.shape[1]] = jnp.dot(
-            attended, cot_ref[...], preferred_element_type=F32
-        ).astype(BF16)
-        out_ref[...] = jnp.dot(attended.T, w_ref[...], preferred_element_type=F32).astype(BF16)
+        out_acc[...] = jnp.dot(attended, cot_ref[...], preferred_element_type=F32).astype(BF16)
         acc[...] = part
 
     @pl.when(step > 0)
@@ -267,29 +266,54 @@
 
     @pl.when(step == pl.num_programs(0) - 1)
     def _():
-        chunk_ref[:, cot_ref.shape[1] :] = acc[...].T.astype(BF16)
-
-
-def weigh(results, x_all, att_back, cot, w_out):
+        in_part = acc[...].T.astype(BF16)
+        out_part = out_acc[...]
+        rows, width = out_part.shape
+        out_cols = width // 8
+        in_cols = in_part.shape[1] // 8
+        fill = jnp.zeros((rows, 128 - out_cols - in_cols), BF16)
+        pieces = [
+            jnp.concatenate(
+                [
+                    out_part[:, k * out_cols : (k + 1) * out_cols],
+                    in_part[:, k * in_cols : (k + 1) * in_cols],
+                    fill,
+                ],
+                axis=1,
+            )
+            for k in range(8)
+        ]
+
+        @pl.when(core_ref[0] == 0)
+        def _():
+            for k in range(4):
+                mine_ref[k] = pieces[2 * k]
+                theirs_ref[k] = pieces[2 * k + 1]
+
+        @pl.when(core_ref[0] != 0)
+        def _():
+            for k in range(4):
+                mine_ref[k] = pieces[2 * k + 1]
+                theirs_ref[k] = pieces[2 * k]
+
+
+def weigh(core, results, x_all, att_back, cot):
     blocks, wide, tok = results.shape
     width = x_all.shape[2]
     whole = pl.BlockSpec(memory_space=pltpu.VMEM)
     return pl.pallas_call(
         weigh_body,
-        grid=(blocks,),
+        grid=(blocks // 4,),
         in_specs=[
-            pl.BlockSpec((1, wide, tok), lambda i: (i, 0, 0)),
-            pl.BlockSpec((1, tok, width), lambda i: (i, 0, 0)),
+            pl.BlockSpec(memory_space=pltpu.SMEM),
+            pl.BlockSpec((4, wide, tok), lambda i: (i, 0, 0)),
+            pl.BlockSpec((4, tok, width), lambda i: (i, 0, 0)),
             whole,
             whole,
-            whole,
         ],
         out_specs=[whole, whole],
-        out_shape=[
-            jax.ShapeDtypeStruct((width, width + wide), BF16),
-            jax.ShapeDtypeStruct((tok, width), BF16),
-        ],
-        scratch_shapes=[pltpu.VMEM((wide, width), F32)],
+        out_shape=[jax.ShapeDtypeStruct((4, width, 128), BF16)] * 2,
+        scratch_shapes=[pltpu.VMEM((wide, width), F32), pltpu.VMEM((width, width), BF16)],
         compiler_params=pltpu.CompilerParams(vmem_limit_bytes=60 * 2**20),
         cost_estimate=pl.CostEstimate(
             flops=2 * blocks * tok * width * wide,
@@ -297,54 +321,88 @@
             transcendentals=0,
         ),
         name="weigh",
-    )(results, x_all, att_back, cot, w_out)
-
-
-def collect_body(core_ref, spread_ref, mine_ref, theirs_ref):
-    width = spread_ref.shape[2] - 3 * HD
-    out_rows = spread_ref[0, :, :width].astype(F32)
+    )(core, results, x_all, att_back, cot)
+
+
+def merge_body(chip_ref, mine_ref, got_ref, *outs):
+    for k, out in enumerate(outs):
+        place = lax.rem(chip_ref[0] + k, 4)
+        out[...] = (mine_ref[place].astype(F32) + got_ref[place].astype(F32)).astype(BF16)
+
+
+def merge(chip, mine, got):
+    whole = pl.BlockSpec(memory_space=pltpu.VMEM)
+    return pl.pallas_call(
+        merge_body,
+        in_specs=[pl.BlockSpec(memory_space=pltpu.SMEM), whole, whole],
+        out_specs=[whole] * 4,
+        out_shape=[jax.ShapeDtypeStruct(mine.shape[1:], BF16)] * 4,
+        compiler_params=pltpu.CompilerParams(vmem_limit_bytes=16 * 2**20),
+        cost_estimate=pl.CostEstimate(flops=10**6, bytes_accessed=2 * 10**6, transcendentals=0),
+        name="merge",
+    )(chip, mine, got)
+
+
+def collect_body(spread_ref, out_ref):
+    in_cols = 3 * HD // 8
+    out_cols = 4 * in_cols
+    total = spread_ref[0].astype(F32)
     for source in range(1, spread_ref.shape[0]):
-        out_rows += spread_ref[source, :, :width].astype(F32)
-    parts = [
+        total += spread_ref[source].astype(F32)
+    ins = [spread_ref[slot_of(h), :, out_cols : out_cols + in_cols].astype(F32) for h in range(H)]
+    out_ref[...] = jnp.concatenate([total[:, :out_cols]] + ins, axis=1).astype(BF16)
+
+
+def collect(spread):
+    whole = pl.BlockSpec(memory_space=pltpu.VMEM)
+    rows = spread.shape[1]
+    return pl.pallas_call(
+        collect_body,
+        in_specs=[whole],
+        out_specs=whole,
+        out_shape=jax.ShapeDtypeStruct((rows, 6 * HD), BF16),
+        compiler_params=pltpu.CompilerParams(vmem_limit_bytes=16 * 2**20),
+        cost_estimate=pl.CostEstimate(flops=10**6, bytes_accessed=10**6, transcendentals=0),
+        name="collect",
+    )(spread)
+
+
+def settle_body(all_ref, in_ref, out_ref):
+    in_cols = 3 * HD // 8
+    out_cols = 4 * in_cols
+    parts = [all_ref[k].astype(F32) for k in range(8)]
+    out_ref[...] = jnp.concatenate([part[:, :out_cols] for part in parts], axis=1)
+    heads = [
         jnp.concatenate(
-            [
-                spread_ref[slot_of(h), :, width + m * HD : width + (m + 1) * HD]
-                for h in range(H)
-            ],
+            [part[:, out_cols + h * in_cols : out_cols + (h + 1) * in_cols] for part in parts],
             axis=1,
         )
-        for m in range(3)
+        for h in range(H)
     ]
-    low = jnp.concatenate(parts[:2], axis=1)
-    high = jnp.concatenate([parts[2], out_rows.astype(BF16)], axis=1)
-
-    @pl.when(core_ref[0] == 0)
-    def _():
-        mine_ref[...] = low
-        theirs_ref[...] = high
-
-    @pl.when(core_ref[0] != 0)
-    def _():
-        mine_ref[...] = high
-        theirs_ref[...] = low
-
-
-def collect(core, spread):
-    peers, rows, wide = spread.shape
-    half = 2 * (wide - 3 * HD)
-    whole = pl.BlockSpec(memory_space=pltpu.VMEM)
-    return pl.pallas_call(
-        collect_body,
-        in_specs=[pl.BlockSpec(memory_space=pltpu.SMEM), whole],
+    in_ref[...] = jnp.concatenate(
+        [head[:, m * HD : (m + 1) * HD] for m in range(3) for head in heads], axis=1
+    )
+
+
+def settle(gathered):
+    whole = pl.BlockSpec(memory_space=pltpu.VMEM)
+    rows = gathered.shape[1]
+    width = H * HD
+    return pl.pallas_call(
+        settle_body,
+        in_specs=[whole],
         out_specs=[whole, whole],
-        out_shape=[jax.ShapeDtypeStruct((rows, half), BF16)] * 2,
+        out_shape=[
+            jax.ShapeDtypeStruct((rows, 3 * width), F32),
+            jax.ShapeDtypeStruct((rows, width), F32),
+        ],
         compiler_params=pltpu.CompilerParams(vmem_limit_bytes=16 * 2**20),
-        cost_estimate=pl.CostEstimate(flops=10**6, bytes_accessed=2 * 10**6, transcendentals=0),
-        name="collect",
-    )(core, spread)
-
-
-def close_body(back_ref, w_ref, out_ref):
+        cost_estimate=pl.CostEstimate(flops=10**6, bytes_accessed=10**6, transcendentals=0),
+        name="settle",
+    )(gathered)
+
+
+def close_body(back_ref, att_ref, w_ref, wo_ref, grad_ref, out_ref):
     grad = jnp.concatenate(
         [
             back_ref[slot_of(h), m * HD : (m + 1) * HD, :]
@@ -353,42 +411,28 @@
         ],
         axis=0,
     )
-    out_ref[...] = lax.dot_general(
+    grad_ref[...] = lax.dot_general(
         grad.T, w_ref[...], (((1,), (1,)), ((), ())), preferred_element_type=F32
     ).astype(BF16)
-
-
-def close(back, w_qkv):
+    attended = jnp.concatenate([att_ref[slot_of(h)] for h in range(H)], axis=0)
+    out_ref[...] = jnp.dot(attended.T, wo_ref[...], preferred_element_type=F32).astype(BF16)
+
+
+def close(back, att_back, w_qkv, w_out):
     tok = back.shape[2]
     width = w_qkv.shape[0]
     whole = pl.BlockSpec(memory_space=pltpu.VMEM)
     return pl.pallas_call(
         close_body,
-        in_specs=[whole, whole],
-        out_specs=whole,
-        out_shape=jax.ShapeDtypeStruct((tok, width), BF16),
+        in_specs=[whole] * 4,
+        out_specs=[whole] * 2,
+        out_shape=[jax.ShapeDtypeStruct((tok, width), BF16)] * 2,
         compiler_params=pltpu.CompilerParams(vmem_limit_bytes=32 * 2**20),
         cost_estimate=pl.CostEstimate(
-            flops=2 * tok * width * 3 * width, bytes_accessed=6 * 2**20, transcendentals=0
+            flops=2 * tok * width * 4 * width, bytes_accessed=8 * 2**20, transcendentals=0
         ),
         name="close",
-    )(back, w_qkv)
-
-
-def swap_cores(value):
-    return lax.ppermute(value, "slide", [(i, i ^ 1) for i in range(lax.axis_size("slide"))])
-
-
-def sum_slides(core, mine, theirs):
-    n = lax.axis_size("slide")
-    chip = (mine.astype(F32) + swap_cores(theirs).astype(F32)).astype(BF16)
-    others = [
-        lax.ppermute(chip, "slide", [(i, (i + 2 * k) % n) for i in range(n)]).astype(F32)
-        for k in (1, 2, 3)
-    ]
-    total = (chip.astype(F32) + others[1]) + (others[0] + others[2])
-    rest = swap_cores(total)
-    return jnp.where(core == 0, total, rest), jnp.where(core == 0, rest, total)
+    )(back, att_back, w_qkv, w_out)
 
 
 def shards(inputs, cotangent, key_tiles, tile_valid, w_qkv, w_out):
@@ -396,8 +440,9 @@
     x = inputs[0]
     cot = cotangent[0]
     peers = lax.axis_size("seq")
+    slides = lax.axis_size("slide")
     myself = lax.axis_index("seq")
-    core = lax.rem(lax.axis_index("slide"), 2)
+    slide = lax.axis_index("slide")
     x_all = lax.all_gather(x, "seq", axis=0)
     sent = project(x, cot, w_qkv, w_out)
     arrived = lax.all_to_all(sent, "seq", split_axis=0, concat_axis=0, tiled=True)
@@ -405,20 +450,21 @@
     att_sent, low, stats = forward(group_tiles, tile_valid[0], arrived)
     att_back = lax.all_to_all(att_sent, "seq", split_axis=0, concat_axis=0, tiled=True)
     results = backward(group_tiles, arrived, low, stats)
-    chunks, outputs = weigh(results, x_all, att_back, cot, w_out)
-    chunks = chunks.reshape(peers, width // peers, -1)
-    spread = lax.all_to_all(chunks, "seq", split_axis=0, concat_axis=0, tiled=True)
-    results, spread = lax.optimization_barrier((results, spread))
     back = lax.all_to_all(results, "seq", split_axis=0, concat_axis=0, tiled=True)
-    mine, theirs = collect(core[None], spread)
-    low_half, high_half = sum_slides(core, mine, theirs)
-    grad_inputs = close(back, w_qkv)
-    return (
-        outputs[None],
-        grad_inputs[None],
-        jnp.concatenate([low_half, high_half[:, :width]], axis=1),
-        high_half[:, width:],
-    )
+    mine, theirs = weigh(lax.rem(slide, 2)[None], results, x_all, att_back, cot)
+    got = lax.ppermute(theirs, "slide", [(i, i ^ 1) for i in range(slides)])
+    keep, *sends = merge((slide // 2)[None], mine, got)
+    takes = [
+        lax.ppermute(send, "slide", [(i, (i + 2 * k) % slides) for i in range(slides)]).astype(F32)
+        for k, send in zip((1, 2, 3), sends)
+    ]
+    piece = ((keep.astype(F32) + takes[1]) + (takes[0] + takes[2])).astype(BF16)
+    piece, back = lax.optimization_barrier((piece, back))
+    piece = piece.reshape(peers, width // peers, piece.shape[1])
+    spread = lax.all_to_all(piece, "seq", split_axis=0, concat_axis=0, tiled=True)
+    w_qkv_grad, w_out_grad = settle(lax.all_gather(collect(spread), "slide", axis=0))
+    grad_inputs, outputs = close(back, att_back, w_qkv, w_out)
+    return outputs[None], grad_inputs[None], w_qkv_grad, w_out_grad
 
 
 def solution(mesh):

time: 191 us -> 170 us (0.89); the launches traced: 187 us -> 170 us
  waiting for transfers between devices: 70.6 us -> 45.8 us
  blocking collectives: 0 us -> 14.9 us
  other arithmetic: 4.77 us -> 0.78 us
  local copies, waits for them, and re-layouts: 7.98 us -> 5.46 us
    all_to_all x1, waiting for transfers between devices: 20.5 us -> 1.09 us  [shards(): lax.all_to_all(piece, 'seq', split_axis=0, concat_axis=0, tiled=True)]
    all_gather x0 -> x1, blocking collectives: none -> 14.9 us  [shards(): lax.all_gather(collect(spread), 'slide', axis=0)]
    all_to_all x1, waiting for transfers between devices: 12.8 us -> 0.01 us  [shards(): lax.all_to_all(results, 'seq', split_axis=0, concat_axis=0, tiled=True)]
    ppermute x5 -> x4, waiting for transfers between devices: 3.32 us -> 9.15 us  [the longest x3 6.9 us: shards(): lax.ppermute(send, 'slide', [(i, (i + 2 * k) % slides) for i in range(sli...]
    ppermute x5 -> x4, starting transfers between devices: 10.3 us -> 7.43 us  [the longest x3 5.66 us: shards(): lax.ppermute(send, 'slide', [(i, (i + 2 * k) % slides) for i in range(sli...]
    all_to_all x1, waiting for transfers between devices: 32.1 us -> 34.8 us  [shards(): lax.all_to_all(sent, 'seq', split_axis=0, concat_axis=0, tiled=True)]
    pallas_call x3 -> x5, Pallas kernels: 18 us -> 15.6 us  [the longest x1 8.21 us: weigh(): pl.pallas_call(weigh_body, grid=(blocks // 4,), in_specs=[pl.BlockSpec(me...]
    all_to_all x1, starting transfers between devices: 4.41 us -> 6.67 us  [shards(): lax.all_to_all(results, 'seq', split_axis=0, concat_axis=0, tiled=True)]
  transfers between devices with their start and end apart: 10 -> 9, of which waited for: 7 -> 5; matrix products, arithmetic and copies ran while one was open for 3% -> 1% of each run, Pallas kernels for 19% -> 30%
where the time goes in v4:
time: 170 us
  Pallas kernels  53.7 us (32%)
  waiting for transfers between devices  45.8 us (27%)
  starting transfers between devices  34.9 us (21%)
  blocking collectives  14.9 us (9%)
  between operations  14.2 us (8%)
  local copies, waits for them, and re-layouts  5.46 us (3%)
    all_to_all x1, waiting for transfers between devices, shards(): lax.all_to_all(sent, 'seq', split_axis=0, concat_axis=0, tiled=True)  34.8 us
    pallas_call x1, Pallas kernels, backward(): pl.pallas_call(backward_body, grid=(blocks // NB,), in_specs=[pl.BlockSpe...  17.4 us
    all_gather x1, blocking collectives, shards(): lax.all_gather(collect(spread), 'slide', axis=0)  14.9 us
    pallas_call x1, Pallas kernels, forward(): pl.pallas_call(forward_body, grid=(blocks // NB,), in_specs=[pl.BlockSpec...  13.1 us
    all_to_all x1, starting transfers between devices, shards(): lax.all_to_all(sent, 'seq', split_axis=0, concat_axis=0, tiled=True)  8.6 us
    pallas_call x1, Pallas kernels, weigh(): pl.pallas_call(weigh_body, grid=(blocks // 4,), in_specs=[pl.BlockSpec(me...  8.21 us
    pallas_call x1, Pallas kernels, project(): pl.pallas_call(project_body, grid=(pairs,), in_specs=[pl.BlockSpec((tok,...  7.7 us
    all_to_all x1, starting transfers between devices, shards(): lax.all_to_all(piece, 'seq', split_axis=0, concat_axis=0, tiled=True)  6.92 us
  transfers between devices with their start and end apart: 9, of which 5 were waited for; matrix products, arithmetic and copies ran while one was open for 1% of the time, Pallas kernels for 30%

profile of v4, /device:TPU:1, one launch (start us, length us, event | category | flops | bytes accessed | tf_op | source)
XLA Modules:
  0.0 169.7 jit_solution(3315198774808793788)
XLA Ops:
  7.2 0.0 copy-start
  7.2 0.0 all-gather.3.cloned.1.call-start
  7.2 0.7 all-gather.3.cloned.1.call-update
  7.9 7.7 %project.1 = bf16[16,256,256]{2,1,0:T(8,128)(2,1)} custom-call(bf16[256,768]{1,0:T(8,128)(2,1)} %bitcast.14, bf16[256,768]{1,0:T(8,128)(2,1)} %bitcast.12, bf16[768,2304]{1,0:T(8,128)(2,1)} %w_ref.1, bf16[768,2304]{1,0:T(8,128)(2,1)} %w_ref.1, bf16[768,2304]{1,0:T(8,128)(2,1)} %w_ref.1, bf16[768,768]{1,0:T(8,128)(2,1)} %wo_ref.3), custom_call_target="tpu_custom_call" | custom-call | flops 1207959552 | bytes 8388608 | tf_op jit(solution)/shard_map/project/pallas_call | solution.py:56
  15.6 8.6 %all-to-all-start = ((bf16[16,256,256]{2,1,0:T(8,128)(2,1)}), bf16[16,256,256]{2,1,0:T(8,128)(2,1)S(1)}, u32[]{:S(2)}, u32[]{:S(2)}) async-start(bf16[16,256,256]{2,1,0:T(8,128)(2,1)} %project.1), calls=%async_computation | async-start | bytes 4194304 | tf_op jit(solution)/shard_map/all_to_all | solution.py:448
  24.2 0.0 copy-done
  24.3 0.7 copy.13.tiles_ref
  24.9 34.8 %all-to-all-done.in_ref = bf16[16,256,256]{2,1,0:T(8,128)(2,1)S(1)} async-done(((bf16[16,256,256]{2,1,0:T(8,128)(2,1)}), bf16[16,256,256]{2,1,0:T(8,128)(2,1)S(1)}, u32[]{:S(2)}, u32[]{:S(2)}) %all-to-all-start) | async-done | bytes 2097184 | tf_op jit(solution)/shard_map/all_to_all | solution.py:448
  59.7 0.0 copy-start.6
  59.8 1.3 copy-done.6
  61.1 13.1 %forward.1 = (bf16[16,64,256]{2,1,0:T(8,128)(2,1)}, bf16[16,1280,256]{2,1,0:T(8,128)(2,1)}, f32[16,8,256]{2,1,0:T(8,128)}) custom-call(s32[16,8]{1,0:T(8,128)} %copy.13.tiles_ref, s32[32]{0:T(128)} %bitcast.18, bf16[16,256,256]{2,1,0:T(8,128)(2,1)} %copy-done.6), custom_call_target="tpu_custom_call" | custom-call | flops 5368709120 | bytes 14680064 | tf_op jit(solution)/shard_map/forward/pallas_call | solution.py:130
  74.2 5.2 %all-to-all-start.1 = ((bf16[16,64,256]{2,1,0:T(8,128)(2,1)}), bf16[16,64,256]{2,1,0:T(8,128)(2,1)S(1)}, u32[]{:S(2)}, u32[]{:S(2)}) async-start(bf16[16,64,256]{2,1,0:T(8,128)(2,1)} %get-tuple-element.21), calls=%async_computation.1 | async-start | bytes 1048576 | tf_op jit(solution)/shard_map/all_to_all | solution.py:451
  79.4 17.4 %backward.1.res_ref = bf16[16,192,256]{2,1,0:T(8,128)(2,1)} custom-call(s32[16,8]{1,0:T(8,128)} %copy.13.tiles_ref, bf16[16,256,256]{2,1,0:T(8,128)(2,1)} %copy-done.6, bf16[16,1280,256]{2,1,0:T(8,128)(2,1)} %get-tuple-element.19.exp_ref, f32[16,8,256]{2,1,0:T(8,128)} %get-tuple-element.20.stat_ref), custom_call_target="tpu_custom_call" | custom-call | flops 10737418240 | bytes 16777216 | tf_op jit(solution)/shard_map/backward/pallas_call | solution.py:225
  96.8 0.0 all-to-all-done.1.back_ref.att_ref
  96.8 0.0 copy-start.3
  96.8 6.7 %all-to-all-start.2 = ((bf16[16,192,256]{2,1,0:T(8,128)(2,1)}), bf16[16,192,256]{2,1,0:T(8,128)(2,1)}, u32[]{:S(2)}, u32[]{:S(2)}) async-start(bf16[16,192,256]{2,1,0:T(8,128)(2,1)} %backward.1.res_ref), calls=%async_computation.2 | async-start | bytes 3145728 | tf_op jit(solution)/shard_map/all_to_all | solution.py:453
  103.5 0.0 all-gather.3.cloned.1.call-done.x_ref
  103.5 0.0 copy-done.3
  103.5 0.0 copy-start.1
  103.5 8.2 %weigh.1 = (bf16[4,768,128]{2,1,0:T(8,128)(2,1)}, bf16[4,768,128]{2,1,0:T(8,128)(2,1)}) custom-call(s32[1]{0:T(128)} %bitcast.1.core_ref, bf16[16,192,256]{2,1,0:T(8,128)(2,1)} %backward.1.res_ref, bf16[16,256,768]{2,1,0:T(8,128)(2,1)} %all-gather.3.cloned.1.call-done.x_ref, bf16[16,64,256]{2,1,0:T(8,128)(2,1)} %copy-done.3, bf16[256,768]{1,0:T(8,128)(2,1)} %bitcast.13), custom_call_target="tpu_custom_call" | custom-call | flops 1207959552 | bytes 10485760 | tf_op jit(solution)/shard_map/weigh/pallas_call | solution.py:304
  111.7 1.8 %collective-permute-start = (bf16[4,768,128]{2,1,0:T(8,128)(2,1)}, bf16[4,768,128]{2,1,0:T(8,128)(2,1)}, u32[]{:S(2)}, u32[]{:S(2)}) collective-permute-start(bf16[4,768,128]{2,1,0:T(8,128)(2,1)} %get-tuple-element.23), channel_id=1, source_target_pairs={{0,1},{1,0},{2,3},{3,2},{4,5},{5,4},{6,7},{7,6},{8,9},{9,8},{10,11... | collective-permute-start | bytes 2359304 | tf_op jit(solution)/shard_map/ppermute | solution.py:455
  113.5 2.3 %collective-permute-done.got_ref = bf16[4,768,128]{2,1,0:T(8,128)(2,1)} collective-permute-done((bf16[4,768,128]{2,1,0:T(8,128)(2,1)}, bf16[4,768,128]{2,1,0:T(8,128)(2,1)}, u32[]{:S(2)}, u32[]{:S(2)}) %collective-permute-start) | collective-permute-done | bytes 786464 | tf_op jit(solution)/shard_map/ppermute | solution.py:455
  115.7 0.0 copy-start.5
  115.7 1.1 copy-done.5
  116.9 1.3 merge.1
  118.2 3.0 %collective-permute-start.1 = (bf16[768,128]{1,0:T(8,128)(2,1)S(1)}, bf16[768,128]{1,0:T(8,128)(2,1)S(1)}, u32[]{:S(2)}, u32[]{:S(2)}) collective-permute-start(bf16[768,128]{1,0:T(8,128)(2,1)S(1)} %get-tuple-element.25), channel_id=1, source_target_pairs={{0,4},{1,5},{2,6},{3,7},{4,0},{5,1},{6,2},{7,3},{8,12},{9,13},{10,... | collective-permute-start | bytes 589832 | tf_op jit(solution)/shard_map/ppermute | solution.py:458
  121.2 0.3 collective-permute-start.2
  121.5 2.4 %collective-permute-start.3 = (bf16[768,128]{1,0:T(8,128)(2,1)S(1)}, bf16[768,128]{1,0:T(8,128)(2,1)S(1)}, u32[]{:S(2)}, u32[]{:S(2)}) collective-permute-start(bf16[768,128]{1,0:T(8,128)(2,1)S(1)} %get-tuple-element.27), channel_id=1, source_target_pairs={{0,6},{1,7},{2,0},{3,1},{4,2},{5,3},{6,4},{7,5},{8,14},{9,15},{10,... | collective-permute-start | bytes 589832 | tf_op jit(solution)/shard_map/ppermute | solution.py:458
  123.9 2.1 %collective-permute-done.1 = bf16[768,128]{1,0:T(8,128)(2,1)S(1)} collective-permute-done((bf16[768,128]{1,0:T(8,128)(2,1)S(1)}, bf16[768,128]{1,0:T(8,128)(2,1)S(1)}, u32[]{:S(2)}, u32[]{:S(2)}) %collective-permute-start.1) | collective-permute-done | bytes 196640 | tf_op jit(solution)/shard_map/ppermute | solution.py:458
  126.0 4.8 %collective-permute-done.2 = bf16[768,128]{1,0:T(8,128)(2,1)S(1)} collective-permute-done((bf16[768,128]{1,0:T(8,128)(2,1)S(1)}, bf16[768,128]{1,0:T(8,128)(2,1)S(1)}, u32[]{:S(2)}, u32[]{:S(2)}) %collective-permute-start.2) | collective-permute-done | bytes 196640 | tf_op jit(solution)/shard_map/ppermute | solution.py:458
  130.8 0.0 collective-permute-done.3
  130.8 0.8 add_convert_fusion
  131.5 0.0 all-to-all-done.2.back_ref
  131.5 6.9 %all-to-all-start.3 = ((bf16[16,48,128]{2,1,0:T(8,128)(2,1)}), bf16[16,48,128]{2,1,0:T(8,128)(2,1)}, u32[]{:S(2)}, u32[]{:S(2)}) async-start(bf16[16,48,128]{2,1,0:T(8,128)(2,1)} %bitcast.15), calls=%async_computation.3 | async-start | bytes 393216 | tf_op jit(solution)/shard_map/all_to_all | solution.py:464
  138.5 0.0 copy-done.1
  138.5 0.0 copy-start.2
  138.5 1.3 copy-done.2
  139.8 0.0 copy-start.4
  139.8 1.0 copy-done.4
  140.8 3.7 %close.1 = (bf16[256,768]{1,0:T(8,128)(2,1)}, bf16[256,768]{1,0:T(8,128)(2,1)}) custom-call(bf16[16,192,256]{2,1,0:T(8,128)(2,1)} %all-to-all-done.2.back_ref, bf16[16,64,256]{2,1,0:T(8,128)(2,1)S(1)} %copy-done.4, bf16[768,2304]{1,0:T(8,128)(2,1)S(1)} %copy-done.1, bf16[768,768]{1,0:T(8,128)(2,1)S(1)} %copy-done.2), custom_call_target="tpu_custom_call" | custom-call | flops 1207959552 | bytes 8388608 | tf_op jit(solution)/shard_map/close/pallas_call | solution.py:425
  144.5 1.1 all-to-all-done.3.spread_ref
  145.6 1.0 collect.1
  146.6 14.9 %all-gather = bf16[384,384]{1,0:T(8,128)(2,1)S(1)} all-gather(bf16[48,384]{1,0:T(8,128)(2,1)S(1)} %collect.1), channel_id=2, replica_groups=mesh['seq'=16,'slide'=8] {'slide'}, dimensions={0}, use_global_device_ids=true | all-gather | bytes 331776 | tf_op jit(solution)/shard_map/all_gather | solution.py:465
  161.5 1.3 settle.1
  (1 shorter events, 0.0 us)
Async XLA Ops:
  7.2 17.1 %copy-start = (s32[1,4,16,8]{2,3,1,0:T(8,128)S(1)}, s32[1,4,16,8]{2,3,1,0:T(8,128)}, u32[]{:S(2)}) copy-start(s32[1,4,16,8]{2,3,1,0:T(8,128)} %param.8) | copy-start | bytes 6148
  7.2 96.3 %all-gather.3.cloned.1.call-start = ((), (), s32[]{:S(2)}) async-start(), calls=%async_computation.4 | async-start | bytes 6684672 | tf_op jit(solution)/shard_map/all_gather | solution.py:446
  15.6 44.1 %all-to-all-start = ((bf16[16,256,256]{2,1,0:T(8,128)(2,1)}), bf16[16,256,256]{2,1,0:T(8,128)(2,1)S(1)}, u32[]{:S(2)}, u32[]{:S(2)}) async-start(bf16[16,256,256]{2,1,0:T(8,128)(2,1)} %project.1), calls=%async_computation | async-start | bytes 4194304 | tf_op jit(solution)/shard_map/all_to_all | solution.py:448
  59.7 1.3 copy-start.6
  74.2 22.6 %all-to-all-start.1 = ((bf16[16,64,256]{2,1,0:T(8,128)(2,1)}), bf16[16,64,256]{2,1,0:T(8,128)(2,1)S(1)}, u32[]{:S(2)}, u32[]{:S(2)}) async-start(bf16[16,64,256]{2,1,0:T(8,128)(2,1)} %get-tuple-element.21), calls=%async_computation.1 | async-start | bytes 1048576 | tf_op jit(solution)/shard_map/all_to_all | solution.py:451
  96.8 6.7 %copy-start.3 = (bf16[16,64,256]{2,1,0:T(8,128)(2,1)}, bf16[16,64,256]{2,1,0:T(8,128)(2,1)S(1)}, u32[]{:S(2)}) copy-start(bf16[16,64,256]{2,1,0:T(8,128)(2,1)S(1)} %all-to-all-done.1.back_ref.att_ref) | copy-start | bytes 1572868
  96.8 34.8 %all-to-all-start.2 = ((bf16[16,192,256]{2,1,0:T(8,128)(2,1)}), bf16[16,192,256]{2,1,0:T(8,128)(2,1)}, u32[]{:S(2)}, u32[]{:S(2)}) async-start(bf16[16,192,256]{2,1,0:T(8,128)(2,1)} %backward.1.res_ref), calls=%async_computation.2 | async-start | bytes 3145728 | tf_op jit(solution)/shard_map/all_to_all | solution.py:453
  103.5 35.0 %copy-start.1 = (bf16[768,2304]{1,0:T(8,128)(2,1)S(1)}, bf16[768,2304]{1,0:T(8,128)(2,1)}, u32[]{:S(2)}) copy-start(bf16[768,2304]{1,0:T(8,128)(2,1)} %w_ref.1) | copy-start | bytes 10616836
  111.7 4.0 %collective-permute-start = (bf16[4,768,128]{2,1,0:T(8,128)(2,1)}, bf16[4,768,128]{2,1,0:T(8,128)(2,1)}, u32[]{:S(2)}, u32[]{:S(2)}) collective-permute-start(bf16[4,768,128]{2,1,0:T(8,128)(2,1)} %get-tuple-element.23), channel_id=1, source_target_pairs={{0,1},{1,0},{2,3},{3,2},{4,5},{5,4},{6,7},{7,6},{8,9},{9,8},{10,11... | collective-permute-start | bytes 2359304 | tf_op jit(solution)/shard_map/ppermute | solution.py:455
  115.7 1.1 copy-start.5
  118.2 7.8 %collective-permute-start.1 = (bf16[768,128]{1,0:T(8,128)(2,1)S(1)}, bf16[768,128]{1,0:T(8,128)(2,1)S(1)}, u32[]{:S(2)}, u32[]{:S(2)}) collective-permute-start(bf16[768,128]{1,0:T(8,128)(2,1)S(1)} %get-tuple-element.25), channel_id=1, source_target_pairs={{0,4},{1,5},{2,6},{3,7},{4,0},{5,1},{6,2},{7,3},{8,12},{9,13},{10,... | collective-permute-start | bytes 589832 | tf_op jit(solution)/shard_map/ppermute | solution.py:458
  121.2 9.6 %collective-permute-start.2 = (bf16[768,128]{1,0:T(8,128)(2,1)S(1)}, bf16[768,128]{1,0:T(8,128)(2,1)S(1)}, u32[]{:S(2)}, u32[]{:S(2)}) collective-permute-start(bf16[768,128]{1,0:T(8,128)(2,1)S(1)} %get-tuple-element.26), channel_id=1, source_target_pairs={{0,2},{1,3},{2,4},{3,5},{4,6},{5,7},{6,0},{7,1},{8,10},{9,11},{10,... | collective-permute-start | bytes 589832 | tf_op jit(solution)/shard_map/ppermute | solution.py:458
  121.5 9.3 %collective-permute-start.3 = (bf16[768,128]{1,0:T(8,128)(2,1)S(1)}, bf16[768,128]{1,0:T(8,128)(2,1)S(1)}, u32[]{:S(2)}, u32[]{:S(2)}) collective-permute-start(bf16[768,128]{1,0:T(8,128)(2,1)S(1)} %get-tuple-element.27), channel_id=1, source_target_pairs={{0,6},{1,7},{2,0},{3,1},{4,2},{5,3},{6,4},{7,5},{8,14},{9,15},{10,... | collective-permute-start | bytes 589832 | tf_op jit(solution)/shard_map/ppermute | solution.py:458
  131.5 14.1 %all-to-all-start.3 = ((bf16[16,48,128]{2,1,0:T(8,128)(2,1)}), bf16[16,48,128]{2,1,0:T(8,128)(2,1)}, u32[]{:S(2)}, u32[]{:S(2)}) async-start(bf16[16,48,128]{2,1,0:T(8,128)(2,1)} %bitcast.15), calls=%async_computation.3 | async-start | bytes 393216 | tf_op jit(solution)/shard_map/all_to_all | solution.py:464
  138.5 1.3 copy-start.2
  139.8 1.0 copy-start.4
Sparse Core Ops, SparseCore 0:
  10.2 91.9 all-gather.2

commit v5 on v4

--- a/solution.py
+++ b/solution.py
@@ -14,6 +14,7 @@
 BF16 = jnp.bfloat16
 SCALE = HD ** (-0.5)
 NB = 4
+HEADS_STEP = 4
 
 
 def slot_of(head):
@@ -33,12 +34,12 @@
         wo_ref[...], cot_ref[...], (((1,), (1,)), ((), ())), preferred_element_type=F32
     ).astype(BF16)
     qt = qt * jnp.asarray(SCALE, BF16)
-    for half in range(2):
-        head = 2 * step + half
+    for part in range(HEADS_STEP):
+        head = HEADS_STEP * step + part
         row = head // HPG
         place = head - row * HPG
         slot = 4 * row + place + jnp.where(place >= row, 1, 0)
-        rows = slice(half * HD, half * HD + HD)
+        rows = slice(part * HD, part * HD + HD)
         out_ref[slot, 0:HD, :] = qt[rows]
         out_ref[slot, HD : 2 * HD, :] = kt[rows]
         out_ref[slot, 2 * HD : 3 * HD, :] = vt[rows]
@@ -52,17 +53,18 @@
 
 def project(x, cot, w_qkv, w_out):
     tok, width = x.shape
-    pairs = H // 2
+    steps = H // HEADS_STEP
+    wide = HEADS_STEP * HD
     return pl.pallas_call(
         project_body,
-        grid=(pairs,),
+        grid=(steps,),
         in_specs=[
             pl.BlockSpec((tok, width), lambda i: (0, 0)),
             pl.BlockSpec((tok, width), lambda i: (0, 0)),
-            pl.BlockSpec((width, 2 * HD), lambda i: (0, i)),
-            pl.BlockSpec((width, 2 * HD), lambda i: (0, i + pairs)),
-            pl.BlockSpec((width, 2 * HD), lambda i: (0, i + 2 * pairs)),
-            pl.BlockSpec((2 * HD, width), lambda i: (i, 0)),
+            pl.BlockSpec((width, wide), lambda i: (0, i)),
+            pl.BlockSpec((width, wide), lambda i: (0, i + steps)),
+            pl.BlockSpec((width, wide), lambda i: (0, i + 2 * steps)),
+            pl.BlockSpec((wide, width), lambda i: (i, 0)),
         ],
         out_specs=pl.BlockSpec((16, 4 * HD, tok), lambda i: (0, 0, 0)),
         out_shape=jax.ShapeDtypeStruct((16, 4 * HD, tok), BF16),
@@ -211,7 +213,7 @@
     def _():
         def finish(i, carry):
             both = jnp.concatenate([dkv[2 * i], dkv[2 * i + 1]], axis=0)
-            out_ref[i, HD:, :] = both.T.astype(BF16)
+            out_ref[i, HD:, :] = both.astype(BF16).T
             return carry
 
         lax.fori_loop(0, blocks, finish, 0)
@@ -256,8 +258,8 @@
 
     @pl.when(step == 0)
     def _():
-        attended = jnp.concatenate([back_ref[slot_of(h)] for h in range(H)], axis=0)
-        out_acc[...] = jnp.dot(attended, cot_ref[...], preferred_element_type=F32).astype(BF16)
+        attended = jnp.concatenate([back_ref[slot_of(h)] for h in range(H)], axis=0).T
+        out_acc[...] = jnp.dot(cot_ref[...].T, attended, preferred_element_type=F32).astype(BF16)
         acc[...] = part
 
     @pl.when(step > 0)
@@ -266,35 +268,27 @@
 
     @pl.when(step == pl.num_programs(0) - 1)
     def _():
-        in_part = acc[...].T.astype(BF16)
-        out_part = out_acc[...]
-        rows, width = out_part.shape
-        out_cols = width // 8
-        in_cols = in_part.shape[1] // 8
-        fill = jnp.zeros((rows, 128 - out_cols - in_cols), BF16)
-        pieces = [
-            jnp.concatenate(
-                [
-                    out_part[:, k * out_cols : (k + 1) * out_cols],
-                    in_part[:, k * in_cols : (k + 1) * in_cols],
-                    fill,
-                ],
-                axis=1,
-            )
-            for k in range(8)
-        ]
+        out_cols = out_acc.shape[0] // 8
+        in_cols = acc.shape[0] // 8
+        fill = jnp.zeros((128 - out_cols - in_cols, acc.shape[1]), F32)
+
+        def place(ref, slot, k):
+            ref[slot, :out_cols, :] = out_acc[k * out_cols : (k + 1) * out_cols]
+            ref[slot, out_cols:, :] = jnp.concatenate(
+                [acc[k * in_cols : (k + 1) * in_cols], fill], axis=0
+            ).astype(BF16)
 
         @pl.when(core_ref[0] == 0)
         def _():
             for k in range(4):
-                mine_ref[k] = pieces[2 * k]
-                theirs_ref[k] = pieces[2 * k + 1]
+                place(mine_ref, k, 2 * k)
+                place(theirs_ref, k, 2 * k + 1)
 
         @pl.when(core_ref[0] != 0)
         def _():
             for k in range(4):
-                mine_ref[k] = pieces[2 * k + 1]
-                theirs_ref[k] = pieces[2 * k]
+                place(mine_ref, k, 2 * k + 1)
+                place(theirs_ref, k, 2 * k)
 
 
 def weigh(core, results, x_all, att_back, cot):
@@ -312,7 +306,7 @@
             whole,
         ],
         out_specs=[whole, whole],
-        out_shape=[jax.ShapeDtypeStruct((4, width, 128), BF16)] * 2,
+        out_shape=[jax.ShapeDtypeStruct((4, 128, width), BF16)] * 2,
         scratch_shapes=[pltpu.VMEM((wide, width), F32), pltpu.VMEM((width, width), BF16)],
         compiler_params=pltpu.CompilerParams(vmem_limit_bytes=60 * 2**20),
         cost_estimate=pl.CostEstimate(
@@ -341,6 +335,26 @@
         cost_estimate=pl.CostEstimate(flops=10**6, bytes_accessed=2 * 10**6, transcendentals=0),
         name="merge",
     )(chip, mine, got)
+
+
+def fold_body(a_ref, b_ref, c_ref, d_ref, out_ref):
+    total = (a_ref[...].astype(F32) + c_ref[...].astype(F32)) + (
+        b_ref[...].astype(F32) + d_ref[...].astype(F32)
+    )
+    out_ref[...] = total.astype(BF16).T
+
+
+def fold(parts):
+    whole = pl.BlockSpec(memory_space=pltpu.VMEM)
+    return pl.pallas_call(
+        fold_body,
+        in_specs=[whole] * 4,
+        out_specs=whole,
+        out_shape=jax.ShapeDtypeStruct(parts[0].shape[::-1], BF16),
+        compiler_params=pltpu.CompilerParams(vmem_limit_bytes=16 * 2**20),
+        cost_estimate=pl.CostEstimate(flops=10**6, bytes_accessed=10**6, transcendentals=0),
+        name="fold",
+    )(*parts)
 
 
 def collect_body(spread_ref, out_ref):
@@ -455,10 +469,10 @@
     got = lax.ppermute(theirs, "slide", [(i, i ^ 1) for i in range(slides)])
     keep, *sends = merge((slide // 2)[None], mine, got)
     takes = [
-        lax.ppermute(send, "slide", [(i, (i + 2 * k) % slides) for i in range(slides)]).astype(F32)
+        lax.ppermute(send, "slide", [(i, (i + 2 * k) % slides) for i in range(slides)])
         for k, send in zip((1, 2, 3), sends)
     ]
-    piece = ((keep.astype(F32) + takes[1]) + (takes[0] + takes[2])).astype(BF16)
+    piece = fold([keep] + takes)
     piece, back = lax.optimization_barrier((piece, back))
     piece = piece.reshape(peers, width // peers, piece.shape[1])
     spread = lax.all_to_all(piece, "seq", split_axis=0, concat_axis=0, tiled=True)

time: 170 us -> 167 us (0.982)
  Pallas kernels: 53.7 us -> 50.3 us
  starting transfers between devices: 34.9 us -> 32.3 us
  waiting for transfers between devices: 45.8 us -> 47.6 us
    all_gather x1, waiting for transfers between devices: 0.02 us -> 2.57 us  [shards(): x_all = lax.all_gather(x, 'seq', axis=0)]
    pallas_call x1 -> x2, Pallas kernels: 7.7 us -> 5.97 us  [the longest x1 5.82 us: project(): pl.pallas_call(project_body, grid=(steps,), in_specs=[pl.BlockSpec((tok,...]
    unnamed x14 -> x16, local copies, waits for them, and re-layouts: 4.79 us -> 5.46 us
  transfers between devices with their start and end apart: 9 -> 9, of which waited for: 5 -> 6; matrix products, arithmetic and copies ran while one was open for 1% -> 0% of each run, Pallas kernels for 30% -> 29%
where the time goes in v5:
time: 167 us; the launch traced here: 166 us
  Pallas kernels  50.3 us (30%)
  waiting for transfers between devices  47.6 us (29%)
  starting transfers between devices  32.3 us (19%)
  blocking collectives  15.3 us (9%)
  between operations  14.2 us (9%)
  local copies, waits for them, and re-layouts  6.13 us (4%)
    all_to_all x1, waiting for transfers between devices, shards(): lax.all_to_all(sent, 'seq', split_axis=0, concat_axis=0, tiled=True)  33.5 us
    pallas_call x1, Pallas kernels, backward(): pl.pallas_call(backward_body, grid=(blocks // NB,), in_specs=[pl.BlockSpe...  16.8 us
    all_gather x1, blocking collectives, shards(): lax.all_gather(collect(spread), 'slide', axis=0)  15.3 us
    pallas_call x1, Pallas kernels, forward(): pl.pallas_call(forward_body, grid=(blocks // NB,), in_specs=[pl.BlockSpec...  13.1 us
    all_to_all x1, starting transfers between devices, shards(): lax.all_to_all(sent, 'seq', split_axis=0, concat_axis=0, tiled=True)  8.6 us
    ppermute x3, waiting for transfers between devices, shards(): lax.ppermute(send, 'slide', [(i, (i + 2 * k) % slides) for i in range(sli...  7.7 us
    pallas_call x1, Pallas kernels, weigh(): pl.pallas_call(weigh_body, grid=(blocks // 4,), in_specs=[pl.BlockSpec(me...  7.06 us
    all_to_all x1, starting transfers between devices, shards(): lax.all_to_all(piece, 'seq', split_axis=0, concat_axis=0, tiled=True)  6.92 us
  transfers between devices with their start and end apart: 9, of which 6 were waited for; matrix products, arithmetic and copies ran while one was open for 0% of the time, Pallas kernels for 29%

profile of v5, /device:TPU:1, one launch (start us, length us, event | category | flops | bytes accessed | tf_op | source)
XLA Modules:
  0.0 165.8 jit_solution(4018407226638771982)
XLA Ops:
  7.2 0.0 copy-start
  7.2 0.0 all-gather.3.cloned.1.call-start
  7.2 0.7 all-gather.3.cloned.1.call-update
  7.9 5.8 %project.1 = bf16[16,256,256]{2,1,0:T(8,128)(2,1)} custom-call(bf16[256,768]{1,0:T(8,128)(2,1)} %bitcast.15, bf16[256,768]{1,0:T(8,128)(2,1)} %bitcast.13, bf16[768,2304]{1,0:T(8,128)(2,1)} %w_ref.1, bf16[768,2304]{1,0:T(8,128)(2,1)} %w_ref.1, bf16[768,2304]{1,0:T(8,128)(2,1)} %w_ref.1, bf16[768,768]{1,0:T(8,128)(2,1)} %wo_ref.3), custom_call_target="tpu_custom_call" | custom-call | flops 1207959552 | bytes 8388608 | tf_op jit(solution)/shard_map/project/pallas_call | solution.py:58
  13.7 8.6 %all-to-all-start = ((bf16[16,256,256]{2,1,0:T(8,128)(2,1)}), bf16[16,256,256]{2,1,0:T(8,128)(2,1)S(1)}, u32[]{:S(2)}, u32[]{:S(2)}) async-start(bf16[16,256,256]{2,1,0:T(8,128)(2,1)} %project.1), calls=%async_computation | async-start | bytes 4194304 | tf_op jit(solution)/shard_map/all_to_all | solution.py:462
  22.4 0.0 copy-done
  22.4 0.7 copy.13.tiles_ref
  23.1 33.5 %all-to-all-done.in_ref = bf16[16,256,256]{2,1,0:T(8,128)(2,1)S(1)} async-done(((bf16[16,256,256]{2,1,0:T(8,128)(2,1)}), bf16[16,256,256]{2,1,0:T(8,128)(2,1)S(1)}, u32[]{:S(2)}, u32[]{:S(2)}) %all-to-all-start) | async-done | bytes 2097184 | tf_op jit(solution)/shard_map/all_to_all | solution.py:462
  56.5 0.0 copy-start.7
  56.5 1.3 copy-done.7
  57.8 13.1 %forward.1 = (bf16[16,64,256]{2,1,0:T(8,128)(2,1)}, bf16[16,1280,256]{2,1,0:T(8,128)(2,1)}, f32[16,8,256]{2,1,0:T(8,128)}) custom-call(s32[16,8]{1,0:T(8,128)} %copy.13.tiles_ref, s32[32]{0:T(128)} %bitcast.18, bf16[16,256,256]{2,1,0:T(8,128)(2,1)} %copy-done.7), custom_call_target="tpu_custom_call" | custom-call | flops 5368709120 | bytes 14680064 | tf_op jit(solution)/shard_map/forward/pallas_call | solution.py:132
  71.0 3.9 %all-to-all-start.1 = ((bf16[16,64,256]{2,1,0:T(8,128)(2,1)}), bf16[16,64,256]{2,1,0:T(8,128)(2,1)S(1)}, u32[]{:S(2)}, u32[]{:S(2)}) async-start(bf16[16,64,256]{2,1,0:T(8,128)(2,1)} %get-tuple-element.21), calls=%async_computation.1 | async-start | bytes 1048576 | tf_op jit(solution)/shard_map/all_to_all | solution.py:465
  74.9 16.8 %backward.1.res_ref = bf16[16,192,256]{2,1,0:T(8,128)(2,1)} custom-call(s32[16,8]{1,0:T(8,128)} %copy.13.tiles_ref, bf16[16,256,256]{2,1,0:T(8,128)(2,1)} %copy-done.7, bf16[16,1280,256]{2,1,0:T(8,128)(2,1)} %get-tuple-element.19.exp_ref, f32[16,8,256]{2,1,0:T(8,128)} %get-tuple-element.20.stat_ref), custom_call_target="tpu_custom_call" | custom-call | flops 10737418240 | bytes 16777216 | tf_op jit(solution)/shard_map/backward/pallas_call | solution.py:227
  91.7 0.0 all-to-all-done.1.back_ref.att_ref
  91.7 0.0 copy-start.3
  91.7 6.7 %all-to-all-start.2 = ((bf16[16,192,256]{2,1,0:T(8,128)(2,1)}), bf16[16,192,256]{2,1,0:T(8,128)(2,1)}, u32[]{:S(2)}, u32[]{:S(2)}) async-start(bf16[16,192,256]{2,1,0:T(8,128)(2,1)} %backward.1.res_ref), calls=%async_computation.2 | async-start | bytes 3145728 | tf_op jit(solution)/shard_map/all_to_all | solution.py:467
  98.4 2.6 %all-gather.3.cloned.1.call-done.x_ref = bf16[16,256,768]{2,1,0:T(8,128)(2,1)} async-done(((bf16[1,256,768]{2,1,0:T(8,128)(2,1)}), bf16[16,256,768]{2,1,0:T(8,128)(2,1)}) %all-gather.3.cloned.1.call-update) | async-done | bytes 6291472 | tf_op jit(solution)/shard_map/all_gather | solution.py:460
  101.0 0.0 copy-done.3
  101.0 0.0 copy-start.1
  101.0 7.1 %weigh.1 = (bf16[4,128,768]{2,1,0:T(8,128)(2,1)}, bf16[4,128,768]{2,1,0:T(8,128)(2,1)}) custom-call(s32[1]{0:T(128)} %bitcast.1.core_ref, bf16[16,192,256]{2,1,0:T(8,128)(2,1)} %backward.1.res_ref, bf16[16,256,768]{2,1,0:T(8,128)(2,1)} %all-gather.3.cloned.1.call-done.x_ref, bf16[16,64,256]{2,1,0:T(8,128)(2,1)} %copy-done.3, bf16[256,768]{1,0:T(8,128)(2,1)} %bitcast.14), custom_call_target="tpu_custom_call" | custom-call | flops 1207959552 | bytes 10485760 | tf_op jit(solution)/shard_map/weigh/pallas_call | solution.py:298
  108.1 1.2 collective-permute-start
  109.3 2.3 %collective-permute-done.got_ref = bf16[4,128,768]{2,1,0:T(8,128)(2,1)} collective-permute-done((bf16[4,128,768]{2,1,0:T(8,128)(2,1)}, bf16[4,128,768]{2,1,0:T(8,128)(2,1)}, u32[]{:S(2)}, u32[]{:S(2)}) %collective-permute-start) | collective-permute-done | bytes 786464 | tf_op jit(solution)/shard_map/ppermute | solution.py:469
  111.5 0.0 copy-start.5
  111.5 1.1 copy-done.5
  112.7 1.3 merge.1
  114.0 1.3 collective-permute-start.1
  115.3 2.4 %collective-permute-start.2 = (bf16[128,768]{1,0:T(8,128)(2,1)S(1)}, bf16[128,768]{1,0:T(8,128)(2,1)S(1)}, u32[]{:S(2)}, u32[]{:S(2)}) collective-permute-start(bf16[128,768]{1,0:T(8,128)(2,1)S(1)} %get-tuple-element.26), channel_id=1, source_target_pairs={{0,4},{1,5},{2,6},{3,7},{4,0},{5,1},{6,2},{7,3},{8,12},{9,13},{10,... | collective-permute-start | bytes 589832 | tf_op jit(solution)/shard_map/ppermute | solution.py:472
  117.7 1.2 collective-permute-start.3
  118.9 2.6 %collective-permute-done.1.b_ref = bf16[128,768]{1,0:T(8,128)(2,1)S(1)} collective-permute-done((bf16[128,768]{1,0:T(8,128)(2,1)S(1)}, bf16[128,768]{1,0:T(8,128)(2,1)S(1)}, u32[]{:S(2)}, u32[]{:S(2)}) %collective-permute-start.1) | collective-permute-done | bytes 196640 | tf_op jit(solution)/shard_map/ppermute | solution.py:472
  121.5 5.1 %collective-permute-done.2.c_ref = bf16[128,768]{1,0:T(8,128)(2,1)S(1)} collective-permute-done((bf16[128,768]{1,0:T(8,128)(2,1)S(1)}, bf16[128,768]{1,0:T(8,128)(2,1)S(1)}, u32[]{:S(2)}, u32[]{:S(2)}) %collective-permute-start.2) | collective-permute-done | bytes 196640 | tf_op jit(solution)/shard_map/ppermute | solution.py:472
  126.6 0.0 collective-permute-done.3.d_ref
  126.6 0.2 fold.1
  126.7 0.0 copy-start.6
  126.7 0.7 copy-done.6
  127.4 0.0 all-to-all-done.2.back_ref
  127.4 6.9 %all-to-all-start.3 = ((bf16[16,48,128]{2,1,0:T(8,128)(2,1)}), bf16[16,48,128]{2,1,0:T(8,128)(2,1)}, u32[]{:S(2)}, u32[]{:S(2)}) async-start(bf16[16,48,128]{2,1,0:T(8,128)(2,1)} %bitcast.12), calls=%async_computation.3 | async-start | bytes 393216 | tf_op jit(solution)/shard_map/all_to_all | solution.py:478
  134.3 0.0 copy-done.1
  134.3 0.0 copy-start.2
  134.4 1.3 copy-done.2
  135.6 0.0 copy-start.4
  135.6 1.0 copy-done.4
  136.7 3.7 %close.1 = (bf16[256,768]{1,0:T(8,128)(2,1)}, bf16[256,768]{1,0:T(8,128)(2,1)}) custom-call(bf16[16,192,256]{2,1,0:T(8,128)(2,1)} %all-to-all-done.2.back_ref, bf16[16,64,256]{2,1,0:T(8,128)(2,1)S(1)} %copy-done.4, bf16[768,2304]{1,0:T(8,128)(2,1)S(1)} %copy-done.1, bf16[768,768]{1,0:T(8,128)(2,1)S(1)} %copy-done.2), custom_call_target="tpu_custom_call" | custom-call | flops 1207959552 | bytes 8388608 | tf_op jit(solution)/shard_map/close/pallas_call | solution.py:439
  140.4 1.0 all-to-all-done.3.spread_ref
  141.3 1.0 collect.1
  142.4 15.3 %all-gather = bf16[384,384]{1,0:T(8,128)(2,1)S(1)} all-gather(bf16[48,384]{1,0:T(8,128)(2,1)S(1)} %collect.1), channel_id=2, replica_groups=mesh['seq'=16,'slide'=8] {'slide'}, dimensions={0}, use_global_device_ids=true | all-gather | bytes 331776 | tf_op jit(solution)/shard_map/all_gather | solution.py:479
  157.7 1.3 settle.1
  (1 shorter events, 0.0 us)
Async XLA Ops:
  7.2 15.2 %copy-start = (s32[1,4,16,8]{2,3,1,0:T(8,128)S(1)}, s32[1,4,16,8]{2,3,1,0:T(8,128)}, u32[]{:S(2)}) copy-start(s32[1,4,16,8]{2,3,1,0:T(8,128)} %param.8) | copy-start | bytes 6148
  7.2 93.8 %all-gather.3.cloned.1.call-start = ((), (), s32[]{:S(2)}) async-start(), calls=%async_computation.4 | async-start | bytes 6684672 | tf_op jit(solution)/shard_map/all_gather | solution.py:460
  13.7 42.8 %all-to-all-start = ((bf16[16,256,256]{2,1,0:T(8,128)(2,1)}), bf16[16,256,256]{2,1,0:T(8,128)(2,1)S(1)}, u32[]{:S(2)}, u32[]{:S(2)}) async-start(bf16[16,256,256]{2,1,0:T(8,128)(2,1)} %project.1), calls=%async_computation | async-start | bytes 4194304 | tf_op jit(solution)/shard_map/all_to_all | solution.py:462
  56.5 1.3 copy-start.7
  71.0 20.7 %all-to-all-start.1 = ((bf16[16,64,256]{2,1,0:T(8,128)(2,1)}), bf16[16,64,256]{2,1,0:T(8,128)(2,1)S(1)}, u32[]{:S(2)}, u32[]{:S(2)}) async-start(bf16[16,64,256]{2,1,0:T(8,128)(2,1)} %get-tuple-element.21), calls=%async_computation.1 | async-start | bytes 1048576 | tf_op jit(solution)/shard_map/all_to_all | solution.py:465
  91.7 9.3 %copy-start.3 = (bf16[16,64,256]{2,1,0:T(8,128)(2,1)}, bf16[16,64,256]{2,1,0:T(8,128)(2,1)S(1)}, u32[]{:S(2)}) copy-start(bf16[16,64,256]{2,1,0:T(8,128)(2,1)S(1)} %all-to-all-done.1.back_ref.att_ref) | copy-start | bytes 1572868
  91.7 35.7 %all-to-all-start.2 = ((bf16[16,192,256]{2,1,0:T(8,128)(2,1)}), bf16[16,192,256]{2,1,0:T(8,128)(2,1)}, u32[]{:S(2)}, u32[]{:S(2)}) async-start(bf16[16,192,256]{2,1,0:T(8,128)(2,1)} %backward.1.res_ref), calls=%async_computation.2 | async-start | bytes 3145728 | tf_op jit(solution)/shard_map/all_to_all | solution.py:467
  101.0 33.3 %copy-start.1 = (bf16[768,2304]{1,0:T(8,128)(2,1)S(1)}, bf16[768,2304]{1,0:T(8,128)(2,1)}, u32[]{:S(2)}) copy-start(bf16[768,2304]{1,0:T(8,128)(2,1)} %w_ref.1) | copy-start | bytes 10616836
  108.1 3.5 %collective-permute-start = (bf16[4,128,768]{2,1,0:T(8,128)(2,1)}, bf16[4,128,768]{2,1,0:T(8,128)(2,1)}, u32[]{:S(2)}, u32[]{:S(2)}) collective-permute-start(bf16[4,128,768]{2,1,0:T(8,128)(2,1)} %get-tuple-element.23), channel_id=1, source_target_pairs={{0,1},{1,0},{2,3},{3,2},{4,5},{5,4},{6,7},{7,6},{8,9},{9,8},{10,11... | collective-permute-start | bytes 2359304 | tf_op jit(solution)/shard_map/ppermute | solution.py:469
  111.5 1.1 copy-start.5
  114.0 7.5 %collective-permute-start.1 = (bf16[128,768]{1,0:T(8,128)(2,1)S(1)}, bf16[128,768]{1,0:T(8,128)(2,1)S(1)}, u32[]{:S(2)}, u32[]{:S(2)}) collective-permute-start(bf16[128,768]{1,0:T(8,128)(2,1)S(1)} %get-tuple-element.25), channel_id=1, source_target_pairs={{0,2},{1,3},{2,4},{3,5},{4,6},{5,7},{6,0},{7,1},{8,10},{9,11},{10,... | collective-permute-start | bytes 589832 | tf_op jit(solution)/shard_map/ppermute | solution.py:472
  115.3 11.3 %collective-permute-start.2 = (bf16[128,768]{1,0:T(8,128)(2,1)S(1)}, bf16[128,768]{1,0:T(8,128)(2,1)S(1)}, u32[]{:S(2)}, u32[]{:S(2)}) collective-permute-start(bf16[128,768]{1,0:T(8,128)(2,1)S(1)} %get-tuple-element.26), channel_id=1, source_target_pairs={{0,4},{1,5},{2,6},{3,7},{4,0},{5,1},{6,2},{7,3},{8,12},{9,13},{10,... | collective-permute-start | bytes 589832 | tf_op jit(solution)/shard_map/ppermute | solution.py:472
  117.7 8.9 %collective-permute-start.3 = (bf16[128,768]{1,0:T(8,128)(2,1)S(1)}, bf16[128,768]{1,0:T(8,128)(2,1)S(1)}, u32[]{:S(2)}, u32[]{:S(2)}) collective-permute-start(bf16[128,768]{1,0:T(8,128)(2,1)S(1)} %get-tuple-element.27), channel_id=1, source_target_pairs={{0,6},{1,7},{2,0},{3,1},{4,2},{5,3},{6,4},{7,5},{8,14},{9,15},{10,... | collective-permute-start | bytes 589832 | tf_op jit(solution)/shard_map/ppermute | solution.py:472
  126.7 0.7 copy-start.6
  127.4 13.9 %all-to-all-start.3 = ((bf16[16,48,128]{2,1,0:T(8,128)(2,1)}), bf16[16,48,128]{2,1,0:T(8,128)(2,1)}, u32[]{:S(2)}, u32[]{:S(2)}) async-start(bf16[16,48,128]{2,1,0:T(8,128)(2,1)} %bitcast.12), calls=%async_computation.3 | async-start | bytes 393216 | tf_op jit(solution)/shard_map/all_to_all | solution.py:478
  134.3 1.3 copy-start.2
  135.6 1.0 copy-start.4
Sparse Core Ops, SparseCore 0:
  10.2 90.7 all-gather.2

commit v6 on v5

--- a/solution.py
+++ b/solution.py
@@ -114,7 +114,7 @@
         expo = jnp.exp(scores - top)
         share = 1.0 / jnp.sum(expo, axis=0, keepdims=True)
         low = expo.astype(BF16)
-        exp_ref[n] = low
+        exp_ref[p] = low
         values_t = jnp.concatenate([vt[t] for t in tiles], axis=1)
         attended = jnp.dot(values_t, low, preferred_element_type=F32) * share
         scaled = (gt.astype(F32) * share).astype(BF16)
@@ -137,17 +137,17 @@
             pl.BlockSpec(memory_space=pltpu.SMEM),
             whole,
         ],
-        out_specs=[whole, pl.BlockSpec((NB, slots, tok), lambda i: (i, 0, 0)), whole],
+        out_specs=[whole] * 4,
         out_shape=[
             jax.ShapeDtypeStruct((blocks, HD, tok), BF16),
             jax.ShapeDtypeStruct((blocks, slots, tok), BF16),
             jax.ShapeDtypeStruct((blocks, 8, tok), F32),
+            jax.ShapeDtypeStruct((total, TILE, 2 * HD), BF16),
         ],
         scratch_shapes=[
-            pltpu.VMEM((total, TILE, 2 * HD), BF16),
             pltpu.VMEM((total, HD, TILE), BF16),
         ],
-        compiler_params=pltpu.CompilerParams(vmem_limit_bytes=60 * 2**20),
+        compiler_params=pltpu.CompilerParams(vmem_limit_bytes=24 * 2**20),
         cost_estimate=pl.CostEstimate(
             flops=blocks * 4 * 2 * tok * slots * 2 * HD,
             bytes_accessed=14 * 2**20,
@@ -157,7 +157,7 @@
     )(tiles, valid, arrived)
 
 
-def backward_body(tiles_ref, in_ref, exp_ref, stat_ref, out_ref, kv, kt, dkv):
+def backward_body(tiles_ref, in_ref, exp_ref, stat_ref, kv, out_ref, kt, dkv):
     b = pl.program_id(0)
     blocks = in_ref.shape[0]
     listed = tiles_ref.shape[1]
@@ -165,11 +165,8 @@
     @pl.when(b == 0)
     def _():
         def prepare(i, carry):
-            both = in_ref[i, HD : 3 * HD, :]
-            flipped = both.T
             for c in range(2):
-                kt[2 * i + c] = both[:HD, c * TILE : (c + 1) * TILE]
-                kv[2 * i + c] = flipped[c * TILE : (c + 1) * TILE]
+                kt[2 * i + c] = in_ref[i, HD : 2 * HD, c * TILE : (c + 1) * TILE]
                 dkv[2 * i + c] = jnp.zeros((TILE, 2 * HD), F32)
             return carry
 
@@ -190,7 +187,7 @@
         work.append((n, p, tiles, scaled, grad_probs))
     for n, p, tiles, scaled, grad_probs in work:
         qt = in_ref[p, 0:HD, :]
-        low = exp_ref[n]
+        low = exp_ref[p]
         center = stat_ref[p, 1:2, :]
         grad_scores = (low.astype(F32) * (grad_probs - center)).astype(BF16)
         keys_t = jnp.concatenate([kt[t] for t in tiles], axis=1)
@@ -219,7 +216,7 @@
         lax.fori_loop(0, blocks, finish, 0)
 
 
-def backward(tiles, arrived, low, stats):
+def backward(tiles, arrived, low, stats, kv):
     blocks, rows, tok = arrived.shape
     total = blocks * tok // TILE
     slots = 10 * TILE
@@ -230,31 +227,31 @@
         in_specs=[
             pl.BlockSpec(memory_space=pltpu.SMEM),
             whole,
-            pl.BlockSpec((NB, slots, tok), lambda i: (i, 0, 0)),
+            whole,
+            whole,
             whole,
         ],
         out_specs=whole,
         out_shape=jax.ShapeDtypeStruct((blocks, 3 * HD, tok), BF16),
         scratch_shapes=[
-            pltpu.VMEM((total, TILE, 2 * HD), BF16),
             pltpu.VMEM((total, HD, TILE), BF16),
             pltpu.VMEM((total, TILE, 2 * HD), F32),
         ],
-        compiler_params=pltpu.CompilerParams(vmem_limit_bytes=60 * 2**20),
+        compiler_params=pltpu.CompilerParams(vmem_limit_bytes=24 * 2**20),
         cost_estimate=pl.CostEstimate(
             flops=blocks * 8 * 2 * tok * slots * 2 * HD,
             bytes_accessed=16 * 2**20,
             transcendentals=0,
         ),
         name="backward",
-    )(tiles, arrived, low, stats)
+    )(tiles, arrived, low, stats, kv)
 
 
 def weigh_body(core_ref, res_ref, x_ref, back_ref, cot_ref, mine_ref, theirs_ref, acc, out_acc):
     step = pl.program_id(0)
-    part = jnp.dot(res_ref[0], x_ref[0], preferred_element_type=F32)
-    for i in range(1, res_ref.shape[0]):
-        part += jnp.dot(res_ref[i], x_ref[i], preferred_element_type=F32)
+    grads = jnp.concatenate([res_ref[i] for i in range(res_ref.shape[0])], axis=1)
+    tokens = x_ref[...].reshape(-1, x_ref.shape[2])
+    part = jnp.dot(grads, tokens, preferred_element_type=F32)
 
     @pl.when(step == 0)
     def _():
@@ -461,18 +458,18 @@
     sent = project(x, cot, w_qkv, w_out)
     arrived = lax.all_to_all(sent, "seq", split_axis=0, concat_axis=0, tiled=True)
     group_tiles = lax.dynamic_index_in_dim(key_tiles[0], myself // 4, 0, keepdims=False)
-    att_sent, low, stats = forward(group_tiles, tile_valid[0], arrived)
+    att_sent, low, stats, kv = forward(group_tiles, tile_valid[0], arrived)
     att_back = lax.all_to_all(att_sent, "seq", split_axis=0, concat_axis=0, tiled=True)
-    results = backward(group_tiles, arrived, low, stats)
+    results = backward(group_tiles, arrived, low, stats, kv)
     back = lax.all_to_all(results, "seq", split_axis=0, concat_axis=0, tiled=True)
     mine, theirs = weigh(lax.rem(slide, 2)[None], results, x_all, att_back, cot)
     got = lax.ppermute(theirs, "slide", [(i, i ^ 1) for i in range(slides)])
     keep, *sends = merge((slide // 2)[None], mine, got)
-    takes = [
-        lax.ppermute(send, "slide", [(i, (i + 2 * k) % slides) for i in range(slides)])
-        for k, send in zip((1, 2, 3), sends)
-    ]
-    piece = fold([keep] + takes)
+    takes = {
+        k: lax.ppermute(sends[k - 1], "slide", [(i, (i + 2 * k) % slides) for i in range(slides)])
+        for k in (2, 1, 3)
+    }
+    piece = fold([keep, takes[1], takes[2], takes[3]])
     piece, back = lax.optimization_barrier((piece, back))
     piece = piece.reshape(peers, width // peers, piece.shape[1])
     spread = lax.all_to_all(piece, "seq", split_axis=0, concat_axis=0, tiled=True)

time: 167 us -> 172 us (1.030)
  local copies, waits for them, and re-layouts: 6.13 us -> 14.6 us
  Pallas kernels: 50.3 us -> 46 us
  starting transfers between devices: 32.3 us -> 34.4 us
    unnamed x16 -> x24, local copies, waits for them, and re-layouts: 5.46 us -> 14.5 us
    pallas_call x1, Pallas kernels: 16.8 us -> 13.9 us  [backward(): pl.pallas_call(backward_body, grid=(blocks // NB,), in_specs=[pl.BlockSpe...]
    all_gather x1, waiting for transfers between devices: 2.57 us -> 0.02 us  [shards(): x_all = lax.all_gather(x, 'seq', axis=0)]
    ppermute x1, starting transfers between devices: 1.21 us -> 3.55 us  [shards(): got = lax.ppermute(theirs, 'slide', [(i, i ^ 1) for i in range(slides)])]
  transfers between devices with their start and end apart: 9 -> 9, of which waited for: 6 -> 5; matrix products, arithmetic and copies ran while one was open for 0% -> 0% of each run, Pallas kernels for 29% -> 26%
where the time goes in v6:
time: 172 us; the launch traced here: 171 us
  waiting for transfers between devices  46.3 us (27%)
  Pallas kernels  46 us (27%)
  starting transfers between devices  34.4 us (20%)
  blocking collectives  15.3 us (9%)
  local copies, waits for them, and re-layouts  14.6 us (8%)
  between operations  14.2 us (8%)
    all_to_all x1, waiting for transfers between devices, shards(): lax.all_to_all(sent, 'seq', split_axis=0, concat_axis=0, tiled=True)  34.6 us
    all_gather x1, blocking collectives, shards(): lax.all_gather(collect(spread), 'slide', axis=0)  15.3 us
    unnamed x24, local copies, waits for them, and re-layouts  14.5 us
    pallas_call x1, Pallas kernels, backward(): pl.pallas_call(backward_body, grid=(blocks // NB,), in_specs=[pl.BlockSpe...  13.9 us
    pallas_call x1, Pallas kernels, forward(): pl.pallas_call(forward_body, grid=(blocks // NB,), in_specs=[pl.BlockSpec...  11.7 us
    all_to_all x1, starting transfers between devices, shards(): lax.all_to_all(sent, 'seq', split_axis=0, concat_axis=0, tiled=True)  8.73 us
    ppermute x3, waiting for transfers between devices, shards(): lax.ppermute(sends[k - 1], 'slide', [(i, (i + 2 * k) % slides) for i in r...  7.72 us
    pallas_call x1, Pallas kernels, weigh(): pl.pallas_call(weigh_body, grid=(blocks // 4,), in_specs=[pl.BlockSpec(me...  7.07 us
  transfers between devices with their start and end apart: 9, of which 5 were waited for; matrix products, arithmetic and copies ran while one was open for 0% of the time, Pallas kernels for 26%

profile of v6, /device:TPU:1, one launch (start us, length us, event | category | flops | bytes accessed | tf_op | source)
XLA Modules:
  0.0 170.7 jit_solution(11370480265513641715)
XLA Ops:
  7.2 0.0 copy-start
  7.2 0.0 all-gather.3.cloned.1.call-start
  7.2 0.7 all-gather.3.cloned.1.call-update
  7.9 5.8 %project.1 = bf16[16,256,256]{2,1,0:T(8,128)(2,1)} custom-call(bf16[256,768]{1,0:T(8,128)(2,1)} %bitcast.16, bf16[256,768]{1,0:T(8,128)(2,1)} %bitcast.14, bf16[768,2304]{1,0:T(8,128)(2,1)} %w_ref.1, bf16[768,2304]{1,0:T(8,128)(2,1)} %w_ref.1, bf16[768,2304]{1,0:T(8,128)(2,1)} %w_ref.1, bf16[768,768]{1,0:T(8,128)(2,1)} %wo_ref.3), custom_call_target="tpu_custom_call" | custom-call | flops 1207959552 | bytes 8388608 | tf_op jit(solution)/shard_map/project/pallas_call | solution.py:58
  13.7 0.0 copy-start.7
  13.8 8.7 %all-to-all-start = ((bf16[16,256,256]{2,1,0:T(8,128)(2,1)}), bf16[16,256,256]{2,1,0:T(8,128)(2,1)S(1)}, u32[]{:S(2)}, u32[]{:S(2)}) async-start(bf16[16,256,256]{2,1,0:T(8,128)(2,1)} %project.1), calls=%async_computation | async-start | bytes 4194304 | tf_op jit(solution)/shard_map/all_to_all | solution.py:459
  22.5 0.0 copy-done
  22.5 0.1 copy.13.tiles_ref
  22.6 34.6 %all-to-all-done.in_ref = bf16[16,256,256]{2,1,0:T(8,128)(2,1)S(1)} async-done(((bf16[16,256,256]{2,1,0:T(8,128)(2,1)}), bf16[16,256,256]{2,1,0:T(8,128)(2,1)S(1)}, u32[]{:S(2)}, u32[]{:S(2)}) %all-to-all-start) | async-done | bytes 2097184 | tf_op jit(solution)/shard_map/all_to_all | solution.py:459
  57.2 0.0 copy-done.7
  57.2 11.7 %forward.1 = (bf16[16,64,256]{2,1,0:T(8,128)(2,1)}, bf16[16,1280,256]{2,1,0:T(8,128)(2,1)S(1)}, f32[16,8,256]{2,1,0:T(8,128)S(1)}, bf16[32,128,128]{2,1,0:T(8,128)(2,1)S(1)}) custom-call(s32[16,8]{1,0:T(8,128)S(1)} %copy.13.tiles_ref, s32[32]{0:T(128)S(1)} %bitcast.13, bf16[16,256,256]{2,1,0:T(8,128)(2,1)S(1)} %all-to-all-done.in_ref), custom_call_target="tpu_custom_call" | custom-call | flops 5368709120 | bytes 14680064 | tf_op jit(solution)/shard_map/forward/pallas_call | solution.py:132
  68.9 0.0 copy-start.8
  68.9 4.0 %copy-done.8 = bf16[16,1280,256]{2,1,0:T(8,128)(2,1)} copy-done((bf16[16,1280,256]{2,1,0:T(8,128)(2,1)}, bf16[16,1280,256]{2,1,0:T(8,128)(2,1)S(1)}, u32[]{:S(2)}) %copy-start.8) | copy-done | bytes 10485784
  72.9 0.0 copy-start.10
  72.9 1.0 copy-done.10
  73.9 3.6 %all-to-all-start.1 = ((bf16[16,64,256]{2,1,0:T(8,128)(2,1)}), bf16[16,64,256]{2,1,0:T(8,128)(2,1)S(1)}, u32[]{:S(2)}, u32[]{:S(2)}) async-start(bf16[16,64,256]{2,1,0:T(8,128)(2,1)} %get-tuple-element.23), calls=%async_computation.1 | async-start | bytes 1048576 | tf_op jit(solution)/shard_map/all_to_all | solution.py:462
  77.5 0.0 copy-start.9
  77.5 4.1 %copy-done.9 = bf16[16,1280,256]{2,1,0:T(8,128)(2,1)S(1)} copy-done((bf16[16,1280,256]{2,1,0:T(8,128)(2,1)S(1)}, bf16[16,1280,256]{2,1,0:T(8,128)(2,1)}, u32[]{:S(2)}) %copy-start.9) | copy-done | bytes 10485784
  81.6 0.0 copy-start.11
  81.6 1.3 copy-done.11
  82.9 13.9 %backward.1.res_ref = bf16[16,192,256]{2,1,0:T(8,128)(2,1)} custom-call(s32[16,8]{1,0:T(8,128)S(1)} %copy.13.tiles_ref, bf16[16,256,256]{2,1,0:T(8,128)(2,1)S(1)} %all-to-all-done.in_ref, bf16[16,1280,256]{2,1,0:T(8,128)(2,1)S(1)} %copy-done.9, f32[16,8,256]{2,1,0:T(8,128)S(1)} %get-tuple-element.21.stat_ref, bf16[32,128,128]{2,1,0:T(8,128)(2,1)S(1)} %copy-done.11), custom_call_target="tpu_custom_call" | custom-call | flops 10737418240 | bytes 16777216 | tf_op jit(solution)/shard_map/backward/pallas_call | solution.py:224
  96.8 0.0 all-to-all-done.1.back_ref.att_ref
  96.8 0.0 copy-start.3
  96.8 6.7 %all-to-all-start.2 = ((bf16[16,192,256]{2,1,0:T(8,128)(2,1)}), bf16[16,192,256]{2,1,0:T(8,128)(2,1)}, u32[]{:S(2)}, u32[]{:S(2)}) async-start(bf16[16,192,256]{2,1,0:T(8,128)(2,1)} %backward.1.res_ref), calls=%async_computation.2 | async-start | bytes 3145728 | tf_op jit(solution)/shard_map/all_to_all | solution.py:464
  103.4 0.0 all-gather.3.cloned.1.call-done.x_ref
  103.5 0.0 copy-done.3
  103.5 0.0 copy-start.1
  103.5 7.1 %weigh.1 = (bf16[4,128,768]{2,1,0:T(8,128)(2,1)}, bf16[4,128,768]{2,1,0:T(8,128)(2,1)}) custom-call(s32[1]{0:T(128)} %bitcast.1.core_ref, bf16[16,192,256]{2,1,0:T(8,128)(2,1)} %backward.1.res_ref, bf16[16,256,768]{2,1,0:T(8,128)(2,1)} %all-gather.3.cloned.1.call-done.x_ref, bf16[16,64,256]{2,1,0:T(8,128)(2,1)} %copy-done.3, bf16[256,768]{1,0:T(8,128)(2,1)} %bitcast.15), custom_call_target="tpu_custom_call" | custom-call | flops 1207959552 | bytes 10485760 | tf_op jit(solution)/shard_map/weigh/pallas_call | solution.py:295
  110.6 3.6 %collective-permute-start = (bf16[4,128,768]{2,1,0:T(8,128)(2,1)}, bf16[4,128,768]{2,1,0:T(8,128)(2,1)}, u32[]{:S(2)}, u32[]{:S(2)}) collective-permute-start(bf16[4,128,768]{2,1,0:T(8,128)(2,1)} %get-tuple-element.25), channel_id=1, source_target_pairs={{0,1},{1,0},{2,3},{3,2},{4,5},{5,4},{6,7},{7,6},{8,9},{9,8},{10,11... | collective-permute-start | bytes 2359304 | tf_op jit(solution)/shard_map/ppermute | solution.py:466
  114.1 2.3 %collective-permute-done.got_ref = bf16[4,128,768]{2,1,0:T(8,128)(2,1)} collective-permute-done((bf16[4,128,768]{2,1,0:T(8,128)(2,1)}, bf16[4,128,768]{2,1,0:T(8,128)(2,1)}, u32[]{:S(2)}, u32[]{:S(2)}) %collective-permute-start) | collective-permute-done | bytes 786464 | tf_op jit(solution)/shard_map/ppermute | solution.py:466
  116.4 0.0 copy-start.5
  116.4 1.1 copy-done.5
  117.5 1.3 merge.1
  118.8 1.3 collective-permute-start.1
  120.1 2.5 %collective-permute-start.2 = (bf16[128,768]{1,0:T(8,128)(2,1)S(1)}, bf16[128,768]{1,0:T(8,128)(2,1)S(1)}, u32[]{:S(2)}, u32[]{:S(2)}) collective-permute-start(bf16[128,768]{1,0:T(8,128)(2,1)S(1)} %get-tuple-element.28), channel_id=1, source_target_pairs={{0,4},{1,5},{2,6},{3,7},{4,0},{5,1},{6,2},{7,3},{8,12},{9,13},{10,... | collective-permute-start | bytes 589832 | tf_op jit(solution)/shard_map/ppermute | solution.py:469
  122.6 1.1 collective-permute-start.3
  123.7 2.6 %collective-permute-done.1.b_ref = bf16[128,768]{1,0:T(8,128)(2,1)S(1)} collective-permute-done((bf16[128,768]{1,0:T(8,128)(2,1)S(1)}, bf16[128,768]{1,0:T(8,128)(2,1)S(1)}, u32[]{:S(2)}, u32[]{:S(2)}) %collective-permute-start.1) | collective-permute-done | bytes 196640 | tf_op jit(solution)/shard_map/ppermute | solution.py:469
  126.3 5.1 %collective-permute-done.2.c_ref = bf16[128,768]{1,0:T(8,128)(2,1)S(1)} collective-permute-done((bf16[128,768]{1,0:T(8,128)(2,1)S(1)}, bf16[128,768]{1,0:T(8,128)(2,1)S(1)}, u32[]{:S(2)}, u32[]{:S(2)}) %collective-permute-start.2) | collective-permute-done | bytes 196640 | tf_op jit(solution)/shard_map/ppermute | solution.py:469
  131.4 0.0 collective-permute-done.3.d_ref
  131.4 0.2 fold.1
  131.6 0.0 copy-start.6
  131.6 0.7 copy-done.6
  132.3 0.0 all-to-all-done.2.back_ref
  132.3 6.9 %all-to-all-start.3 = ((bf16[16,48,128]{2,1,0:T(8,128)(2,1)}), bf16[16,48,128]{2,1,0:T(8,128)(2,1)}, u32[]{:S(2)}, u32[]{:S(2)}) async-start(bf16[16,48,128]{2,1,0:T(8,128)(2,1)} %bitcast.12), calls=%async_computation.3 | async-start | bytes 393216 | tf_op jit(solution)/shard_map/all_to_all | solution.py:475
  139.2 0.0 copy-done.1
  139.2 0.0 copy-start.2
  139.2 1.3 copy-done.2
  140.5 0.0 copy-start.4
  140.5 1.0 copy-done.4
  141.5 3.7 %close.1 = (bf16[256,768]{1,0:T(8,128)(2,1)}, bf16[256,768]{1,0:T(8,128)(2,1)}) custom-call(bf16[16,192,256]{2,1,0:T(8,128)(2,1)} %all-to-all-done.2.back_ref, bf16[16,64,256]{2,1,0:T(8,128)(2,1)S(1)} %copy-done.4, bf16[768,2304]{1,0:T(8,128)(2,1)S(1)} %copy-done.1, bf16[768,768]{1,0:T(8,128)(2,1)S(1)} %copy-done.2), custom_call_target="tpu_custom_call" | custom-call | flops 1207959552 | bytes 8388608 | tf_op jit(solution)/shard_map/close/pallas_call | solution.py:436
  145.2 1.0 all-to-all-done.3.spread_ref
  146.2 1.0 collect.1
  147.2 15.3 %all-gather = bf16[384,384]{1,0:T(8,128)(2,1)S(1)} all-gather(bf16[48,384]{1,0:T(8,128)(2,1)S(1)} %collect.1), channel_id=2, replica_groups=mesh['seq'=16,'slide'=8] {'slide'}, dimensions={0}, use_global_device_ids=true | all-gather | bytes 331776 | tf_op jit(solution)/shard_map/all_gather | solution.py:476
  162.6 1.3 settle.1
  (1 shorter events, 0.0 us)
Async XLA Ops:
  7.2 15.3 %copy-start = (s32[1,4,16,8]{2,3,1,0:T(8,128)S(1)}, s32[1,4,16,8]{2,3,1,0:T(8,128)}, u32[]{:S(2)}) copy-start(s32[1,4,16,8]{2,3,1,0:T(8,128)} %param.8) | copy-start | bytes 6148
  7.2 96.3 %all-gather.3.cloned.1.call-start = ((), (), s32[]{:S(2)}) async-start(), calls=%async_computation.4 | async-start | bytes 6684672 | tf_op jit(solution)/shard_map/all_gather | solution.py:457
  13.7 43.5 %copy-start.7 = (s32[1,32]{1,0:T(1,128)S(1)}, s32[1,32]{1,0:T(1,128)}, u32[]{:S(2)}) copy-start(s32[1,32]{1,0:T(1,128)} %param.9) | copy-start | bytes 388
  13.8 43.5 %all-to-all-start = ((bf16[16,256,256]{2,1,0:T(8,128)(2,1)}), bf16[16,256,256]{2,1,0:T(8,128)(2,1)S(1)}, u32[]{:S(2)}, u32[]{:S(2)}) async-start(bf16[16,256,256]{2,1,0:T(8,128)(2,1)} %project.1), calls=%async_computation | async-start | bytes 4194304 | tf_op jit(solution)/shard_map/all_to_all | solution.py:459
  68.9 4.0 %copy-start.8 = (bf16[16,1280,256]{2,1,0:T(8,128)(2,1)}, bf16[16,1280,256]{2,1,0:T(8,128)(2,1)S(1)}, u32[]{:S(2)}) copy-start(bf16[16,1280,256]{2,1,0:T(8,128)(2,1)S(1)} %get-tuple-element.20.exp_ref) | copy-start | bytes 31457284
  72.9 1.0 copy-start.10
  73.9 22.9 %all-to-all-start.1 = ((bf16[16,64,256]{2,1,0:T(8,128)(2,1)}), bf16[16,64,256]{2,1,0:T(8,128)(2,1)S(1)}, u32[]{:S(2)}, u32[]{:S(2)}) async-start(bf16[16,64,256]{2,1,0:T(8,128)(2,1)} %get-tuple-element.23), calls=%async_computation.1 | async-start | bytes 1048576 | tf_op jit(solution)/shard_map/all_to_all | solution.py:462
  77.5 4.1 %copy-start.9 = (bf16[16,1280,256]{2,1,0:T(8,128)(2,1)S(1)}, bf16[16,1280,256]{2,1,0:T(8,128)(2,1)}, u32[]{:S(2)}) copy-start(bf16[16,1280,256]{2,1,0:T(8,128)(2,1)} %copy-done.8) | copy-start | bytes 31457284
  81.6 1.3 copy-start.11
  96.8 6.7 %copy-start.3 = (bf16[16,64,256]{2,1,0:T(8,128)(2,1)}, bf16[16,64,256]{2,1,0:T(8,128)(2,1)S(1)}, u32[]{:S(2)}) copy-start(bf16[16,64,256]{2,1,0:T(8,128)(2,1)S(1)} %all-to-all-done.1.back_ref.att_ref) | copy-start | bytes 1572868
  96.8 35.5 %all-to-all-start.2 = ((bf16[16,192,256]{2,1,0:T(8,128)(2,1)}), bf16[16,192,256]{2,1,0:T(8,128)(2,1)}, u32[]{:S(2)}, u32[]{:S(2)}) async-start(bf16[16,192,256]{2,1,0:T(8,128)(2,1)} %backward.1.res_ref), calls=%async_computation.2 | async-start | bytes 3145728 | tf_op jit(solution)/shard_map/all_to_all | solution.py:464
  103.5 35.7 %copy-start.1 = (bf16[768,2304]{1,0:T(8,128)(2,1)S(1)}, bf16[768,2304]{1,0:T(8,128)(2,1)}, u32[]{:S(2)}) copy-start(bf16[768,2304]{1,0:T(8,128)(2,1)} %w_ref.1) | copy-start | bytes 10616836
  110.6 5.8 %collective-permute-start = (bf16[4,128,768]{2,1,0:T(8,128)(2,1)}, bf16[4,128,768]{2,1,0:T(8,128)(2,1)}, u32[]{:S(2)}, u32[]{:S(2)}) collective-permute-start(bf16[4,128,768]{2,1,0:T(8,128)(2,1)} %get-tuple-element.25), channel_id=1, source_target_pairs={{0,1},{1,0},{2,3},{3,2},{4,5},{5,4},{6,7},{7,6},{8,9},{9,8},{10,11... | collective-permute-start | bytes 2359304 | tf_op jit(solution)/shard_map/ppermute | solution.py:466
  116.4 1.1 copy-start.5
  118.8 7.5 %collective-permute-start.1 = (bf16[128,768]{1,0:T(8,128)(2,1)S(1)}, bf16[128,768]{1,0:T(8,128)(2,1)S(1)}, u32[]{:S(2)}, u32[]{:S(2)}) collective-permute-start(bf16[128,768]{1,0:T(8,128)(2,1)S(1)} %get-tuple-element.27), channel_id=1, source_target_pairs={{0,2},{1,3},{2,4},{3,5},{4,6},{5,7},{6,0},{7,1},{8,10},{9,11},{10,... | collective-permute-start | bytes 589832 | tf_op jit(solution)/shard_map/ppermute | solution.py:469
  120.1 11.3 %collective-permute-start.2 = (bf16[128,768]{1,0:T(8,128)(2,1)S(1)}, bf16[128,768]{1,0:T(8,128)(2,1)S(1)}, u32[]{:S(2)}, u32[]{:S(2)}) collective-permute-start(bf16[128,768]{1,0:T(8,128)(2,1)S(1)} %get-tuple-element.28), channel_id=1, source_target_pairs={{0,4},{1,5},{2,6},{3,7},{4,0},{5,1},{6,2},{7,3},{8,12},{9,13},{10,... | collective-permute-start | bytes 589832 | tf_op jit(solution)/shard_map/ppermute | solution.py:469
  122.6 8.9 %collective-permute-start.3 = (bf16[128,768]{1,0:T(8,128)(2,1)S(1)}, bf16[128,768]{1,0:T(8,128)(2,1)S(1)}, u32[]{:S(2)}, u32[]{:S(2)}) collective-permute-start(bf16[128,768]{1,0:T(8,128)(2,1)S(1)} %get-tuple-element.29), channel_id=1, source_target_pairs={{0,6},{1,7},{2,0},{3,1},{4,2},{5,3},{6,4},{7,5},{8,14},{9,15},{10,... | collective-permute-start | bytes 589832 | tf_op jit(solution)/shard_map/ppermute | solution.py:469
  131.6 0.7 copy-start.6
  132.3 13.9 %all-to-all-start.3 = ((bf16[16,48,128]{2,1,0:T(8,128)(2,1)}), bf16[16,48,128]{2,1,0:T(8,128)(2,1)}, u32[]{:S(2)}, u32[]{:S(2)}) async-start(bf16[16,48,128]{2,1,0:T(8,128)(2,1)} %bitcast.12), calls=%async_computation.3 | async-start | bytes 393216 | tf_op jit(solution)/shard_map/all_to_all | solution.py:475
  139.2 1.3 copy-start.2
  140.5 1.0 copy-start.4
Sparse Core Ops, SparseCore 0:
  10.2 91.0 all-gather.2

commit v7 on v5

--- a/solution.py
+++ b/solution.py
@@ -14,7 +14,7 @@
 BF16 = jnp.bfloat16
 SCALE = HD ** (-0.5)
 NB = 4
-HEADS_STEP = 4
+HEADS_STEP = 6
 
 
 def slot_of(head):
@@ -252,9 +252,9 @@
 
 def weigh_body(core_ref, res_ref, x_ref, back_ref, cot_ref, mine_ref, theirs_ref, acc, out_acc):
     step = pl.program_id(0)
-    part = jnp.dot(res_ref[0], x_ref[0], preferred_element_type=F32)
-    for i in range(1, res_ref.shape[0]):
-        part += jnp.dot(res_ref[i], x_ref[i], preferred_element_type=F32)
+    grads = jnp.concatenate([res_ref[i] for i in range(res_ref.shape[0])], axis=1)
+    tokens = x_ref[...].reshape(-1, x_ref.shape[2])
+    part = jnp.dot(grads, tokens, preferred_element_type=F32)
 
     @pl.when(step == 0)
     def _():
@@ -297,11 +297,11 @@
     whole = pl.BlockSpec(memory_space=pltpu.VMEM)
     return pl.pallas_call(
         weigh_body,
-        grid=(blocks // 4,),
+        grid=(blocks // 8,),
         in_specs=[
             pl.BlockSpec(memory_space=pltpu.SMEM),
-            pl.BlockSpec((4, wide, tok), lambda i: (i, 0, 0)),
-            pl.BlockSpec((4, tok, width), lambda i: (i, 0, 0)),
+            pl.BlockSpec((8, wide, tok), lambda i: (i, 0, 0)),
+            pl.BlockSpec((8, tok, width), lambda i: (i, 0, 0)),
             whole,
             whole,
         ],

time: 167 us -> 165 us (0.988)
  transfers between devices with their start and end apart: 9 -> 9, of which waited for: 6 -> 6; matrix products, arithmetic and copies ran while one was open for 0% -> 0% of each run, Pallas kernels for 29% -> 28%
where the time goes in v7:
time: 165 us; the launch traced here: 164 us
  Pallas kernels  48.7 us (30%)
  waiting for transfers between devices  47.7 us (29%)
  starting transfers between devices  32.2 us (20%)
  blocking collectives  15.3 us (9%)
  between operations  14.2 us (9%)
  local copies, waits for them, and re-layouts  6.13 us (4%)
    all_to_all x1, waiting for transfers between devices, shards(): lax.all_to_all(sent, 'seq', split_axis=0, concat_axis=0, tiled=True)  33.5 us
    pallas_call x1, Pallas kernels, backward(): pl.pallas_call(backward_body, grid=(blocks // NB,), in_specs=[pl.BlockSpe...  16.8 us
    all_gather x1, blocking collectives, shards(): lax.all_gather(collect(spread), 'slide', axis=0)  15.3 us
    pallas_call x1, Pallas kernels, forward(): pl.pallas_call(forward_body, grid=(blocks // NB,), in_specs=[pl.BlockSpec...  13.1 us
    all_to_all x1, starting transfers between devices, shards(): lax.all_to_all(sent, 'seq', split_axis=0, concat_axis=0, tiled=True)  8.59 us
    ppermute x3, waiting for transfers between devices, shards(): lax.ppermute(send, 'slide', [(i, (i + 2 * k) % slides) for i in range(sli...  7.69 us
    all_to_all x1, starting transfers between devices, shards(): lax.all_to_all(piece, 'seq', split_axis=0, concat_axis=0, tiled=True)  6.92 us
    all_to_all x1, starting transfers between devices, shards(): lax.all_to_all(results, 'seq', split_axis=0, concat_axis=0, tiled=True)  6.74 us
  transfers between devices with their start and end apart: 9, of which 6 were waited for; matrix products, arithmetic and copies ran while one was open for 0% of the time, Pallas kernels for 28%

profile of v7, /device:TPU:1, one launch (start us, length us, event | category | flops | bytes accessed | tf_op | source)
XLA Modules:
  0.0 164.3 jit_solution(13982997692114697719)
XLA Ops:
  7.2 0.0 copy-start
  7.2 0.0 all-gather.3.cloned.1.call-start
  7.2 0.7 all-gather.3.cloned.1.call-update
  7.9 5.3 %project.1 = bf16[16,256,256]{2,1,0:T(8,128)(2,1)} custom-call(bf16[256,768]{1,0:T(8,128)(2,1)} %bitcast.15, bf16[256,768]{1,0:T(8,128)(2,1)} %bitcast.13, bf16[768,2304]{1,0:T(8,128)(2,1)} %w_ref.1, bf16[768,2304]{1,0:T(8,128)(2,1)} %w_ref.1, bf16[768,2304]{1,0:T(8,128)(2,1)} %w_ref.1, bf16[768,768]{1,0:T(8,128)(2,1)} %wo_ref.3), custom_call_target="tpu_custom_call" | custom-call | flops 1207959552 | bytes 8388608 | tf_op jit(solution)/shard_map/project/pallas_call | solution.py:58
  13.2 8.6 %all-to-all-start = ((bf16[16,256,256]{2,1,0:T(8,128)(2,1)}), bf16[16,256,256]{2,1,0:T(8,128)(2,1)S(1)}, u32[]{:S(2)}, u32[]{:S(2)}) async-start(bf16[16,256,256]{2,1,0:T(8,128)(2,1)} %project.1), calls=%async_computation | async-start | bytes 4194304 | tf_op jit(solution)/shard_map/all_to_all | solution.py:462
  21.9 0.0 copy-done
  21.9 0.7 copy.13.tiles_ref
  22.6 33.5 %all-to-all-done.in_ref = bf16[16,256,256]{2,1,0:T(8,128)(2,1)S(1)} async-done(((bf16[16,256,256]{2,1,0:T(8,128)(2,1)}), bf16[16,256,256]{2,1,0:T(8,128)(2,1)S(1)}, u32[]{:S(2)}, u32[]{:S(2)}) %all-to-all-start) | async-done | bytes 2097184 | tf_op jit(solution)/shard_map/all_to_all | solution.py:462
  56.1 0.0 copy-start.7
  56.1 1.3 copy-done.7
  57.4 13.1 %forward.1 = (bf16[16,64,256]{2,1,0:T(8,128)(2,1)}, bf16[16,1280,256]{2,1,0:T(8,128)(2,1)}, f32[16,8,256]{2,1,0:T(8,128)}) custom-call(s32[16,8]{1,0:T(8,128)} %copy.13.tiles_ref, s32[32]{0:T(128)} %bitcast.18, bf16[16,256,256]{2,1,0:T(8,128)(2,1)} %copy-done.7), custom_call_target="tpu_custom_call" | custom-call | flops 5368709120 | bytes 14680064 | tf_op jit(solution)/shard_map/forward/pallas_call | solution.py:132
  70.5 3.9 %all-to-all-start.1 = ((bf16[16,64,256]{2,1,0:T(8,128)(2,1)}), bf16[16,64,256]{2,1,0:T(8,128)(2,1)S(1)}, u32[]{:S(2)}, u32[]{:S(2)}) async-start(bf16[16,64,256]{2,1,0:T(8,128)(2,1)} %get-tuple-element.21), calls=%async_computation.1 | async-start | bytes 1048576 | tf_op jit(solution)/shard_map/all_to_all | solution.py:465
  74.4 16.8 %backward.1.res_ref = bf16[16,192,256]{2,1,0:T(8,128)(2,1)} custom-call(s32[16,8]{1,0:T(8,128)} %copy.13.tiles_ref, bf16[16,256,256]{2,1,0:T(8,128)(2,1)} %copy-done.7, bf16[16,1280,256]{2,1,0:T(8,128)(2,1)} %get-tuple-element.19.exp_ref, f32[16,8,256]{2,1,0:T(8,128)} %get-tuple-element.20.stat_ref), custom_call_target="tpu_custom_call" | custom-call | flops 10737418240 | bytes 16777216 | tf_op jit(solution)/shard_map/backward/pallas_call | solution.py:227
  91.2 0.0 all-to-all-done.1.back_ref.att_ref
  91.2 0.0 copy-start.3
  91.2 6.7 %all-to-all-start.2 = ((bf16[16,192,256]{2,1,0:T(8,128)(2,1)}), bf16[16,192,256]{2,1,0:T(8,128)(2,1)}, u32[]{:S(2)}, u32[]{:S(2)}) async-start(bf16[16,192,256]{2,1,0:T(8,128)(2,1)} %backward.1.res_ref), calls=%async_computation.2 | async-start | bytes 3145728 | tf_op jit(solution)/shard_map/all_to_all | solution.py:467
  98.0 2.7 %all-gather.3.cloned.1.call-done.x_ref = bf16[16,256,768]{2,1,0:T(8,128)(2,1)} async-done(((bf16[1,256,768]{2,1,0:T(8,128)(2,1)}), bf16[16,256,768]{2,1,0:T(8,128)(2,1)}) %all-gather.3.cloned.1.call-update) | async-done | bytes 6291472 | tf_op jit(solution)/shard_map/all_gather | solution.py:460
  100.6 0.0 copy-done.3
  100.6 0.0 copy-start.1
  100.6 6.0 %weigh.1 = (bf16[4,128,768]{2,1,0:T(8,128)(2,1)}, bf16[4,128,768]{2,1,0:T(8,128)(2,1)}) custom-call(s32[1]{0:T(128)} %bitcast.1.core_ref, bf16[16,192,256]{2,1,0:T(8,128)(2,1)} %backward.1.res_ref, bf16[16,256,768]{2,1,0:T(8,128)(2,1)} %all-gather.3.cloned.1.call-done.x_ref, bf16[16,64,256]{2,1,0:T(8,128)(2,1)} %copy-done.3, bf16[256,768]{1,0:T(8,128)(2,1)} %bitcast.14), custom_call_target="tpu_custom_call" | custom-call | flops 1207959552 | bytes 10485760 | tf_op jit(solution)/shard_map/weigh/pallas_call | solution.py:298
  106.6 1.1 collective-permute-start
  107.7 2.3 %collective-permute-done.got_ref = bf16[4,128,768]{2,1,0:T(8,128)(2,1)} collective-permute-done((bf16[4,128,768]{2,1,0:T(8,128)(2,1)}, bf16[4,128,768]{2,1,0:T(8,128)(2,1)}, u32[]{:S(2)}, u32[]{:S(2)}) %collective-permute-start) | collective-permute-done | bytes 786464 | tf_op jit(solution)/shard_map/ppermute | solution.py:469
  110.0 0.0 copy-start.5
  110.0 1.1 copy-done.5
  111.1 1.3 merge.1
  112.4 1.3 collective-permute-start.1
  113.7 2.5 %collective-permute-start.2 = (bf16[128,768]{1,0:T(8,128)(2,1)S(1)}, bf16[128,768]{1,0:T(8,128)(2,1)S(1)}, u32[]{:S(2)}, u32[]{:S(2)}) collective-permute-start(bf16[128,768]{1,0:T(8,128)(2,1)S(1)} %get-tuple-element.26), channel_id=1, source_target_pairs={{0,4},{1,5},{2,6},{3,7},{4,0},{5,1},{6,2},{7,3},{8,12},{9,13},{10,... | collective-permute-start | bytes 589832 | tf_op jit(solution)/shard_map/ppermute | solution.py:472
  116.2 1.2 collective-permute-start.3
  117.3 2.6 %collective-permute-done.1.b_ref = bf16[128,768]{1,0:T(8,128)(2,1)S(1)} collective-permute-done((bf16[128,768]{1,0:T(8,128)(2,1)S(1)}, bf16[128,768]{1,0:T(8,128)(2,1)S(1)}, u32[]{:S(2)}, u32[]{:S(2)}) %collective-permute-start.1) | collective-permute-done | bytes 196640 | tf_op jit(solution)/shard_map/ppermute | solution.py:472
  119.9 5.1 %collective-permute-done.2.c_ref = bf16[128,768]{1,0:T(8,128)(2,1)S(1)} collective-permute-done((bf16[128,768]{1,0:T(8,128)(2,1)S(1)}, bf16[128,768]{1,0:T(8,128)(2,1)S(1)}, u32[]{:S(2)}, u32[]{:S(2)}) %collective-permute-start.2) | collective-permute-done | bytes 196640 | tf_op jit(solution)/shard_map/ppermute | solution.py:472
  125.0 0.0 collective-permute-done.3.d_ref
  125.0 0.2 fold.1
  125.2 0.0 copy-start.6
  125.2 0.7 copy-done.6
  125.9 0.0 all-to-all-done.2.back_ref
  125.9 6.9 %all-to-all-start.3 = ((bf16[16,48,128]{2,1,0:T(8,128)(2,1)}), bf16[16,48,128]{2,1,0:T(8,128)(2,1)}, u32[]{:S(2)}, u32[]{:S(2)}) async-start(bf16[16,48,128]{2,1,0:T(8,128)(2,1)} %bitcast.12), calls=%async_computation.3 | async-start | bytes 393216 | tf_op jit(solution)/shard_map/all_to_all | solution.py:478
  132.8 0.0 copy-done.1
  132.8 0.0 copy-start.2
  132.8 1.3 copy-done.2
  134.1 0.0 copy-start.4
  134.1 1.0 copy-done.4
  135.1 3.7 %close.1 = (bf16[256,768]{1,0:T(8,128)(2,1)}, bf16[256,768]{1,0:T(8,128)(2,1)}) custom-call(bf16[16,192,256]{2,1,0:T(8,128)(2,1)} %all-to-all-done.2.back_ref, bf16[16,64,256]{2,1,0:T(8,128)(2,1)S(1)} %copy-done.4, bf16[768,2304]{1,0:T(8,128)(2,1)S(1)} %copy-done.1, bf16[768,768]{1,0:T(8,128)(2,1)S(1)} %copy-done.2), custom_call_target="tpu_custom_call" | custom-call | flops 1207959552 | bytes 8388608 | tf_op jit(solution)/shard_map/close/pallas_call | solution.py:439
  138.8 1.0 all-to-all-done.3.spread_ref
  139.8 1.0 collect.1
  140.8 15.3 %all-gather = bf16[384,384]{1,0:T(8,128)(2,1)S(1)} all-gather(bf16[48,384]{1,0:T(8,128)(2,1)S(1)} %collect.1), channel_id=2, replica_groups=mesh['seq'=16,'slide'=8] {'slide'}, dimensions={0}, use_global_device_ids=true | all-gather | bytes 331776 | tf_op jit(solution)/shard_map/all_gather | solution.py:479
  156.2 1.3 settle.1
  (1 shorter events, 0.0 us)
Async XLA Ops:
  7.2 14.7 %copy-start = (s32[1,4,16,8]{2,3,1,0:T(8,128)S(1)}, s32[1,4,16,8]{2,3,1,0:T(8,128)}, u32[]{:S(2)}) copy-start(s32[1,4,16,8]{2,3,1,0:T(8,128)} %param.8) | copy-start | bytes 6148
  7.2 93.4 %all-gather.3.cloned.1.call-start = ((), (), s32[]{:S(2)}) async-start(), calls=%async_computation.4 | async-start | bytes 6684672 | tf_op jit(solution)/shard_map/all_gather | solution.py:460
  13.2 42.8 %all-to-all-start = ((bf16[16,256,256]{2,1,0:T(8,128)(2,1)}), bf16[16,256,256]{2,1,0:T(8,128)(2,1)S(1)}, u32[]{:S(2)}, u32[]{:S(2)}) async-start(bf16[16,256,256]{2,1,0:T(8,128)(2,1)} %project.1), calls=%async_computation | async-start | bytes 4194304 | tf_op jit(solution)/shard_map/all_to_all | solution.py:462
  56.1 1.3 copy-start.7
  70.5 20.7 %all-to-all-start.1 = ((bf16[16,64,256]{2,1,0:T(8,128)(2,1)}), bf16[16,64,256]{2,1,0:T(8,128)(2,1)S(1)}, u32[]{:S(2)}, u32[]{:S(2)}) async-start(bf16[16,64,256]{2,1,0:T(8,128)(2,1)} %get-tuple-element.21), calls=%async_computation.1 | async-start | bytes 1048576 | tf_op jit(solution)/shard_map/all_to_all | solution.py:465
  91.2 9.4 %copy-start.3 = (bf16[16,64,256]{2,1,0:T(8,128)(2,1)}, bf16[16,64,256]{2,1,0:T(8,128)(2,1)S(1)}, u32[]{:S(2)}) copy-start(bf16[16,64,256]{2,1,0:T(8,128)(2,1)S(1)} %all-to-all-done.1.back_ref.att_ref) | copy-start | bytes 1572868
  91.2 34.6 %all-to-all-start.2 = ((bf16[16,192,256]{2,1,0:T(8,128)(2,1)}), bf16[16,192,256]{2,1,0:T(8,128)(2,1)}, u32[]{:S(2)}, u32[]{:S(2)}) async-start(bf16[16,192,256]{2,1,0:T(8,128)(2,1)} %backward.1.res_ref), calls=%async_computation.2 | async-start | bytes 3145728 | tf_op jit(solution)/shard_map/all_to_all | solution.py:467
  100.6 32.2 %copy-start.1 = (bf16[768,2304]{1,0:T(8,128)(2,1)S(1)}, bf16[768,2304]{1,0:T(8,128)(2,1)}, u32[]{:S(2)}) copy-start(bf16[768,2304]{1,0:T(8,128)(2,1)} %w_ref.1) | copy-start | bytes 10616836
  106.6 3.3 %collective-permute-start = (bf16[4,128,768]{2,1,0:T(8,128)(2,1)}, bf16[4,128,768]{2,1,0:T(8,128)(2,1)}, u32[]{:S(2)}, u32[]{:S(2)}) collective-permute-start(bf16[4,128,768]{2,1,0:T(8,128)(2,1)} %get-tuple-element.23), channel_id=1, source_target_pairs={{0,1},{1,0},{2,3},{3,2},{4,5},{5,4},{6,7},{7,6},{8,9},{9,8},{10,11... | collective-permute-start | bytes 2359304 | tf_op jit(solution)/shard_map/ppermute | solution.py:469
  110.0 1.1 copy-start.5
  112.4 7.5 %collective-permute-start.1 = (bf16[128,768]{1,0:T(8,128)(2,1)S(1)}, bf16[128,768]{1,0:T(8,128)(2,1)S(1)}, u32[]{:S(2)}, u32[]{:S(2)}) collective-permute-start(bf16[128,768]{1,0:T(8,128)(2,1)S(1)} %get-tuple-element.25), channel_id=1, source_target_pairs={{0,2},{1,3},{2,4},{3,5},{4,6},{5,7},{6,0},{7,1},{8,10},{9,11},{10,... | collective-permute-start | bytes 589832 | tf_op jit(solution)/shard_map/ppermute | solution.py:472
  113.7 11.3 %collective-permute-start.2 = (bf16[128,768]{1,0:T(8,128)(2,1)S(1)}, bf16[128,768]{1,0:T(8,128)(2,1)S(1)}, u32[]{:S(2)}, u32[]{:S(2)}) collective-permute-start(bf16[128,768]{1,0:T(8,128)(2,1)S(1)} %get-tuple-element.26), channel_id=1, source_target_pairs={{0,4},{1,5},{2,6},{3,7},{4,0},{5,1},{6,2},{7,3},{8,12},{9,13},{10,... | collective-permute-start | bytes 589832 | tf_op jit(solution)/shard_map/ppermute | solution.py:472
  116.2 8.9 %collective-permute-start.3 = (bf16[128,768]{1,0:T(8,128)(2,1)S(1)}, bf16[128,768]{1,0:T(8,128)(2,1)S(1)}, u32[]{:S(2)}, u32[]{:S(2)}) collective-permute-start(bf16[128,768]{1,0:T(8,128)(2,1)S(1)} %get-tuple-element.27), channel_id=1, source_target_pairs={{0,6},{1,7},{2,0},{3,1},{4,2},{5,3},{6,4},{7,5},{8,14},{9,15},{10,... | collective-permute-start | bytes 589832 | tf_op jit(solution)/shard_map/ppermute | solution.py:472
  125.2 0.7 copy-start.6
  125.9 13.9 %all-to-all-start.3 = ((bf16[16,48,128]{2,1,0:T(8,128)(2,1)}), bf16[16,48,128]{2,1,0:T(8,128)(2,1)}, u32[]{:S(2)}, u32[]{:S(2)}) async-start(bf16[16,48,128]{2,1,0:T(8,128)(2,1)} %bitcast.12), calls=%async_computation.3 | async-start | bytes 393216 | tf_op jit(solution)/shard_map/all_to_all | solution.py:478
  132.8 1.3 copy-start.2
  134.1 1.0 copy-start.4
Sparse Core Ops, SparseCore 0:
  10.2 90.3 all-gather.2

commit v8 on v7

--- a/solution.py
+++ b/solution.py
@@ -147,7 +147,7 @@
             pltpu.VMEM((total, TILE, 2 * HD), BF16),
             pltpu.VMEM((total, HD, TILE), BF16),
         ],
-        compiler_params=pltpu.CompilerParams(vmem_limit_bytes=60 * 2**20),
+        compiler_params=pltpu.CompilerParams(vmem_limit_bytes=50 * 2**20),
         cost_estimate=pl.CostEstimate(
             flops=blocks * 4 * 2 * tok * slots * 2 * HD,
             bytes_accessed=14 * 2**20,
@@ -240,7 +240,7 @@
             pltpu.VMEM((total, HD, TILE), BF16),
             pltpu.VMEM((total, TILE, 2 * HD), F32),
         ],
-        compiler_params=pltpu.CompilerParams(vmem_limit_bytes=60 * 2**20),
+        compiler_params=pltpu.CompilerParams(vmem_limit_bytes=56 * 2**20),
         cost_estimate=pl.CostEstimate(
             flops=blocks * 8 * 2 * tok * slots * 2 * HD,
             bytes_accessed=16 * 2**20,
@@ -250,7 +250,50 @@
     )(tiles, arrived, low, stats)
 
 
-def weigh_body(core_ref, res_ref, x_ref, back_ref, cot_ref, mine_ref, theirs_ref, acc, out_acc):
+def by_core(core, refs, write):
+    mine, theirs = refs
+
+    @pl.when(core == 0)
+    def _():
+        for k in range(4):
+            write(mine, k, 2 * k)
+            write(theirs, k, 2 * k + 1)
+
+    @pl.when(core != 0)
+    def _():
+        for k in range(4):
+            write(mine, k, 2 * k + 1)
+            write(theirs, k, 2 * k)
+
+
+def outer_body(core_ref, back_ref, cot_ref, mine_ref, theirs_ref):
+    attended = jnp.concatenate([back_ref[slot_of(h)] for h in range(H)], axis=0).T
+    total = jnp.dot(cot_ref[...].T, attended, preferred_element_type=F32).astype(BF16)
+    cols = mine_ref.shape[1]
+
+    def write(ref, slot, k):
+        ref[slot] = total[k * cols : (k + 1) * cols]
+
+    by_core(core_ref[0], (mine_ref, theirs_ref), write)
+
+
+def outer(core, att_back, cot):
+    tok, width = cot.shape
+    whole = pl.BlockSpec(memory_space=pltpu.VMEM)
+    return pl.pallas_call(
+        outer_body,
+        in_specs=[pl.BlockSpec(memory_space=pltpu.SMEM), whole, whole],
+        out_specs=[whole, whole],
+        out_shape=[jax.ShapeDtypeStruct((4, width // 8, width), BF16)] * 2,
+        compiler_params=pltpu.CompilerParams(vmem_limit_bytes=24 * 2**20),
+        cost_estimate=pl.CostEstimate(
+            flops=2 * tok * width * width, bytes_accessed=2 * 2**20, transcendentals=0
+        ),
+        name="outer",
+    )(core, att_back, cot)
+
+
+def weigh_body(core_ref, res_ref, x_ref, mine_ref, theirs_ref, acc):
     step = pl.program_id(0)
     grads = jnp.concatenate([res_ref[i] for i in range(res_ref.shape[0])], axis=1)
     tokens = x_ref[...].reshape(-1, x_ref.shape[2])
@@ -258,8 +301,6 @@
 
     @pl.when(step == 0)
     def _():
-        attended = jnp.concatenate([back_ref[slot_of(h)] for h in range(H)], axis=0).T
-        out_acc[...] = jnp.dot(cot_ref[...].T, attended, preferred_element_type=F32).astype(BF16)
         acc[...] = part
 
     @pl.when(step > 0)
@@ -268,30 +309,16 @@
 
     @pl.when(step == pl.num_programs(0) - 1)
     def _():
-        out_cols = out_acc.shape[0] // 8
-        in_cols = acc.shape[0] // 8
-        fill = jnp.zeros((128 - out_cols - in_cols, acc.shape[1]), F32)
-
-        def place(ref, slot, k):
-            ref[slot, :out_cols, :] = out_acc[k * out_cols : (k + 1) * out_cols]
-            ref[slot, out_cols:, :] = jnp.concatenate(
-                [acc[k * in_cols : (k + 1) * in_cols], fill], axis=0
-            ).astype(BF16)
-
-        @pl.when(core_ref[0] == 0)
-        def _():
-            for k in range(4):
-                place(mine_ref, k, 2 * k)
-                place(theirs_ref, k, 2 * k + 1)
-
-        @pl.when(core_ref[0] != 0)
-        def _():
-            for k in range(4):
-                place(mine_ref, k, 2 * k + 1)
-                place(theirs_ref, k, 2 * k)
-
-
-def weigh(core, results, x_all, att_back, cot):
+        cols = acc.shape[0] // 8
+        fill = jnp.zeros((mine_ref.shape[1] - cols, acc.shape[1]), F32)
+
+        def write(ref, slot, k):
+            ref[slot] = jnp.concatenate([acc[k * cols : (k + 1) * cols], fill], axis=0).astype(BF16)
+
+        by_core(core_ref[0], (mine_ref, theirs_ref), write)
+
+
+def weigh(core, results, x_all):
     blocks, wide, tok = results.shape
     width = x_all.shape[2]
     whole = pl.BlockSpec(memory_space=pltpu.VMEM)
@@ -302,39 +329,44 @@
             pl.BlockSpec(memory_space=pltpu.SMEM),
             pl.BlockSpec((8, wide, tok), lambda i: (i, 0, 0)),
             pl.BlockSpec((8, tok, width), lambda i: (i, 0, 0)),
-            whole,
-            whole,
         ],
         out_specs=[whole, whole],
-        out_shape=[jax.ShapeDtypeStruct((4, 128, width), BF16)] * 2,
-        scratch_shapes=[pltpu.VMEM((wide, width), F32), pltpu.VMEM((width, width), BF16)],
-        compiler_params=pltpu.CompilerParams(vmem_limit_bytes=60 * 2**20),
+        out_shape=[jax.ShapeDtypeStruct((4, 32, width), BF16)] * 2,
+        scratch_shapes=[pltpu.VMEM((wide, width), F32)],
+        compiler_params=pltpu.CompilerParams(vmem_limit_bytes=58 * 2**20),
         cost_estimate=pl.CostEstimate(
             flops=2 * blocks * tok * width * wide,
-            bytes_accessed=10 * 2**20,
+            bytes_accessed=8 * 2**20,
             transcendentals=0,
         ),
         name="weigh",
-    )(core, results, x_all, att_back, cot)
-
-
-def merge_body(chip_ref, mine_ref, got_ref, *outs):
+    )(core, results, x_all)
+
+
+def merge_body(chip_ref, mine_out_ref, got_out_ref, mine_in_ref, got_in_ref, *outs):
+    rows = mine_out_ref.shape[1]
     for k, out in enumerate(outs):
         place = lax.rem(chip_ref[0] + k, 4)
-        out[...] = (mine_ref[place].astype(F32) + got_ref[place].astype(F32)).astype(BF16)
-
-
-def merge(chip, mine, got):
-    whole = pl.BlockSpec(memory_space=pltpu.VMEM)
+        out[:rows, :] = (
+            mine_out_ref[place].astype(F32) + got_out_ref[place].astype(F32)
+        ).astype(BF16)
+        out[rows:, :] = (mine_in_ref[place].astype(F32) + got_in_ref[place].astype(F32)).astype(
+            BF16
+        )
+
+
+def merge(chip, *parts):
+    whole = pl.BlockSpec(memory_space=pltpu.VMEM)
+    shape = (parts[0].shape[1] + parts[2].shape[1], parts[0].shape[2])
     return pl.pallas_call(
         merge_body,
-        in_specs=[pl.BlockSpec(memory_space=pltpu.SMEM), whole, whole],
+        in_specs=[pl.BlockSpec(memory_space=pltpu.SMEM)] + [whole] * 4,
         out_specs=[whole] * 4,
-        out_shape=[jax.ShapeDtypeStruct(mine.shape[1:], BF16)] * 4,
+        out_shape=[jax.ShapeDtypeStruct(shape, BF16)] * 4,
         compiler_params=pltpu.CompilerParams(vmem_limit_bytes=16 * 2**20),
         cost_estimate=pl.CostEstimate(flops=10**6, bytes_accessed=2 * 10**6, transcendentals=0),
         name="merge",
-    )(chip, mine, got)
+    )(chip, *parts)
 
 
 def fold_body(a_ref, b_ref, c_ref, d_ref, out_ref):
@@ -465,9 +497,16 @@
     att_back = lax.all_to_all(att_sent, "seq", split_axis=0, concat_axis=0, tiled=True)
     results = backward(group_tiles, arrived, low, stats)
     back = lax.all_to_all(results, "seq", split_axis=0, concat_axis=0, tiled=True)
-    mine, theirs = weigh(lax.rem(slide, 2)[None], results, x_all, att_back, cot)
-    got = lax.ppermute(theirs, "slide", [(i, i ^ 1) for i in range(slides)])
-    keep, *sends = merge((slide // 2)[None], mine, got)
+    core = lax.rem(slide, 2)[None]
+
+    def swap(value):
+        return lax.ppermute(value, "slide", [(i, i ^ 1) for i in range(slides)])
+
+    mine_out, theirs_out = outer(core, att_back, cot)
+    got_out = swap(theirs_out)
+    mine_in, theirs_in = weigh(core, results, x_all)
+    got_in = swap(theirs_in)
+    keep, *sends = merge((slide // 2)[None], mine_out, got_out, mine_in, got_in)
     takes = [
         lax.ppermute(send, "slide", [(i, (i + 2 * k) % slides) for i in range(slides)])
         for k, send in zip((1, 2, 3), sends)

time: 165 us -> 166 us (level)
  starting transfers between devices: 32.2 us -> 35 us
  waiting for transfers between devices: 47.7 us -> 45.6 us
    all_gather x1, waiting for transfers between devices: 2.67 us -> 0.01 us  [shards(): x_all = lax.all_gather(x, 'seq', axis=0)]
    ppermute x1 -> x2, starting transfers between devices: 1.05 us -> 3.72 us  [swap(): return lax.ppermute(value, 'slide', [(i, i ^ 1) for i in range(slides)])]
    unnamed x16 -> x28, local copies, waits for them, and re-layouts: 5.46 us -> 6.5 us
  transfers between devices with their start and end apart: 9 -> 10, of which waited for: 6 -> 5; matrix products, arithmetic and copies ran while one was open for 0% -> 0% of each run, Pallas kernels for 28% -> 28%
where the time goes in v8:
time: 166 us; the launch traced here: 165 us
  Pallas kernels  48.6 us (29%)
  waiting for transfers between devices  45.6 us (27%)
  starting transfers between devices  35 us (21%)
  blocking collectives  15.1 us (9%)
  between operations  14.2 us (9%)
  local copies, waits for them, and re-layouts  6.58 us (4%)
    all_to_all x1, waiting for transfers between devices, shards(): lax.all_to_all(sent, 'seq', split_axis=0, concat_axis=0, tiled=True)  34.1 us
    pallas_call x1, Pallas kernels, backward(): pl.pallas_call(backward_body, grid=(blocks // NB,), in_specs=[pl.BlockSpe...  16.8 us
    all_gather x1, blocking collectives, shards(): lax.all_gather(collect(spread), 'slide', axis=0)  15.1 us
    pallas_call x1, Pallas kernels, forward(): pl.pallas_call(forward_body, grid=(blocks // NB,), in_specs=[pl.BlockSpec...  12.4 us
    all_to_all x1, starting transfers between devices, shards(): lax.all_to_all(sent, 'seq', split_axis=0, concat_axis=0, tiled=True)  8.73 us
    ppermute x3, waiting for transfers between devices, shards(): lax.ppermute(send, 'slide', [(i, (i + 2 * k) % slides) for i in range(sli...  7.95 us
    all_to_all x1, starting transfers between devices, shards(): lax.all_to_all(piece, 'seq', split_axis=0, concat_axis=0, tiled=True)  6.93 us
    all_to_all x1, starting transfers between devices, shards(): lax.all_to_all(results, 'seq', split_axis=0, concat_axis=0, tiled=True)  6.82 us
  transfers between devices with their start and end apart: 10, of which 5 were waited for; matrix products, arithmetic and copies ran while one was open for 0% of the time, Pallas kernels for 28%

profile of v8, /device:TPU:1, one launch (start us, length us, event | category | flops | bytes accessed | tf_op | source)
XLA Modules:
  0.0 165.0 jit_solution(9972270338717646480)
XLA Ops:
  7.2 0.0 copy-start
  7.2 0.0 all-gather.3.cloned.1.call-start
  7.2 0.7 all-gather.3.cloned.1.call-update
  7.9 5.3 %project.1 = bf16[16,256,256]{2,1,0:T(8,128)(2,1)} custom-call(bf16[256,768]{1,0:T(8,128)(2,1)} %bitcast.16, bf16[256,768]{1,0:T(8,128)(2,1)} %bitcast.13, bf16[768,2304]{1,0:T(8,128)(2,1)} %w_ref.1, bf16[768,2304]{1,0:T(8,128)(2,1)} %w_ref.1, bf16[768,2304]{1,0:T(8,128)(2,1)} %w_ref.1, bf16[768,768]{1,0:T(8,128)(2,1)} %wo_ref.3), custom_call_target="tpu_custom_call" | custom-call | flops 1207959552 | bytes 8388608 | tf_op jit(solution)/shard_map/project/pallas_call | solution.py:58
  13.3 0.0 copy-start.12
  13.3 8.7 %all-to-all-start = ((bf16[16,256,256]{2,1,0:T(8,128)(2,1)}), bf16[16,256,256]{2,1,0:T(8,128)(2,1)S(1)}, u32[]{:S(2)}, u32[]{:S(2)}) async-start(bf16[16,256,256]{2,1,0:T(8,128)(2,1)} %project.1), calls=%async_computation | async-start | bytes 4194304 | tf_op jit(solution)/shard_map/all_to_all | solution.py:494
  22.0 0.0 copy-done
  22.0 0.1 copy.12.tiles_ref
  22.1 0.0 copy-start.11
  22.1 34.1 %all-to-all-done.in_ref = bf16[16,256,256]{2,1,0:T(8,128)(2,1)S(1)} async-done(((bf16[16,256,256]{2,1,0:T(8,128)(2,1)}), bf16[16,256,256]{2,1,0:T(8,128)(2,1)S(1)}, u32[]{:S(2)}, u32[]{:S(2)}) %all-to-all-start) | async-done | bytes 2097184 | tf_op jit(solution)/shard_map/all_to_all | solution.py:494
  56.3 0.0 copy-start.3
  56.3 0.0 copy-done.12
  56.3 12.4 %forward.1 = (bf16[16,64,256]{2,1,0:T(8,128)(2,1)}, bf16[16,1280,256]{2,1,0:T(8,128)(2,1)}, f32[16,8,256]{2,1,0:T(8,128)S(1)}) custom-call(s32[16,8]{1,0:T(8,128)S(1)} %copy.12.tiles_ref, s32[32]{0:T(128)S(1)} %bitcast.15, bf16[16,256,256]{2,1,0:T(8,128)(2,1)S(1)} %all-to-all-done.in_ref), custom_call_target="tpu_custom_call" | custom-call | flops 5368709120 | bytes 14680064 | tf_op jit(solution)/shard_map/forward/pallas_call | solution.py:132
  68.7 0.0 copy-done.11
  68.7 0.0 copy-done.3
  68.7 0.0 copy-start.13
  68.7 0.6 copy-done.13
  69.3 3.9 %all-to-all-start.1 = ((bf16[16,64,256]{2,1,0:T(8,128)(2,1)}), bf16[16,64,256]{2,1,0:T(8,128)(2,1)S(1)}, u32[]{:S(2)}, u32[]{:S(2)}) async-start(bf16[16,64,256]{2,1,0:T(8,128)(2,1)} %get-tuple-element.21), calls=%async_computation.1 | async-start | bytes 1048576 | tf_op jit(solution)/shard_map/all_to_all | solution.py:497
  73.2 16.8 %backward.1.res_ref = bf16[16,192,256]{2,1,0:T(8,128)(2,1)} custom-call(s32[16,8]{1,0:T(8,128)} %copy-done.11, bf16[16,256,256]{2,1,0:T(8,128)(2,1)} %copy-done.3, bf16[16,1280,256]{2,1,0:T(8,128)(2,1)} %get-tuple-element.24.exp_ref, f32[16,8,256]{2,1,0:T(8,128)} %copy-done.13), custom_call_target="tpu_custom_call" | custom-call | flops 10737418240 | bytes 16777216 | tf_op jit(solution)/shard_map/backward/pallas_call | solution.py:227
  90.0 0.0 copy-start.9
  90.0 0.0 all-to-all-done.1.back_ref.att_ref
  90.1 0.0 copy-start.4
  90.1 6.8 %all-to-all-start.2 = ((bf16[16,192,256]{2,1,0:T(8,128)(2,1)}), bf16[16,192,256]{2,1,0:T(8,128)(2,1)}, u32[]{:S(2)}, u32[]{:S(2)}) async-start(bf16[16,192,256]{2,1,0:T(8,128)(2,1)} %backward.1.res_ref), calls=%async_computation.2 | async-start | bytes 3145728 | tf_op jit(solution)/shard_map/all_to_all | solution.py:499
  96.9 0.0 copy-done.9
  96.9 1.4 outer.1
  98.3 0.0 copy-done.4
  98.3 0.0 copy-start.7
  98.3 0.8 copy-done.7
  99.2 3.7 %collective-permute-start = (bf16[4,96,768]{2,1,0:T(8,128)(2,1)}, bf16[4,96,768]{2,1,0:T(8,128)(2,1)}, u32[]{:S(2)}, u32[]{:S(2)}) collective-permute-start(bf16[4,96,768]{2,1,0:T(8,128)(2,1)} %get-tuple-element.23), channel_id=1, source_target_pairs={{0,1},{1,0},{2,3},{3,2},{4,5},{5,4},{6,7},{7,6},{8,9},{9,8},{10,11... | collective-permute-start | bytes 1769480 | tf_op jit(solution)/shard_map/ppermute | solution.py:503
  102.9 0.0 all-gather.3.cloned.1.call-done.x_ref
  102.9 0.0 copy-start.1
  102.9 5.1 %weigh.1 = (bf16[4,32,768]{2,1,0:T(8,128)(2,1)}, bf16[4,32,768]{2,1,0:T(8,128)(2,1)}) custom-call(s32[1]{0:T(128)} %bitcast.1.core_ref, bf16[16,192,256]{2,1,0:T(8,128)(2,1)} %backward.1.res_ref, bf16[16,256,768]{2,1,0:T(8,128)(2,1)} %all-gather.3.cloned.1.call-done.x_ref), custom_call_target="tpu_custom_call" | custom-call | flops 1207959552 | bytes 8388608 | tf_op jit(solution)/shard_map/weigh/pallas_call | solution.py:325
  108.0 0.0 collective-permute-start.1
  108.0 0.0 collective-permute-done.got_out_ref
  108.0 1.8 %collective-permute-done.1.got_in_ref = bf16[4,32,768]{2,1,0:T(8,128)(2,1)} collective-permute-done((bf16[4,32,768]{2,1,0:T(8,128)(2,1)}, bf16[4,32,768]{2,1,0:T(8,128)(2,1)}, u32[]{:S(2)}, u32[]{:S(2)}) %collective-permute-start.1) | collective-permute-done | bytes 196640 | tf_op jit(solution)/shard_map/ppermute | solution.py:503
  109.8 0.0 copy-start.8
  109.8 1.1 copy-done.8
  110.8 0.0 copy-start.10
  110.8 0.9 copy-done.10
  111.8 1.3 merge.1
  113.0 1.2 collective-permute-start.2
  114.3 2.5 %collective-permute-start.3 = (bf16[128,768]{1,0:T(8,128)(2,1)S(1)}, bf16[128,768]{1,0:T(8,128)(2,1)S(1)}, u32[]{:S(2)}, u32[]{:S(2)}) collective-permute-start(bf16[128,768]{1,0:T(8,128)(2,1)S(1)} %get-tuple-element.30), channel_id=1, source_target_pairs={{0,4},{1,5},{2,6},{3,7},{4,0},{5,1},{6,2},{7,3},{8,12},{9,13},{10,... | collective-permute-start | bytes 589832 | tf_op jit(solution)/shard_map/ppermute | solution.py:511
  116.8 1.2 collective-permute-start.4
  117.9 2.7 %collective-permute-done.2.b_ref = bf16[128,768]{1,0:T(8,128)(2,1)S(1)} collective-permute-done((bf16[128,768]{1,0:T(8,128)(2,1)S(1)}, bf16[128,768]{1,0:T(8,128)(2,1)S(1)}, u32[]{:S(2)}, u32[]{:S(2)}) %collective-permute-start.2) | collective-permute-done | bytes 196640 | tf_op jit(solution)/shard_map/ppermute | solution.py:511
  120.7 5.2 %collective-permute-done.3.c_ref = bf16[128,768]{1,0:T(8,128)(2,1)S(1)} collective-permute-done((bf16[128,768]{1,0:T(8,128)(2,1)S(1)}, bf16[128,768]{1,0:T(8,128)(2,1)S(1)}, u32[]{:S(2)}, u32[]{:S(2)}) %collective-permute-start.3) | collective-permute-done | bytes 196640 | tf_op jit(solution)/shard_map/ppermute | solution.py:511
  125.9 0.0 collective-permute-done.4.d_ref
  125.9 0.2 fold.1
  126.1 0.0 copy-start.6
  126.1 0.7 copy-done.6
  126.7 0.0 all-to-all-done.2.back_ref
  126.7 6.9 %all-to-all-start.3 = ((bf16[16,48,128]{2,1,0:T(8,128)(2,1)}), bf16[16,48,128]{2,1,0:T(8,128)(2,1)}, u32[]{:S(2)}, u32[]{:S(2)}) async-start(bf16[16,48,128]{2,1,0:T(8,128)(2,1)} %bitcast.12), calls=%async_computation.3 | async-start | bytes 393216 | tf_op jit(solution)/shard_map/all_to_all | solution.py:517
  133.7 0.0 copy-done.1
  133.7 0.0 copy-start.2
  133.7 1.3 copy-done.2
  135.0 0.0 copy-start.5
  135.0 1.0 copy-done.5
  136.0 3.7 %close.1 = (bf16[256,768]{1,0:T(8,128)(2,1)}, bf16[256,768]{1,0:T(8,128)(2,1)}) custom-call(bf16[16,192,256]{2,1,0:T(8,128)(2,1)} %all-to-all-done.2.back_ref, bf16[16,64,256]{2,1,0:T(8,128)(2,1)S(1)} %copy-done.5, bf16[768,2304]{1,0:T(8,128)(2,1)S(1)} %copy-done.1, bf16[768,768]{1,0:T(8,128)(2,1)S(1)} %copy-done.2), custom_call_target="tpu_custom_call" | custom-call | flops 1207959552 | bytes 8388608 | tf_op jit(solution)/shard_map/close/pallas_call | solution.py:471
  139.7 1.0 all-to-all-done.3.spread_ref
  140.7 1.0 collect.1
  141.7 15.1 %all-gather = bf16[384,384]{1,0:T(8,128)(2,1)S(1)} all-gather(bf16[48,384]{1,0:T(8,128)(2,1)S(1)} %collect.1), channel_id=2, replica_groups=mesh['seq'=16,'slide'=8] {'slide'}, dimensions={0}, use_global_device_ids=true | all-gather | bytes 331776 | tf_op jit(solution)/shard_map/all_gather | solution.py:518
  156.9 1.3 settle.1
  (1 shorter events, 0.0 us)
Async XLA Ops:
  7.2 14.9 %copy-start = (s32[1,4,16,8]{2,3,1,0:T(8,128)S(1)}, s32[1,4,16,8]{2,3,1,0:T(8,128)}, u32[]{:S(2)}) copy-start(s32[1,4,16,8]{2,3,1,0:T(8,128)} %param.8) | copy-start | bytes 6148
  7.2 95.7 %all-gather.3.cloned.1.call-start = ((), (), s32[]{:S(2)}) async-start(), calls=%async_computation.4 | async-start | bytes 6684672 | tf_op jit(solution)/shard_map/all_gather | solution.py:492
  13.3 43.0 %copy-start.12 = (s32[1,32]{1,0:T(1,128)S(1)}, s32[1,32]{1,0:T(1,128)}, u32[]{:S(2)}) copy-start(s32[1,32]{1,0:T(1,128)} %param.9) | copy-start | bytes 388
  13.3 43.0 %all-to-all-start = ((bf16[16,256,256]{2,1,0:T(8,128)(2,1)}), bf16[16,256,256]{2,1,0:T(8,128)(2,1)S(1)}, u32[]{:S(2)}, u32[]{:S(2)}) async-start(bf16[16,256,256]{2,1,0:T(8,128)(2,1)} %project.1), calls=%async_computation | async-start | bytes 4194304 | tf_op jit(solution)/shard_map/all_to_all | solution.py:494
  22.1 46.6 %copy-start.11 = (s32[16,8]{1,0:T(8,128)}, s32[16,8]{1,0:T(8,128)S(1)}, u32[]{:S(2)}) copy-start(s32[16,8]{1,0:T(8,128)S(1)} %copy.12.tiles_ref) | copy-start | bytes 1540
  56.3 12.4 %copy-start.3 = (bf16[16,256,256]{2,1,0:T(8,128)(2,1)}, bf16[16,256,256]{2,1,0:T(8,128)(2,1)S(1)}, u32[]{:S(2)}) copy-start(bf16[16,256,256]{2,1,0:T(8,128)(2,1)S(1)} %all-to-all-done.in_ref) | copy-start | bytes 6291460
  68.7 0.7 copy-start.13
  69.3 20.7 %all-to-all-start.1 = ((bf16[16,64,256]{2,1,0:T(8,128)(2,1)}), bf16[16,64,256]{2,1,0:T(8,128)(2,1)S(1)}, u32[]{:S(2)}, u32[]{:S(2)}) async-start(bf16[16,64,256]{2,1,0:T(8,128)(2,1)} %get-tuple-element.21), calls=%async_computation.1 | async-start | bytes 1048576 | tf_op jit(solution)/shard_map/all_to_all | solution.py:497
  90.0 6.9 %copy-start.9 = (bf16[1,256,768]{2,1,0:T(8,128)(2,1)S(1)}, bf16[1,256,768]{2,1,0:T(8,128)(2,1)}, u32[]{:S(2)}) copy-start(bf16[1,256,768]{2,1,0:T(8,128)(2,1)} %param.7) | copy-start | bytes 1179652
  90.1 8.3 %copy-start.4 = (bf16[16,64,256]{2,1,0:T(8,128)(2,1)}, bf16[16,64,256]{2,1,0:T(8,128)(2,1)S(1)}, u32[]{:S(2)}) copy-start(bf16[16,64,256]{2,1,0:T(8,128)(2,1)S(1)} %all-to-all-done.1.back_ref.att_ref) | copy-start | bytes 1572868
  90.1 36.7 %all-to-all-start.2 = ((bf16[16,192,256]{2,1,0:T(8,128)(2,1)}), bf16[16,192,256]{2,1,0:T(8,128)(2,1)}, u32[]{:S(2)}, u32[]{:S(2)}) async-start(bf16[16,192,256]{2,1,0:T(8,128)(2,1)} %backward.1.res_ref), calls=%async_computation.2 | async-start | bytes 3145728 | tf_op jit(solution)/shard_map/all_to_all | solution.py:499
  98.3 0.8 copy-start.7
  99.2 8.8 %collective-permute-start = (bf16[4,96,768]{2,1,0:T(8,128)(2,1)}, bf16[4,96,768]{2,1,0:T(8,128)(2,1)}, u32[]{:S(2)}, u32[]{:S(2)}) collective-permute-start(bf16[4,96,768]{2,1,0:T(8,128)(2,1)} %get-tuple-element.23), channel_id=1, source_target_pairs={{0,1},{1,0},{2,3},{3,2},{4,5},{5,4},{6,7},{7,6},{8,9},{9,8},{10,11... | collective-permute-start | bytes 1769480 | tf_op jit(solution)/shard_map/ppermute | solution.py:503
  102.9 30.8 %copy-start.1 = (bf16[768,2304]{1,0:T(8,128)(2,1)S(1)}, bf16[768,2304]{1,0:T(8,128)(2,1)}, u32[]{:S(2)}) copy-start(bf16[768,2304]{1,0:T(8,128)(2,1)} %w_ref.1) | copy-start | bytes 10616836
  108.0 1.8 %collective-permute-start.1 = (bf16[4,32,768]{2,1,0:T(8,128)(2,1)}, bf16[4,32,768]{2,1,0:T(8,128)(2,1)}, u32[]{:S(2)}, u32[]{:S(2)}) collective-permute-start(bf16[4,32,768]{2,1,0:T(8,128)(2,1)} %get-tuple-element.27), channel_id=1, source_target_pairs={{0,1},{1,0},{2,3},{3,2},{4,5},{5,4},{6,7},{7,6},{8,9},{9,8},{10,11... | collective-permute-start | bytes 589832 | tf_op jit(solution)/shard_map/ppermute | solution.py:503
  109.8 1.1 copy-start.8
  110.8 0.9 copy-start.10
  113.0 7.6 %collective-permute-start.2 = (bf16[128,768]{1,0:T(8,128)(2,1)S(1)}, bf16[128,768]{1,0:T(8,128)(2,1)S(1)}, u32[]{:S(2)}, u32[]{:S(2)}) collective-permute-start(bf16[128,768]{1,0:T(8,128)(2,1)S(1)} %get-tuple-element.29), channel_id=1, source_target_pairs={{0,2},{1,3},{2,4},{3,5},{4,6},{5,7},{6,0},{7,1},{8,10},{9,11},{10,... | collective-permute-start | bytes 589832 | tf_op jit(solution)/shard_map/ppermute | solution.py:511
  114.3 11.6 %collective-permute-start.3 = (bf16[128,768]{1,0:T(8,128)(2,1)S(1)}, bf16[128,768]{1,0:T(8,128)(2,1)S(1)}, u32[]{:S(2)}, u32[]{:S(2)}) collective-permute-start(bf16[128,768]{1,0:T(8,128)(2,1)S(1)} %get-tuple-element.30), channel_id=1, source_target_pairs={{0,4},{1,5},{2,6},{3,7},{4,0},{5,1},{6,2},{7,3},{8,12},{9,13},{10,... | collective-permute-start | bytes 589832 | tf_op jit(solution)/shard_map/ppermute | solution.py:511
  116.8 9.1 %collective-permute-start.4 = (bf16[128,768]{1,0:T(8,128)(2,1)S(1)}, bf16[128,768]{1,0:T(8,128)(2,1)S(1)}, u32[]{:S(2)}, u32[]{:S(2)}) collective-permute-start(bf16[128,768]{1,0:T(8,128)(2,1)S(1)} %get-tuple-element.31), channel_id=1, source_target_pairs={{0,6},{1,7},{2,0},{3,1},{4,2},{5,3},{6,4},{7,5},{8,14},{9,15},{10,... | collective-permute-start | bytes 589832 | tf_op jit(solution)/shard_map/ppermute | solution.py:511
  126.1 0.7 copy-start.6
  126.7 14.0 %all-to-all-start.3 = ((bf16[16,48,128]{2,1,0:T(8,128)(2,1)}), bf16[16,48,128]{2,1,0:T(8,128)(2,1)}, u32[]{:S(2)}, u32[]{:S(2)}) async-start(bf16[16,48,128]{2,1,0:T(8,128)(2,1)} %bitcast.12), calls=%async_computation.3 | async-start | bytes 393216 | tf_op jit(solution)/shard_map/all_to_all | solution.py:517
  133.7 1.3 copy-start.2
  135.0 1.0 copy-start.5
Sparse Core Ops, SparseCore 0:
  10.2 90.6 all-gather.2

commit v9 on v8

--- a/solution.py
+++ b/solution.py
@@ -240,7 +240,7 @@
             pltpu.VMEM((total, HD, TILE), BF16),
             pltpu.VMEM((total, TILE, 2 * HD), F32),
         ],
-        compiler_params=pltpu.CompilerParams(vmem_limit_bytes=56 * 2**20),
+        compiler_params=pltpu.CompilerParams(vmem_limit_bytes=50 * 2**20),
         cost_estimate=pl.CostEstimate(
             flops=blocks * 8 * 2 * tok * slots * 2 * HD,
             bytes_accessed=16 * 2**20,
@@ -285,7 +285,7 @@
         in_specs=[pl.BlockSpec(memory_space=pltpu.SMEM), whole, whole],
         out_specs=[whole, whole],
         out_shape=[jax.ShapeDtypeStruct((4, width // 8, width), BF16)] * 2,
-        compiler_params=pltpu.CompilerParams(vmem_limit_bytes=24 * 2**20),
+        compiler_params=pltpu.CompilerParams(vmem_limit_bytes=60 * 2**20),
         cost_estimate=pl.CostEstimate(
             flops=2 * tok * width * width, bytes_accessed=2 * 2**20, transcendentals=0
         ),
@@ -343,16 +343,28 @@
     )(core, results, x_all)
 
 
-def merge_body(chip_ref, mine_out_ref, got_out_ref, mine_in_ref, got_in_ref, *outs):
-    rows = mine_out_ref.shape[1]
-    for k, out in enumerate(outs):
+def merge_body(chip_ref, *refs):
+    parts, outs, held, sems = refs[:4], refs[4:8], refs[8:12], refs[12]
+    rows = held[0].shape[1]
+    order = (2, 1, 3, 0)
+    copies = []
+    for k in order:
         place = lax.rem(chip_ref[0] + k, 4)
-        out[:rows, :] = (
-            mine_out_ref[place].astype(F32) + got_out_ref[place].astype(F32)
-        ).astype(BF16)
-        out[rows:, :] = (mine_in_ref[place].astype(F32) + got_in_ref[place].astype(F32)).astype(
-            BF16
+        copies.append(
+            [
+                pltpu.make_async_copy(part.at[place], hold.at[k], sems.at[k, i])
+                for i, (part, hold) in enumerate(zip(parts, held))
+            ]
         )
+    for group in copies:
+        for copy in group:
+            copy.start()
+    for k, group in zip(order, copies):
+        for copy in group:
+            copy.wait()
+        mine_out, got_out, mine_in, got_in = [hold[k].astype(F32) for hold in held]
+        outs[k][:rows, :] = (mine_out + got_out).astype(BF16)
+        outs[k][rows:, :] = (mine_in + got_in).astype(BF16)
 
 
 def merge(chip, *parts):
@@ -360,10 +372,13 @@
     shape = (parts[0].shape[1] + parts[2].shape[1], parts[0].shape[2])
     return pl.pallas_call(
         merge_body,
-        in_specs=[pl.BlockSpec(memory_space=pltpu.SMEM)] + [whole] * 4,
+        in_specs=[pl.BlockSpec(memory_space=pltpu.SMEM)]
+        + [pl.BlockSpec(memory_space=pl.ANY)] * 4,
         out_specs=[whole] * 4,
         out_shape=[jax.ShapeDtypeStruct(shape, BF16)] * 4,
-        compiler_params=pltpu.CompilerParams(vmem_limit_bytes=16 * 2**20),
+        scratch_shapes=[pltpu.VMEM(part.shape, BF16) for part in parts]
+        + [pltpu.SemaphoreType.DMA((4, 4))],
+        compiler_params=pltpu.CompilerParams(vmem_limit_bytes=53 * 2**20),
         cost_estimate=pl.CostEstimate(flops=10**6, bytes_accessed=2 * 10**6, transcendentals=0),
         name="merge",
     )(chip, *parts)

time: 166 us -> 169 us (1.018)
  starting transfers between devices: 35 us -> 41.1 us
  local copies, waits for them, and re-layouts: 6.58 us -> 3.08 us
    all_to_all x1, starting transfers between devices: 6.93 us -> 12 us  [shards(): lax.all_to_all(piece, 'seq', split_axis=0, concat_axis=0, tiled=True)]
    unnamed x28 -> x14, local copies, waits for them, and re-layouts: 6.5 us -> 3 us
where the time goes in v9:
time: 169 us; the launch traced here: 168 us
  Pallas kernels  49.7 us (29%)
  waiting for transfers between devices  44.8 us (27%)
  starting transfers between devices  41.1 us (24%)
  blocking collectives  15.3 us (9%)
  between operations  14.2 us (8%)
  local copies, waits for them, and re-layouts  3.08 us (2%)
    all_to_all x1, waiting for transfers between devices, shards(): lax.all_to_all(sent, 'seq', split_axis=0, concat_axis=0, tiled=True)  34.1 us
    pallas_call x1, Pallas kernels, backward(): pl.pallas_call(backward_body, grid=(blocks // NB,), in_specs=[pl.BlockSpe...  16.3 us
    all_gather x1, blocking collectives, shards(): lax.all_gather(collect(spread), 'slide', axis=0)  15.3 us
    pallas_call x1, Pallas kernels, forward(): pl.pallas_call(forward_body, grid=(blocks // NB,), in_specs=[pl.BlockSpec...  12.4 us
    all_to_all x1, starting transfers between devices, shards(): lax.all_to_all(piece, 'seq', split_axis=0, concat_axis=0, tiled=True)  12 us
    all_to_all x1, starting transfers between devices, shards(): lax.all_to_all(sent, 'seq', split_axis=0, concat_axis=0, tiled=True)  8.73 us
    ppermute x3, waiting for transfers between devices, shards(): lax.ppermute(send, 'slide', [(i, (i + 2 * k) % slides) for i in range(sli...  7.68 us
    all_to_all x1, starting transfers between devices, shards(): lax.all_to_all(results, 'seq', split_axis=0, concat_axis=0, tiled=True)  6.74 us
  transfers between devices with their start and end apart: 10, of which 5 were waited for; matrix products, arithmetic and copies ran while one was open for 0% of the time, Pallas kernels for 28%

profile of v9, /device:TPU:1, one launch (start us, length us, event | category | flops | bytes accessed | tf_op | source)
XLA Modules:
  0.0 168.3 jit_solution(18347221379046866256)
XLA Ops:
  7.2 0.0 copy-start
  7.2 0.0 all-gather.3.cloned.1.call-start
  7.2 0.7 all-gather.3.cloned.1.call-update
  7.9 5.3 %project.1 = bf16[16,256,256]{2,1,0:T(8,128)(2,1)} custom-call(bf16[256,768]{1,0:T(8,128)(2,1)} %bitcast.14, bf16[256,768]{1,0:T(8,128)(2,1)} %bitcast.15, bf16[768,2304]{1,0:T(8,128)(2,1)} %w_ref.1, bf16[768,2304]{1,0:T(8,128)(2,1)} %w_ref.1, bf16[768,2304]{1,0:T(8,128)(2,1)} %w_ref.1, bf16[768,768]{1,0:T(8,128)(2,1)} %wo_ref.3), custom_call_target="tpu_custom_call" | custom-call | flops 1207959552 | bytes 8388608 | tf_op jit(solution)/shard_map/project/pallas_call | solution.py:58
  13.3 0.0 copy-start.6
  13.3 8.7 %all-to-all-start = ((bf16[16,256,256]{2,1,0:T(8,128)(2,1)}), bf16[16,256,256]{2,1,0:T(8,128)(2,1)S(1)}, u32[]{:S(2)}, u32[]{:S(2)}) async-start(bf16[16,256,256]{2,1,0:T(8,128)(2,1)} %project.1), calls=%async_computation | async-start | bytes 4194304 | tf_op jit(solution)/shard_map/all_to_all | solution.py:509
  22.0 0.0 copy-done
  22.0 0.1 copy.12.tiles_ref
  22.1 34.1 %all-to-all-done.in_ref = bf16[16,256,256]{2,1,0:T(8,128)(2,1)S(1)} async-done(((bf16[16,256,256]{2,1,0:T(8,128)(2,1)}), bf16[16,256,256]{2,1,0:T(8,128)(2,1)S(1)}, u32[]{:S(2)}, u32[]{:S(2)}) %all-to-all-start) | async-done | bytes 2097184 | tf_op jit(solution)/shard_map/all_to_all | solution.py:509
  56.2 0.0 copy-done.6
  56.2 12.4 %forward.1 = (bf16[16,64,256]{2,1,0:T(8,128)(2,1)}, bf16[16,1280,256]{2,1,0:T(8,128)(2,1)}, f32[16,8,256]{2,1,0:T(8,128)S(1)}) custom-call(s32[16,8]{1,0:T(8,128)S(1)} %copy.12.tiles_ref, s32[32]{0:T(128)S(1)} %bitcast.13, bf16[16,256,256]{2,1,0:T(8,128)(2,1)S(1)} %all-to-all-done.in_ref), custom_call_target="tpu_custom_call" | custom-call | flops 5368709120 | bytes 14680064 | tf_op jit(solution)/shard_map/forward/pallas_call | solution.py:132
  68.6 3.9 %all-to-all-start.1 = ((bf16[16,64,256]{2,1,0:T(8,128)(2,1)}), bf16[16,64,256]{2,1,0:T(8,128)(2,1)S(1)}, u32[]{:S(2)}, u32[]{:S(2)}) async-start(bf16[16,64,256]{2,1,0:T(8,128)(2,1)} %get-tuple-element.21), calls=%async_computation.1 | async-start | bytes 1048576 | tf_op jit(solution)/shard_map/all_to_all | solution.py:512
  72.5 16.3 %backward.1.res_ref = bf16[16,192,256]{2,1,0:T(8,128)(2,1)} custom-call(s32[16,8]{1,0:T(8,128)S(1)} %copy.12.tiles_ref, bf16[16,256,256]{2,1,0:T(8,128)(2,1)S(1)} %all-to-all-done.in_ref, bf16[16,1280,256]{2,1,0:T(8,128)(2,1)} %get-tuple-element.24.exp_ref, f32[16,8,256]{2,1,0:T(8,128)S(1)} %get-tuple-element.25.stat_ref), custom_call_target="tpu_custom_call" | custom-call | flops 10737418240 | bytes 16777216 | tf_op jit(solution)/shard_map/backward/pallas_call | solution.py:227
  88.8 0.0 all-to-all-done.1.back_ref.att_ref
  88.8 0.0 copy-start.3
  88.8 6.7 %all-to-all-start.2 = ((bf16[16,192,256]{2,1,0:T(8,128)(2,1)}), bf16[16,192,256]{2,1,0:T(8,128)(2,1)}, u32[]{:S(2)}, u32[]{:S(2)}) async-start(bf16[16,192,256]{2,1,0:T(8,128)(2,1)} %backward.1.res_ref), calls=%async_computation.2 | async-start | bytes 3145728 | tf_op jit(solution)/shard_map/all_to_all | solution.py:514
  95.6 0.0 copy-done.3
  95.6 2.8 %outer.1 = (bf16[4,96,768]{2,1,0:T(8,128)(2,1)}, bf16[4,96,768]{2,1,0:T(8,128)(2,1)}) custom-call(s32[1]{0:T(128)} %bitcast.1.core_ref, bf16[16,64,256]{2,1,0:T(8,128)(2,1)} %copy-done.3, bf16[256,768]{1,0:T(8,128)(2,1)} %bitcast.16), custom_call_target="tpu_custom_call" | custom-call | flops 301989888 | bytes 2097152 | tf_op jit(solution)/shard_map/outer/pallas_call | solution.py:283
  98.4 3.7 %collective-permute-start = (bf16[4,96,768]{2,1,0:T(8,128)(2,1)}, bf16[4,96,768]{2,1,0:T(8,128)(2,1)}, u32[]{:S(2)}, u32[]{:S(2)}) collective-permute-start(bf16[4,96,768]{2,1,0:T(8,128)(2,1)} %get-tuple-element.23), channel_id=1, source_target_pairs={{0,1},{1,0},{2,3},{3,2},{4,5},{5,4},{6,7},{7,6},{8,9},{9,8},{10,11... | collective-permute-start | bytes 1769480 | tf_op jit(solution)/shard_map/ppermute | solution.py:518
  102.1 0.0 all-gather.3.cloned.1.call-done.x_ref
  102.1 0.0 copy-start.1
  102.1 5.1 %weigh.1 = (bf16[4,32,768]{2,1,0:T(8,128)(2,1)}, bf16[4,32,768]{2,1,0:T(8,128)(2,1)}) custom-call(s32[1]{0:T(128)} %bitcast.1.core_ref, bf16[16,192,256]{2,1,0:T(8,128)(2,1)} %backward.1.res_ref, bf16[16,256,768]{2,1,0:T(8,128)(2,1)} %all-gather.3.cloned.1.call-done.x_ref), custom_call_target="tpu_custom_call" | custom-call | flops 1207959552 | bytes 8388608 | tf_op jit(solution)/shard_map/weigh/pallas_call | solution.py:325
  107.2 1.2 collective-permute-start.1
  108.3 0.0 collective-permute-done.refs_1_
  108.4 1.4 collective-permute-done.1.refs_3_
  109.8 1.6 merge.1
  111.4 1.3 collective-permute-start.2
  112.6 2.4 %collective-permute-start.3 = (bf16[128,768]{1,0:T(8,128)(2,1)S(1)}, bf16[128,768]{1,0:T(8,128)(2,1)S(1)}, u32[]{:S(2)}, u32[]{:S(2)}) collective-permute-start(bf16[128,768]{1,0:T(8,128)(2,1)S(1)} %get-tuple-element.30), channel_id=1, source_target_pairs={{0,4},{1,5},{2,6},{3,7},{4,0},{5,1},{6,2},{7,3},{8,12},{9,13},{10,... | collective-permute-start | bytes 589832 | tf_op jit(solution)/shard_map/ppermute | solution.py:526
  115.0 1.2 collective-permute-start.4
  116.2 2.7 %collective-permute-done.2.b_ref = bf16[128,768]{1,0:T(8,128)(2,1)S(1)} collective-permute-done((bf16[128,768]{1,0:T(8,128)(2,1)S(1)}, bf16[128,768]{1,0:T(8,128)(2,1)S(1)}, u32[]{:S(2)}, u32[]{:S(2)}) %collective-permute-start.2) | collective-permute-done | bytes 196640 | tf_op jit(solution)/shard_map/ppermute | solution.py:526
  118.9 5.0 %collective-permute-done.3.c_ref = bf16[128,768]{1,0:T(8,128)(2,1)S(1)} collective-permute-done((bf16[128,768]{1,0:T(8,128)(2,1)S(1)}, bf16[128,768]{1,0:T(8,128)(2,1)S(1)}, u32[]{:S(2)}, u32[]{:S(2)}) %collective-permute-start.3) | collective-permute-done | bytes 196640 | tf_op jit(solution)/shard_map/ppermute | solution.py:526
  123.9 0.0 collective-permute-done.4.d_ref
  123.9 0.2 fold.1
  124.0 0.0 copy-start.5
  124.1 0.7 copy-done.5
  124.7 0.0 all-to-all-done.2.back_ref
  124.7 12.0 %all-to-all-start.3 = ((bf16[16,48,128]{2,1,0:T(8,128)(2,1)}), bf16[16,48,128]{2,1,0:T(8,128)(2,1)}, u32[]{:S(2)}, u32[]{:S(2)}) async-start(bf16[16,48,128]{2,1,0:T(8,128)(2,1)} %bitcast.12), calls=%async_computation.3 | async-start | bytes 393216 | tf_op jit(solution)/shard_map/all_to_all | solution.py:532
  136.8 0.0 copy-done.1
  136.8 0.0 copy-start.2
  136.8 1.3 copy-done.2
  138.0 0.0 copy-start.4
  138.0 1.0 copy-done.4
  139.1 3.7 %close.1 = (bf16[256,768]{1,0:T(8,128)(2,1)}, bf16[256,768]{1,0:T(8,128)(2,1)}) custom-call(bf16[16,192,256]{2,1,0:T(8,128)(2,1)} %all-to-all-done.2.back_ref, bf16[16,64,256]{2,1,0:T(8,128)(2,1)S(1)} %copy-done.4, bf16[768,2304]{1,0:T(8,128)(2,1)S(1)} %copy-done.1, bf16[768,768]{1,0:T(8,128)(2,1)S(1)} %copy-done.2), custom_call_target="tpu_custom_call" | custom-call | flops 1207959552 | bytes 8388608 | tf_op jit(solution)/shard_map/close/pallas_call | solution.py:486
  142.8 1.0 all-to-all-done.3.spread_ref
  143.7 1.0 collect.1
  144.8 15.3 %all-gather = bf16[384,384]{1,0:T(8,128)(2,1)S(1)} all-gather(bf16[48,384]{1,0:T(8,128)(2,1)S(1)} %collect.1), channel_id=2, replica_groups=mesh['seq'=16,'slide'=8] {'slide'}, dimensions={0}, use_global_device_ids=true | all-gather | bytes 331776 | tf_op jit(solution)/shard_map/all_gather | solution.py:533
  160.1 1.3 settle.1
  (1 shorter events, 0.0 us)
Async XLA Ops:
  7.2 14.8 %copy-start = (s32[1,4,16,8]{2,3,1,0:T(8,128)S(1)}, s32[1,4,16,8]{2,3,1,0:T(8,128)}, u32[]{:S(2)}) copy-start(s32[1,4,16,8]{2,3,1,0:T(8,128)} %param.8) | copy-start | bytes 6148
  7.2 94.9 %all-gather.3.cloned.1.call-start = ((), (), s32[]{:S(2)}) async-start(), calls=%async_computation.4 | async-start | bytes 6684672 | tf_op jit(solution)/shard_map/all_gather | solution.py:507
  13.3 42.9 %copy-start.6 = (s32[1,32]{1,0:T(1,128)S(1)}, s32[1,32]{1,0:T(1,128)}, u32[]{:S(2)}) copy-start(s32[1,32]{1,0:T(1,128)} %param.9) | copy-start | bytes 388
  13.3 42.9 %all-to-all-start = ((bf16[16,256,256]{2,1,0:T(8,128)(2,1)}), bf16[16,256,256]{2,1,0:T(8,128)(2,1)S(1)}, u32[]{:S(2)}, u32[]{:S(2)}) async-start(bf16[16,256,256]{2,1,0:T(8,128)(2,1)} %project.1), calls=%async_computation | async-start | bytes 4194304 | tf_op jit(solution)/shard_map/all_to_all | solution.py:509
  68.6 20.2 %all-to-all-start.1 = ((bf16[16,64,256]{2,1,0:T(8,128)(2,1)}), bf16[16,64,256]{2,1,0:T(8,128)(2,1)S(1)}, u32[]{:S(2)}, u32[]{:S(2)}) async-start(bf16[16,64,256]{2,1,0:T(8,128)(2,1)} %get-tuple-element.21), calls=%async_computation.1 | async-start | bytes 1048576 | tf_op jit(solution)/shard_map/all_to_all | solution.py:512
  88.8 6.8 %copy-start.3 = (bf16[16,64,256]{2,1,0:T(8,128)(2,1)}, bf16[16,64,256]{2,1,0:T(8,128)(2,1)S(1)}, u32[]{:S(2)}) copy-start(bf16[16,64,256]{2,1,0:T(8,128)(2,1)S(1)} %all-to-all-done.1.back_ref.att_ref) | copy-start | bytes 1572868
  88.8 35.9 %all-to-all-start.2 = ((bf16[16,192,256]{2,1,0:T(8,128)(2,1)}), bf16[16,192,256]{2,1,0:T(8,128)(2,1)}, u32[]{:S(2)}, u32[]{:S(2)}) async-start(bf16[16,192,256]{2,1,0:T(8,128)(2,1)} %backward.1.res_ref), calls=%async_computation.2 | async-start | bytes 3145728 | tf_op jit(solution)/shard_map/all_to_all | solution.py:514
  98.4 10.0 %collective-permute-start = (bf16[4,96,768]{2,1,0:T(8,128)(2,1)}, bf16[4,96,768]{2,1,0:T(8,128)(2,1)}, u32[]{:S(2)}, u32[]{:S(2)}) collective-permute-start(bf16[4,96,768]{2,1,0:T(8,128)(2,1)} %get-tuple-element.23), channel_id=1, source_target_pairs={{0,1},{1,0},{2,3},{3,2},{4,5},{5,4},{6,7},{7,6},{8,9},{9,8},{10,11... | collective-permute-start | bytes 1769480 | tf_op jit(solution)/shard_map/ppermute | solution.py:518
  102.1 34.7 %copy-start.1 = (bf16[768,2304]{1,0:T(8,128)(2,1)S(1)}, bf16[768,2304]{1,0:T(8,128)(2,1)}, u32[]{:S(2)}) copy-start(bf16[768,2304]{1,0:T(8,128)(2,1)} %w_ref.1) | copy-start | bytes 10616836
  107.2 2.6 %collective-permute-start.1 = (bf16[4,32,768]{2,1,0:T(8,128)(2,1)}, bf16[4,32,768]{2,1,0:T(8,128)(2,1)}, u32[]{:S(2)}, u32[]{:S(2)}) collective-permute-start(bf16[4,32,768]{2,1,0:T(8,128)(2,1)} %get-tuple-element.27), channel_id=1, source_target_pairs={{0,1},{1,0},{2,3},{3,2},{4,5},{5,4},{6,7},{7,6},{8,9},{9,8},{10,11... | collective-permute-start | bytes 589832 | tf_op jit(solution)/shard_map/ppermute | solution.py:518
  111.4 7.5 %collective-permute-start.2 = (bf16[128,768]{1,0:T(8,128)(2,1)S(1)}, bf16[128,768]{1,0:T(8,128)(2,1)S(1)}, u32[]{:S(2)}, u32[]{:S(2)}) collective-permute-start(bf16[128,768]{1,0:T(8,128)(2,1)S(1)} %get-tuple-element.29), channel_id=1, source_target_pairs={{0,2},{1,3},{2,4},{3,5},{4,6},{5,7},{6,0},{7,1},{8,10},{9,11},{10,... | collective-permute-start | bytes 589832 | tf_op jit(solution)/shard_map/ppermute | solution.py:526
  112.6 11.2 %collective-permute-start.3 = (bf16[128,768]{1,0:T(8,128)(2,1)S(1)}, bf16[128,768]{1,0:T(8,128)(2,1)S(1)}, u32[]{:S(2)}, u32[]{:S(2)}) collective-permute-start(bf16[128,768]{1,0:T(8,128)(2,1)S(1)} %get-tuple-element.30), channel_id=1, source_target_pairs={{0,4},{1,5},{2,6},{3,7},{4,0},{5,1},{6,2},{7,3},{8,12},{9,13},{10,... | collective-permute-start | bytes 589832 | tf_op jit(solution)/shard_map/ppermute | solution.py:526
  115.0 8.9 %collective-permute-start.4 = (bf16[128,768]{1,0:T(8,128)(2,1)S(1)}, bf16[128,768]{1,0:T(8,128)(2,1)S(1)}, u32[]{:S(2)}, u32[]{:S(2)}) collective-permute-start(bf16[128,768]{1,0:T(8,128)(2,1)S(1)} %get-tuple-element.31), channel_id=1, source_target_pairs={{0,6},{1,7},{2,0},{3,1},{4,2},{5,3},{6,4},{7,5},{8,14},{9,15},{10,... | collective-permute-start | bytes 589832 | tf_op jit(solution)/shard_map/ppermute | solution.py:526
  124.0 0.7 copy-start.5
  124.7 19.0 %all-to-all-start.3 = ((bf16[16,48,128]{2,1,0:T(8,128)(2,1)}), bf16[16,48,128]{2,1,0:T(8,128)(2,1)}, u32[]{:S(2)}, u32[]{:S(2)}) async-start(bf16[16,48,128]{2,1,0:T(8,128)(2,1)} %bitcast.12), calls=%async_computation.3 | async-start | bytes 393216 | tf_op jit(solution)/shard_map/all_to_all | solution.py:532
  136.8 1.3 copy-start.2
  138.0 1.0 copy-start.4
Sparse Core Ops, SparseCore 0:
  10.2 91.8 all-gather.2

commit v10 on v9

--- a/solution.py
+++ b/solution.py
@@ -511,13 +511,14 @@
     att_sent, low, stats = forward(group_tiles, tile_valid[0], arrived)
     att_back = lax.all_to_all(att_sent, "seq", split_axis=0, concat_axis=0, tiled=True)
     results = backward(group_tiles, arrived, low, stats)
-    back = lax.all_to_all(results, "seq", split_axis=0, concat_axis=0, tiled=True)
     core = lax.rem(slide, 2)[None]
 
     def swap(value):
         return lax.ppermute(value, "slide", [(i, i ^ 1) for i in range(slides)])
 
     mine_out, theirs_out = outer(core, att_back, cot)
+    results, theirs_out = lax.optimization_barrier((results, theirs_out))
+    back = lax.all_to_all(results, "seq", split_axis=0, concat_axis=0, tiled=True)
     got_out = swap(theirs_out)
     mine_in, theirs_in = weigh(core, results, x_all)
     got_in = swap(theirs_in)

time: 169 us -> 164 us (0.970)
  starting transfers between devices: 41.1 us -> 35 us
    all_to_all x1, starting transfers between devices: 12 us -> 6.86 us  [shards(): lax.all_to_all(piece, 'seq', split_axis=0, concat_axis=0, tiled=True)]
  transfers between devices with their start and end apart: 10 -> 10, of which waited for: 5 -> 5; matrix products, arithmetic and copies ran while one was open for 0% -> 0% of each run, Pallas kernels for 28% -> 29%
where the time goes in v10:
time: 164 us; the launch traced here: 163 us
  Pallas kernels  49.7 us (30%)
  waiting for transfers between devices  45.4 us (28%)
  starting transfers between devices  35 us (21%)
  blocking collectives  15.1 us (9%)
  between operations  14.2 us (9%)
  local copies, waits for them, and re-layouts  3.87 us (2%)
    all_to_all x1, waiting for transfers between devices, shards(): lax.all_to_all(sent, 'seq', split_axis=0, concat_axis=0, tiled=True)  34.1 us
    pallas_call x1, Pallas kernels, backward(): pl.pallas_call(backward_body, grid=(blocks // NB,), in_specs=[pl.BlockSpe...  16.3 us
    all_gather x1, blocking collectives, shards(): lax.all_gather(collect(spread), 'slide', axis=0)  15.1 us
    pallas_call x1, Pallas kernels, forward(): pl.pallas_call(forward_body, grid=(blocks // NB,), in_specs=[pl.BlockSpec...  12.4 us
    all_to_all x1, starting transfers between devices, shards(): lax.all_to_all(sent, 'seq', split_axis=0, concat_axis=0, tiled=True)  8.73 us
    ppermute x3, waiting for transfers between devices, shards(): lax.ppermute(send, 'slide', [(i, (i + 2 * k) % slides) for i in range(sli...  7.95 us
    all_to_all x1, starting transfers between devices, shards(): lax.all_to_all(piece, 'seq', split_axis=0, concat_axis=0, tiled=True)  6.86 us
    all_to_all x1, starting transfers between devices, shards(): lax.all_to_all(results, 'seq', split_axis=0, concat_axis=0, tiled=True)  6.62 us
  transfers between devices with their start and end apart: 10, of which 5 were waited for; matrix products, arithmetic and copies ran while one was open for 0% of the time, Pallas kernels for 29%

profile of v10, /device:TPU:1, one launch (start us, length us, event | category | flops | bytes accessed | tf_op | source)
XLA Modules:
  0.0 163.3 jit_solution(7949338009656640307)
XLA Ops:
  7.2 0.0 copy-start
  7.2 0.0 all-gather.3.cloned.1.call-start
  7.2 0.7 all-gather.3.cloned.1.call-update
  7.9 5.3 %project.1 = bf16[16,256,256]{2,1,0:T(8,128)(2,1)} custom-call(bf16[256,768]{1,0:T(8,128)(2,1)} %bitcast.14, bf16[256,768]{1,0:T(8,128)(2,1)} %bitcast.15, bf16[768,2304]{1,0:T(8,128)(2,1)} %w_ref.1, bf16[768,2304]{1,0:T(8,128)(2,1)} %w_ref.1, bf16[768,2304]{1,0:T(8,128)(2,1)} %w_ref.1, bf16[768,768]{1,0:T(8,128)(2,1)} %wo_ref.3), custom_call_target="tpu_custom_call" | custom-call | flops 1207959552 | bytes 8388608 | tf_op jit(solution)/shard_map/project/pallas_call | solution.py:58
  13.3 0.0 copy-start.6
  13.3 8.7 %all-to-all-start = ((bf16[16,256,256]{2,1,0:T(8,128)(2,1)}), bf16[16,256,256]{2,1,0:T(8,128)(2,1)S(1)}, u32[]{:S(2)}, u32[]{:S(2)}) async-start(bf16[16,256,256]{2,1,0:T(8,128)(2,1)} %project.1), calls=%async_computation | async-start | bytes 4194304 | tf_op jit(solution)/shard_map/all_to_all | solution.py:509
  22.0 0.0 copy-done
  22.0 0.1 copy.12.tiles_ref
  22.1 34.1 %all-to-all-done.in_ref = bf16[16,256,256]{2,1,0:T(8,128)(2,1)S(1)} async-done(((bf16[16,256,256]{2,1,0:T(8,128)(2,1)}), bf16[16,256,256]{2,1,0:T(8,128)(2,1)S(1)}, u32[]{:S(2)}, u32[]{:S(2)}) %all-to-all-start) | async-done | bytes 2097184 | tf_op jit(solution)/shard_map/all_to_all | solution.py:509
  56.2 0.0 copy-done.6
  56.2 12.4 %forward.1 = (bf16[16,64,256]{2,1,0:T(8,128)(2,1)}, bf16[16,1280,256]{2,1,0:T(8,128)(2,1)}, f32[16,8,256]{2,1,0:T(8,128)S(1)}) custom-call(s32[16,8]{1,0:T(8,128)S(1)} %copy.12.tiles_ref, s32[32]{0:T(128)S(1)} %bitcast.13, bf16[16,256,256]{2,1,0:T(8,128)(2,1)S(1)} %all-to-all-done.in_ref), custom_call_target="tpu_custom_call" | custom-call | flops 5368709120 | bytes 14680064 | tf_op jit(solution)/shard_map/forward/pallas_call | solution.py:132
  68.6 3.9 %all-to-all-start.1 = ((bf16[16,64,256]{2,1,0:T(8,128)(2,1)}), bf16[16,64,256]{2,1,0:T(8,128)(2,1)S(1)}, u32[]{:S(2)}, u32[]{:S(2)}) async-start(bf16[16,64,256]{2,1,0:T(8,128)(2,1)} %get-tuple-element.23), calls=%async_computation.1 | async-start | bytes 1048576 | tf_op jit(solution)/shard_map/all_to_all | solution.py:512
  72.5 16.3 %backward.1.res_ref = bf16[16,192,256]{2,1,0:T(8,128)(2,1)} custom-call(s32[16,8]{1,0:T(8,128)S(1)} %copy.12.tiles_ref, bf16[16,256,256]{2,1,0:T(8,128)(2,1)S(1)} %all-to-all-done.in_ref, bf16[16,1280,256]{2,1,0:T(8,128)(2,1)} %get-tuple-element.25.exp_ref, f32[16,8,256]{2,1,0:T(8,128)S(1)} %get-tuple-element.26.stat_ref), custom_call_target="tpu_custom_call" | custom-call | flops 10737418240 | bytes 16777216 | tf_op jit(solution)/shard_map/backward/pallas_call | solution.py:227
  88.8 0.0 all-to-all-done.1.back_ref.att_ref
  88.8 0.0 copy-start.3
  88.8 0.8 copy-done.3
  89.6 2.8 %outer.1 = (bf16[4,96,768]{2,1,0:T(8,128)(2,1)}, bf16[4,96,768]{2,1,0:T(8,128)(2,1)}) custom-call(s32[1]{0:T(128)} %bitcast.1.core_ref, bf16[16,64,256]{2,1,0:T(8,128)(2,1)} %copy-done.3, bf16[256,768]{1,0:T(8,128)(2,1)} %bitcast.16), custom_call_target="tpu_custom_call" | custom-call | flops 301989888 | bytes 2097152 | tf_op jit(solution)/shard_map/outer/pallas_call | solution.py:283
  92.4 6.6 %all-to-all-start.2 = ((bf16[16,192,256]{2,1,0:T(8,128)(2,1)}), bf16[16,192,256]{2,1,0:T(8,128)(2,1)}, u32[]{:S(2)}, u32[]{:S(2)}) async-start(bf16[16,192,256]{2,1,0:T(8,128)(2,1)} %backward.1.res_ref), calls=%async_computation.2 | async-start | bytes 3145728 | tf_op jit(solution)/shard_map/all_to_all | solution.py:521
  99.0 3.9 %collective-permute-start = (bf16[4,96,768]{2,1,0:T(8,128)(2,1)}, bf16[4,96,768]{2,1,0:T(8,128)(2,1)}, u32[]{:S(2)}, u32[]{:S(2)}) collective-permute-start(bf16[4,96,768]{2,1,0:T(8,128)(2,1)} %get-tuple-element.28), channel_id=1, source_target_pairs={{0,1},{1,0},{2,3},{3,2},{4,5},{5,4},{6,7},{7,6},{8,9},{9,8},{10,11... | collective-permute-start | bytes 1769480 | tf_op jit(solution)/shard_map/ppermute | solution.py:517
  102.9 0.0 all-gather.3.cloned.1.call-done.x_ref
  102.9 0.0 copy-start.1
  102.9 5.1 %weigh.1 = (bf16[4,32,768]{2,1,0:T(8,128)(2,1)}, bf16[4,32,768]{2,1,0:T(8,128)(2,1)}) custom-call(s32[1]{0:T(128)} %bitcast.1.core_ref, bf16[16,192,256]{2,1,0:T(8,128)(2,1)} %backward.1.res_ref, bf16[16,256,768]{2,1,0:T(8,128)(2,1)} %all-gather.3.cloned.1.call-done.x_ref), custom_call_target="tpu_custom_call" | custom-call | flops 1207959552 | bytes 8388608 | tf_op jit(solution)/shard_map/weigh/pallas_call | solution.py:325
  108.0 0.1 collective-permute-start.1
  108.1 0.0 collective-permute-done.refs_1_
  108.1 1.7 %collective-permute-done.1.refs_3_ = bf16[4,32,768]{2,1,0:T(8,128)(2,1)} collective-permute-done((bf16[4,32,768]{2,1,0:T(8,128)(2,1)}, bf16[4,32,768]{2,1,0:T(8,128)(2,1)}, u32[]{:S(2)}, u32[]{:S(2)}) %collective-permute-start.1) | collective-permute-done | bytes 196640 | tf_op jit(solution)/shard_map/ppermute | solution.py:517
  109.8 1.6 merge.1
  111.4 1.3 collective-permute-start.2
  112.7 2.4 %collective-permute-start.3 = (bf16[128,768]{1,0:T(8,128)(2,1)S(1)}, bf16[128,768]{1,0:T(8,128)(2,1)S(1)}, u32[]{:S(2)}, u32[]{:S(2)}) collective-permute-start(bf16[128,768]{1,0:T(8,128)(2,1)S(1)} %get-tuple-element.34), channel_id=1, source_target_pairs={{0,4},{1,5},{2,6},{3,7},{4,0},{5,1},{6,2},{7,3},{8,12},{9,13},{10,... | collective-permute-start | bytes 589832 | tf_op jit(solution)/shard_map/ppermute | solution.py:527
  115.1 1.2 collective-permute-start.4
  116.3 2.9 %collective-permute-done.2.b_ref = bf16[128,768]{1,0:T(8,128)(2,1)S(1)} collective-permute-done((bf16[128,768]{1,0:T(8,128)(2,1)S(1)}, bf16[128,768]{1,0:T(8,128)(2,1)S(1)}, u32[]{:S(2)}, u32[]{:S(2)}) %collective-permute-start.2) | collective-permute-done | bytes 196640 | tf_op jit(solution)/shard_map/ppermute | solution.py:527
  119.1 5.1 %collective-permute-done.3.c_ref = bf16[128,768]{1,0:T(8,128)(2,1)S(1)} collective-permute-done((bf16[128,768]{1,0:T(8,128)(2,1)S(1)}, bf16[128,768]{1,0:T(8,128)(2,1)S(1)}, u32[]{:S(2)}, u32[]{:S(2)}) %collective-permute-start.3) | collective-permute-done | bytes 196640 | tf_op jit(solution)/shard_map/ppermute | solution.py:527
  124.2 0.0 collective-permute-done.4.d_ref
  124.2 0.2 fold.1
  124.4 0.0 copy-start.5
  124.4 0.7 copy-done.5
  125.1 0.0 all-to-all-done.2.back_ref
  125.1 6.9 %all-to-all-start.3 = ((bf16[16,48,128]{2,1,0:T(8,128)(2,1)}), bf16[16,48,128]{2,1,0:T(8,128)(2,1)}, u32[]{:S(2)}, u32[]{:S(2)}) async-start(bf16[16,48,128]{2,1,0:T(8,128)(2,1)} %bitcast.12), calls=%async_computation.3 | async-start | bytes 393216 | tf_op jit(solution)/shard_map/all_to_all | solution.py:533
  131.9 0.0 copy-done.1
  131.9 0.0 copy-start.2
  132.0 1.3 copy-done.2
  133.2 0.0 copy-start.4
  133.2 1.0 copy-done.4
  134.3 3.7 %close.1 = (bf16[256,768]{1,0:T(8,128)(2,1)}, bf16[256,768]{1,0:T(8,128)(2,1)}) custom-call(bf16[16,192,256]{2,1,0:T(8,128)(2,1)} %all-to-all-done.2.back_ref, bf16[16,64,256]{2,1,0:T(8,128)(2,1)S(1)} %copy-done.4, bf16[768,2304]{1,0:T(8,128)(2,1)S(1)} %copy-done.1, bf16[768,768]{1,0:T(8,128)(2,1)S(1)} %copy-done.2), custom_call_target="tpu_custom_call" | custom-call | flops 1207959552 | bytes 8388608 | tf_op jit(solution)/shard_map/close/pallas_call | solution.py:486
  138.0 1.0 all-to-all-done.3.spread_ref
  139.0 1.0 collect.1
  140.0 15.1 %all-gather = bf16[384,384]{1,0:T(8,128)(2,1)S(1)} all-gather(bf16[48,384]{1,0:T(8,128)(2,1)S(1)} %collect.1), channel_id=2, replica_groups=mesh['seq'=16,'slide'=8] {'slide'}, dimensions={0}, use_global_device_ids=true | all-gather | bytes 331776 | tf_op jit(solution)/shard_map/all_gather | solution.py:534
  155.1 1.3 settle.1
  (1 shorter events, 0.0 us)
Async XLA Ops:
  7.2 14.8 %copy-start = (s32[1,4,16,8]{2,3,1,0:T(8,128)S(1)}, s32[1,4,16,8]{2,3,1,0:T(8,128)}, u32[]{:S(2)}) copy-start(s32[1,4,16,8]{2,3,1,0:T(8,128)} %param.8) | copy-start | bytes 6148
  7.2 95.7 %all-gather.3.cloned.1.call-start = ((), (), s32[]{:S(2)}) async-start(), calls=%async_computation.4 | async-start | bytes 6684672 | tf_op jit(solution)/shard_map/all_gather | solution.py:507
  13.3 42.9 %copy-start.6 = (s32[1,32]{1,0:T(1,128)S(1)}, s32[1,32]{1,0:T(1,128)}, u32[]{:S(2)}) copy-start(s32[1,32]{1,0:T(1,128)} %param.9) | copy-start | bytes 388
  13.3 42.9 %all-to-all-start = ((bf16[16,256,256]{2,1,0:T(8,128)(2,1)}), bf16[16,256,256]{2,1,0:T(8,128)(2,1)S(1)}, u32[]{:S(2)}, u32[]{:S(2)}) async-start(bf16[16,256,256]{2,1,0:T(8,128)(2,1)} %project.1), calls=%async_computation | async-start | bytes 4194304 | tf_op jit(solution)/shard_map/all_to_all | solution.py:509
  68.6 20.2 %all-to-all-start.1 = ((bf16[16,64,256]{2,1,0:T(8,128)(2,1)}), bf16[16,64,256]{2,1,0:T(8,128)(2,1)S(1)}, u32[]{:S(2)}, u32[]{:S(2)}) async-start(bf16[16,64,256]{2,1,0:T(8,128)(2,1)} %get-tuple-element.23), calls=%async_computation.1 | async-start | bytes 1048576 | tf_op jit(solution)/shard_map/all_to_all | solution.py:512
  88.8 0.8 copy-start.3
  92.4 32.7 %all-to-all-start.2 = ((bf16[16,192,256]{2,1,0:T(8,128)(2,1)}), bf16[16,192,256]{2,1,0:T(8,128)(2,1)}, u32[]{:S(2)}, u32[]{:S(2)}) async-start(bf16[16,192,256]{2,1,0:T(8,128)(2,1)} %backward.1.res_ref), calls=%async_computation.2 | async-start | bytes 3145728 | tf_op jit(solution)/shard_map/all_to_all | solution.py:521
  99.0 9.0 %collective-permute-start = (bf16[4,96,768]{2,1,0:T(8,128)(2,1)}, bf16[4,96,768]{2,1,0:T(8,128)(2,1)}, u32[]{:S(2)}, u32[]{:S(2)}) collective-permute-start(bf16[4,96,768]{2,1,0:T(8,128)(2,1)} %get-tuple-element.28), channel_id=1, source_target_pairs={{0,1},{1,0},{2,3},{3,2},{4,5},{5,4},{6,7},{7,6},{8,9},{9,8},{10,11... | collective-permute-start | bytes 1769480 | tf_op jit(solution)/shard_map/ppermute | solution.py:517
  102.9 29.0 %copy-start.1 = (bf16[768,2304]{1,0:T(8,128)(2,1)S(1)}, bf16[768,2304]{1,0:T(8,128)(2,1)}, u32[]{:S(2)}) copy-start(bf16[768,2304]{1,0:T(8,128)(2,1)} %w_ref.1) | copy-start | bytes 10616836
  108.0 1.8 %collective-permute-start.1 = (bf16[4,32,768]{2,1,0:T(8,128)(2,1)}, bf16[4,32,768]{2,1,0:T(8,128)(2,1)}, u32[]{:S(2)}, u32[]{:S(2)}) collective-permute-start(bf16[4,32,768]{2,1,0:T(8,128)(2,1)} %get-tuple-element.31), channel_id=1, source_target_pairs={{0,1},{1,0},{2,3},{3,2},{4,5},{5,4},{6,7},{7,6},{8,9},{9,8},{10,11... | collective-permute-start | bytes 589832 | tf_op jit(solution)/shard_map/ppermute | solution.py:517
  111.4 7.7 %collective-permute-start.2 = (bf16[128,768]{1,0:T(8,128)(2,1)S(1)}, bf16[128,768]{1,0:T(8,128)(2,1)S(1)}, u32[]{:S(2)}, u32[]{:S(2)}) collective-permute-start(bf16[128,768]{1,0:T(8,128)(2,1)S(1)} %get-tuple-element.33), channel_id=1, source_target_pairs={{0,2},{1,3},{2,4},{3,5},{4,6},{5,7},{6,0},{7,1},{8,10},{9,11},{10,... | collective-permute-start | bytes 589832 | tf_op jit(solution)/shard_map/ppermute | solution.py:527
  112.7 11.6 %collective-permute-start.3 = (bf16[128,768]{1,0:T(8,128)(2,1)S(1)}, bf16[128,768]{1,0:T(8,128)(2,1)S(1)}, u32[]{:S(2)}, u32[]{:S(2)}) collective-permute-start(bf16[128,768]{1,0:T(8,128)(2,1)S(1)} %get-tuple-element.34), channel_id=1, source_target_pairs={{0,4},{1,5},{2,6},{3,7},{4,0},{5,1},{6,2},{7,3},{8,12},{9,13},{10,... | collective-permute-start | bytes 589832 | tf_op jit(solution)/shard_map/ppermute | solution.py:527
  115.1 9.1 %collective-permute-start.4 = (bf16[128,768]{1,0:T(8,128)(2,1)S(1)}, bf16[128,768]{1,0:T(8,128)(2,1)S(1)}, u32[]{:S(2)}, u32[]{:S(2)}) collective-permute-start(bf16[128,768]{1,0:T(8,128)(2,1)S(1)} %get-tuple-element.35), channel_id=1, source_target_pairs={{0,6},{1,7},{2,0},{3,1},{4,2},{5,3},{6,4},{7,5},{8,14},{9,15},{10,... | collective-permute-start | bytes 589832 | tf_op jit(solution)/shard_map/ppermute | solution.py:527
  124.4 0.7 copy-start.5
  125.1 13.9 %all-to-all-start.3 = ((bf16[16,48,128]{2,1,0:T(8,128)(2,1)}), bf16[16,48,128]{2,1,0:T(8,128)(2,1)}, u32[]{:S(2)}, u32[]{:S(2)}) async-start(bf16[16,48,128]{2,1,0:T(8,128)(2,1)} %bitcast.12), calls=%async_computation.3 | async-start | bytes 393216 | tf_op jit(solution)/shard_map/all_to_all | solution.py:533
  131.9 1.3 copy-start.2
  133.2 1.0 copy-start.4
Sparse Core Ops, SparseCore 0:
  10.2 90.6 all-gather.2
